TPU v7x, 32 devices: a whole 2x2x4 slice. The times are simulated.
32 devices in a mesh: tile: 8 (over z, x), height: 4 (over y, core).
Axes of the slice: x: 2, y: 2, z: 4, core: 2. Of those that a mesh axis runs over, the one named last changes fastest.
Arguments:
- material: int32 [32, 256, 128], P('height', 'tile'), may hold values from 0 to 2
- clamped: int32 [32, 256, 128], P('height', 'tile'), may hold values from 0 to 1, as said below
- stiffness_table: float32 [3], replicated, may hold values from 0.5 to 4
- eigenstrain: float32 [3, 3], replicated, may hold values from -6 to 6
Outputs:
- displacement: float32 [3, 32, 256, 128], P(None, 'height', 'tile')
Inputs may be any that keep to these rules, and one draw needn't show every extreme that they name: `clamped`: only voxels of the lowest 2 layers can be 1; in those layers 0 and 1 are equally likely.
All inputs are finite; a program needn't handle non-finite values.
Results may differ from a plain program's by a relative error of at most 0.00016.
Values sent between devices are 32-bit elements; how exact they have to be, the bound alone decides.
No kernel may reach another device: no remote copies, remote signals or barrier semaphores. Data moves between devices by JAX's collectives and lax.ppermute only.
A program may use at most 128 MiB of HBM per device.

v0:
```python
import jax
import jax.numpy as jnp
from jax import lax
from jax.sharding import PartitionSpec as P

NLABEL = 3
LEVELS = 3
PRE = 2
COARSE_SWEEPS = 6


GAMMA = 1.0
PENALTY = 50.0
OMEGA = 0.6


def with_halo(block, sides, width):
    for axis, dim in sides:
        count = lax.axis_size(axis)
        forward = [(i, i + 1) for i in range(count - 1)]
        backward = [(target, source) for source, target in forward]
        low = lax.ppermute(
            lax.slice_in_dim(block, block.shape[dim] - width, None, axis=dim), axis, forward
        )
        high = lax.ppermute(lax.slice_in_dim(block, 0, width, axis=dim), axis, backward)
        block = jnp.concatenate([low, block, high], axis=dim)
    return block


def passed_along(x, axis, by):
    size = lax.axis_size(axis)
    pairs = [(i, i + by) for i in range(size) if 0 <= i + by < size]
    return lax.ppermute(x, axis, pairs)


def lookup(labels, table):
    result = jnp.zeros(labels.shape, table.dtype)
    for label_id in range(NLABEL):
        result = result + (labels == label_id).astype(table.dtype) * table[label_id]
    return result


def block_sum(field):
    dims_now = field.shape
    shaped = field.reshape(
        dims_now[0], dims_now[1] // 2, 2, dims_now[2] // 2, 2, dims_now[3] // 2, 2
    )
    return shaped.sum(axis=(2, 4, 6))


def prolong(field):
    return jnp.repeat(jnp.repeat(jnp.repeat(field, 2, axis=1), 2, axis=2), 2, axis=3)


def direction_factor(direction, dtype):
    return jnp.where(jnp.arange(3) == direction, 1.0 + GAMMA, 1.0).astype(dtype).reshape(3, 1, 1, 1)


def coefficients(stiffness, spring, pairs):
    k_lower, k_upper = ([], [])
    diagonal = jnp.broadcast_to(spring, (3,) + spring.shape[1:])
    for direction in range(3):
        lower_nb, upper_nb = pairs[direction]
        low_face = 0.5 * (stiffness + lower_nb)
        high_face = 0.5 * (stiffness + upper_nb)
        diagonal = diagonal + direction_factor(direction, stiffness.dtype) * (low_face + high_face)
        k_lower.append(low_face)
        k_upper.append(high_face)
    return (k_lower, k_upper, diagonal)


def apply_operator(motion, spring, k_lower, k_upper, pairs):
    result = spring * motion
    for direction in range(3):
        lower_nb, upper_nb = pairs[direction]
        term = k_lower[direction] * (motion - lower_nb) + k_upper[direction] * (motion - upper_nb)
        result = result + direction_factor(direction, motion.dtype) * term
    return result


def smooth_from_zero(source, spring, terms, sweeps, pairs_fn):
    k_lower, k_upper, diagonal = terms
    motion = OMEGA * source / diagonal
    for turn_idx in range(sweeps - 1):
        motion = (
            motion
            + OMEGA
            * (source - apply_operator(motion, spring, k_lower, k_upper, pairs_fn(motion)))
            / diagonal
        )
    return motion


def layer_slabs(field, width):
    extended = with_halo(field, (("height", 1),), width)
    total = extended.shape[1]
    return (
        lax.slice_in_dim(extended, 0, width, axis=1),
        lax.slice_in_dim(extended, total - width, total, axis=1),
    )


def row_slabs(field, width):
    edge = field.shape[2]
    slabs = []
    for offset in (1, -1):
        if offset > 0:
            sent = lax.slice_in_dim(field, edge - width, edge, axis=2)
        else:
            sent = lax.slice_in_dim(field, 0, width, axis=2)
        slabs.append(passed_along(sent, "tile", offset))
    return (slabs[0], slabs[1])


def column_slabs(field, width):
    empty = jnp.zeros(field.shape[:3] + (width,), field.dtype)
    return (empty, empty)


def face_pair(field, direction, width):
    if direction == 0:
        return layer_slabs(field, width)
    if direction == 1:
        return row_slabs(field, width)
    return column_slabs(field, width)


def neighbour_arrays(field, axis_dim, low_slab, high_slab):
    length = field.shape[axis_dim]
    lower_nb = jnp.concatenate(
        [low_slab, lax.slice_in_dim(field, 0, length - 1, axis=axis_dim)], axis=axis_dim
    )
    upper_nb = jnp.concatenate(
        [lax.slice_in_dim(field, 1, length, axis=axis_dim), high_slab], axis=axis_dim
    )
    return (lower_nb, upper_nb)


def local_pairs(field):
    pairs = []
    for direction in range(3):
        low_slab, high_slab = face_pair(field, direction, 1)
        pairs.append(neighbour_arrays(field, direction + 1, low_slab, high_slab))
    return pairs


def stiffness_pairs(stiffness):
    pairs = []
    for direction in range(3):
        low_slab, high_slab = face_pair(stiffness, direction, 1)
        pairs.append(neighbour_arrays(stiffness, direction + 1, low_slab, high_slab))
    return pairs


def local(material, clamped, stiffness_table, eigenstrain):
    labels = material[None]
    stiffness = lookup(labels, stiffness_table)
    spring = PENALTY * clamped[None].astype(jnp.float32)
    pieces = []
    for component in range(3):
        stress = stiffness * lookup(labels, eigenstrain[:, component])
        low_slab, high_slab = face_pair(stress, component, 1)
        lower_nb, upper_nb = neighbour_arrays(stress, component + 1, low_slab, high_slab)
        pieces.append(0.5 * (lower_nb - upper_nb))
    source = jnp.concatenate(pieces, 0)
    saved = []
    for grid_level in range(LEVELS):
        terms = coefficients(stiffness, spring, stiffness_pairs(stiffness))
        motion = smooth_from_zero(source, spring, terms, PRE, local_pairs)
        remain = source - apply_operator(motion, spring, terms[0], terms[1], local_pairs(motion))
        saved.append((motion, source, spring, terms))
        source = block_sum(remain)
        stiffness = 0.5 * block_sum(stiffness)
        spring = block_sum(spring)
    terms = coefficients(stiffness, spring, stiffness_pairs(stiffness))
    motion = smooth_from_zero(source, spring, terms, COARSE_SWEEPS, local_pairs)
    for grid_level in reversed(range(LEVELS)):
        level_motion, level_source, level_spring, terms = saved[grid_level]
        k_lower, k_upper, diagonal = terms
        motion = level_motion + prolong(motion)
        motion = (
            motion
            + OMEGA
            * (
                level_source
                - apply_operator(motion, level_spring, k_lower, k_upper, local_pairs(motion))
            )
            / diagonal
        )
    return motion


def solution(mesh):
    in_specs = (P("height", "tile", None), P("height", "tile", None), P(), P())
    out_specs = P(None, "height", "tile", None)
    return jax.shard_map(local, mesh=mesh, in_specs=in_specs, out_specs=out_specs, check_vma=False)
```

profile of v0, /device:TPU:0, one launch (start us, length us, event | category | flops | bytes accessed | tf_op | source)
XLA Modules:
  0.0 370.7 jit_solution(11484711678146226422)
XLA Ops:
  7.5 9.8 %reshape.836 = f32[4,2,16,2,64,2]{5,4,3,2,1,0:T(8,128)} reshape(f32[8,32,128]{2,1,0:T(8,128)S(1)} %copy.176) | data formatting | bytes 262144 | tf_op jit(solution)/shard_map/reshape | solution.py:45
  27.0 6.1 %collective-permute-start.18 = (f32[1,4,1,64]{3,1,2,0:T(4,128)S(1)}, f32[1,4,1,64]{3,1,2,0:T(4,128)S(1)}, u32[]{:S(2)}, u32[]{:S(2)}) collective-permute-start(f32[1,4,1,64]{3,1,2,0:T(4,128)S(1)} %bitcast.178), channel_id=1, source_target_pairs={{0,4},{4,8},{8,12},{12,16},{16,20},{20,24},{24,28},{1,5},{5,9},{9,... | collective-permute-start | bytes 3080 | tf_op jit(solution)/shard_map/ppermute | solution.py:33
  36.3 9.8 %reshape.835 = f32[4,2,16,2,64,2]{5,4,3,2,1,0:T(8,128)} reshape(f32[8,32,128]{2,1,0:T(8,128)S(1)} %get-tuple-element.64) | data formatting | bytes 262144 | tf_op jit(solution)/shard_map/reshape | solution.py:45
  53.7 4.8 %collective-permute-start.6 = (f32[1,8,1,128]{3,1,2,0:T(8,128)S(1)}, f32[1,8,1,128]{3,1,2,0:T(8,128)S(1)}, u32[]{:S(2)}, u32[]{:S(2)}) collective-permute-start(f32[1,8,1,128]{3,1,2,0:T(8,128)S(1)} %get-tuple-element.79), channel_id=1, source_target_pairs={{0,4},{4,8},{8,12},{12,16},{16,20},{20,24},{24,28},{1,5},{5,9},{9,... | collective-permute-start | bytes 12296 | tf_op jit(solution)/shard_map/ppermute | solution.py:33
  67.9 4.5 %collective-permute-start.30 = (f32[1,2,1,32]{3,2,1,0:T(1,128)S(1)}, f32[1,2,1,32]{3,2,1,0:T(1,128)S(1)}, u32[]{:S(2)}, u32[]{:S(2)}) collective-permute-start(f32[1,2,1,32]{3,2,1,0:T(1,128)S(1)} %get-tuple-element.170), channel_id=1, source_target_pairs={{0,4},{4,8},{8,12},{12,16},{16,20},{20,24},{24,28},{1,5},{5,9},{9,... | collective-permute-start | bytes 776 | tf_op jit(solution)/shard_map/ppermute | solution.py:33
  84.6 4.9 %collective-permute-start.42 = (f32[1,1,1,16]{3,2,1,0:T(1,128)S(1)}, f32[1,1,1,16]{3,2,1,0:T(1,128)S(1)}, u32[]{:S(2)}, u32[]{:S(2)}) collective-permute-start(f32[1,1,1,16]{3,2,1,0:T(1,128)S(1)} %get-tuple-element.215), channel_id=1, source_target_pairs={{0,4},{4,8},{8,12},{12,16},{16,20},{20,24},{24,28},{1,5},{5,9},{9,... | collective-permute-start | bytes 200 | tf_op jit(solution)/shard_map/ppermute | solution.py:33
  93.3 7.6 %fusion.226 = (f32[8,32,128]{2,0,1:T(8,128)S(1)}, f32[8,32,128]{2,0,1:T(8,128)S(1)}, f32[8,32,128]{2,0,1:T(8,128)S(1)}, f32[1,8,32,128]{3,1,2,0:T(8,128)S(1)}, f...) fusion(f32[1,32,128]{2,0,1:T(1,128)S(1)} %bitcast.166, f32[7,32,128]{2,0,1:T(8,128)S(1)} %get-tuple-element.78, ...), kind=kLoop, calls=%fused_computation.330 | loop fusion | flops 983040 | bytes 1146928 | tf_op jit(solution)/shard_map/add | solution.py:66
  101.1 4.8 %collective-permute-start.2 = (f32[1,8,1,128]{3,1,2,0:T(8,128)S(1)}, f32[1,8,1,128]{3,1,2,0:T(8,128)S(1)}, u32[]{:S(2)}, u32[]{:S(2)}) collective-permute-start(f32[1,8,1,128]{3,1,2,0:T(8,128)S(1)} %get-tuple-element.72), channel_id=1, source_target_pairs={{0,4},{4,8},{8,12},{12,16},{16,20},{20,24},{24,28},{1,5},{5,9},{9,... | collective-permute-start | bytes 12296 | tf_op jit(solution)/shard_map/ppermute | solution.py:33
  113.9 4.2 %collective-permute-start.8 = (f32[3,1,32,128]{3,1,2,0:T(1,128)S(1)}, f32[3,1,32,128]{3,1,2,0:T(1,128)S(1)}, u32[]{:S(2)}, u32[]{:S(2)}) collective-permute-start(f32[3,1,32,128]{3,1,2,0:T(1,128)S(1)} %get-tuple-element.59), channel_id=1, source_target_pairs={{0,1},{1,2},{2,3},{4,5},{5,6},{6,7},{8,9},{9,10},{10,11},{12,13},{... | collective-permute-start | bytes 147464 | tf_op jit(solution)/shard_map/ppermute | solution.py:22
  119.4 4.5 %collective-permute-start.10 = (f32[3,8,1,128]{3,1,2,0:T(8,128)S(1)}, f32[3,8,1,128]{3,1,2,0:T(8,128)S(1)}, u32[]{:S(2)}, u32[]{:S(2)}) collective-permute-start(f32[3,8,1,128]{3,1,2,0:T(8,128)S(1)} %get-tuple-element.55), channel_id=1, source_target_pairs={{0,4},{4,8},{8,12},{12,16},{16,20},{20,24},{24,28},{1,5},{5,9},{9,... | collective-permute-start | bytes 36872 | tf_op jit(solution)/shard_map/ppermute | solution.py:33
  125.3 4.2 %collective-permute-done.11 = f32[3,8,1,128]{3,1,2,0:T(8,128)S(1)} collective-permute-done((f32[3,8,1,128]{3,1,2,0:T(8,128)S(1)}, f32[3,8,1,128]{3,1,2,0:T(8,128)S(1)}, u32[]{:S(2)}, u32[]{:S(2)}) %collective-permute-start.11) | collective-permute-done | bytes 12320 | tf_op jit(solution)/shard_map/ppermute | solution.py:33
  133.8 4.4 %collective-permute-start.14 = (f32[3,8,1,128]{3,1,2,0:T(8,128)S(1)}, f32[3,8,1,128]{3,1,2,0:T(8,128)S(1)}, u32[]{:S(2)}, u32[]{:S(2)}) collective-permute-start(f32[3,8,1,128]{3,1,2,0:T(8,128)S(1)} %get-tuple-element.45), channel_id=1, source_target_pairs={{0,4},{4,8},{8,12},{12,16},{16,20},{20,24},{24,28},{1,5},{5,9},{9,... | collective-permute-start | bytes 36872 | tf_op jit(solution)/shard_map/ppermute | solution.py:33
  144.4 26.5 %reshape.834 = f32[3,4,2,16,2,64,2]{6,5,4,3,2,1,0:T(8,128)} reshape(f32[3,8,32,128]{3,2,1,0:T(8,128)S(1)} %copy.175) | data formatting | bytes 786432 | tf_op jit(solution)/shard_map/reshape | solution.py:45
  171.0 9.4 %reduce_sum.95 = f32[3,4,16,64]{3,2,1,0:T(8,128)S(1)} reduce(f32[3,4,2,16,2,64,2]{6,5,4,3,2,1,0:T(8,128)} %reshape.834, f32[]{:T(128)} %constant.13.clone.1), dimensions={2,4,6}, to_apply=%region_0.1 | reduce | flops 86016 | bytes 442372 | tf_op jit(solution)/shard_map/reduce_sum | solution.py:48
  194.8 4.3 %collective-permute-start.24 = (f32[3,1,16,64]{3,2,1,0:T(8,128)S(1)}, f32[3,1,16,64]{3,2,1,0:T(8,128)S(1)}, u32[]{:S(2)}, u32[]{:S(2)}) collective-permute-start(f32[3,1,16,64]{3,2,1,0:T(8,128)S(1)} %get-tuple-element.104), channel_id=1, source_target_pairs={{0,1},{1,2},{2,3},{4,5},{5,6},{6,7},{8,9},{9,10},{10,11},{12,13},{... | collective-permute-start | bytes 36872 | tf_op jit(solution)/shard_map/ppermute | solution.py:22
  200.4 4.3 %collective-permute-start.26 = (f32[3,4,1,64]{3,2,1,0:T(1,128)S(1)}, f32[3,4,1,64]{3,2,1,0:T(1,128)S(1)}, u32[]{:S(2)}, u32[]{:S(2)}) collective-permute-start(f32[3,4,1,64]{3,2,1,0:T(1,128)S(1)} %get-tuple-element.100), channel_id=1, source_target_pairs={{0,4},{4,8},{8,12},{12,16},{16,20},{20,24},{24,28},{1,5},{5,9},{9,... | collective-permute-start | bytes 9224 | tf_op jit(solution)/shard_map/ppermute | solution.py:33
  217.1 4.3 %collective-permute-start.32 = (f32[3,1,8,32]{3,2,1,0:T(8,128)S(1)}, f32[3,1,8,32]{3,2,1,0:T(8,128)S(1)}, u32[]{:S(2)}, u32[]{:S(2)}) collective-permute-start(f32[3,1,8,32]{3,2,1,0:T(8,128)S(1)} %get-tuple-element.157), channel_id=1, source_target_pairs={{0,1},{1,2},{2,3},{4,5},{5,6},{6,7},{8,9},{9,10},{10,11},{12,13},{... | collective-permute-start | bytes 9224 | tf_op jit(solution)/shard_map/ppermute | solution.py:22
  232.6 4.3 %collective-permute-start.36 = (f32[3,1,8,32]{3,2,1,0:T(8,128)S(1)}, f32[3,1,8,32]{3,2,1,0:T(8,128)S(1)}, u32[]{:S(2)}, u32[]{:S(2)}) collective-permute-start(f32[3,1,8,32]{3,2,1,0:T(8,128)S(1)} %get-tuple-element.149), channel_id=1, source_target_pairs={{0,1},{1,2},{2,3},{4,5},{5,6},{6,7},{8,9},{9,10},{10,11},{12,13},{... | collective-permute-start | bytes 9224 | tf_op jit(solution)/shard_map/ppermute | solution.py:22
  238.1 4.3 %collective-permute-start.38 = (f32[3,2,1,32]{3,2,1,0:T(1,128)S(1)}, f32[3,2,1,32]{3,2,1,0:T(1,128)S(1)}, u32[]{:S(2)}, u32[]{:S(2)}) collective-permute-start(f32[3,2,1,32]{3,2,1,0:T(1,128)S(1)} %get-tuple-element.148), channel_id=1, source_target_pairs={{0,4},{4,8},{8,12},{12,16},{16,20},{20,24},{24,28},{1,5},{5,9},{9,... | collective-permute-start | bytes 2312 | tf_op jit(solution)/shard_map/ppermute | solution.py:33
  251.3 4.9 %collective-permute-start.44 = (f32[3,1,4,16]{3,2,0,1:T(4,128)S(1)}, f32[3,1,4,16]{3,2,0,1:T(4,128)S(1)}, u32[]{:S(2)}, u32[]{:S(2)}) collective-permute-start(f32[3,1,4,16]{3,2,0,1:T(4,128)S(1)} %fusion.198), channel_id=1, source_target_pairs={{0,1},{1,2},{2,3},{4,5},{5,6},{6,7},{8,9},{9,10},{10,11},{12,13},{... | collective-permute-start | bytes 2312 | tf_op jit(solution)/shard_map/ppermute | solution.py:22
  313.2 4.5 %collective-permute-start.62 = (f32[3,1,1,16]{3,2,0,1:T(1,128)S(1)}, f32[3,1,1,16]{3,2,0,1:T(1,128)S(1)}, u32[]{:S(2)}, u32[]{:S(2)}) collective-permute-start(f32[3,1,1,16]{3,2,0,1:T(1,128)S(1)} %get-tuple-element.176), channel_id=1, source_target_pairs={{0,4},{4,8},{8,12},{12,16},{16,20},{20,24},{24,28},{1,5},{5,9},{9,... | collective-permute-start | bytes 584 | tf_op jit(solution)/shard_map/ppermute | solution.py:33
  329.1 5.0 %collective-permute-done.67 = f32[3,2,1,32]{3,2,1,0:T(1,128)S(1)} collective-permute-done((f32[3,2,1,32]{3,2,1,0:T(1,128)S(1)}, f32[3,2,1,32]{3,2,1,0:T(1,128)S(1)}, u32[]{:S(2)}, u32[]{:S(2)}) %collective-permute-start.67) | collective-permute-done | bytes 800 | tf_op jit(solution)/shard_map/ppermute | solution.py:33
  340.9 4.5 %collective-permute-start.70 = (f32[3,4,1,64]{3,2,1,0:T(1,128)S(1)}, f32[3,4,1,64]{3,2,1,0:T(1,128)S(1)}, u32[]{:S(2)}, u32[]{:S(2)}) collective-permute-start(f32[3,4,1,64]{3,2,1,0:T(1,128)S(1)} %get-tuple-element.90), channel_id=1, source_target_pairs={{0,4},{4,8},{8,12},{12,16},{16,20},{20,24},{24,28},{1,5},{5,9},{9,... | collective-permute-start | bytes 9224 | tf_op jit(solution)/shard_map/ppermute | solution.py:33
  353.6 4.3 %collective-permute-start.72 = (f32[3,1,32,128]{3,1,2,0:T(1,128)S(1)}, f32[3,1,32,128]{3,1,2,0:T(1,128)S(1)}, u32[]{:S(2)}, u32[]{:S(2)}) collective-permute-start(f32[3,1,32,128]{3,1,2,0:T(1,128)S(1)} %get-tuple-element.39), channel_id=1, source_target_pairs={{0,1},{1,2},{2,3},{4,5},{5,6},{6,7},{8,9},{9,10},{10,11},{12,13},{... | collective-permute-start | bytes 147464 | tf_op jit(solution)/shard_map/ppermute | solution.py:22
  (361 shorter events, 218.2 us)
Async XLA Ops:
  6.1 60.5 %collective-permute-start.7 = (f32[1,8,1,128]{3,1,2,0:T(8,128)S(1)}, f32[1,8,1,128]{3,1,2,0:T(8,128)S(1)}, u32[]{:S(2)}, u32[]{:S(2)}) collective-permute-start(f32[1,8,1,128]{3,1,2,0:T(8,128)S(1)} %get-tuple-element.80), channel_id=1, source_target_pairs={{4,0},{8,4},{12,8},{16,12},{20,16},{24,20},{28,24},{5,1},{9,5},{13... | collective-permute-start | bytes 12296 | tf_op jit(solution)/shard_map/ppermute | solution.py:33
  21.3 38.5 %collective-permute-start.17 = (f32[1,1,16,64]{3,2,1,0:T(8,128)S(1)}, f32[1,1,16,64]{3,2,1,0:T(8,128)S(1)}, u32[]{:S(2)}, u32[]{:S(2)}) collective-permute-start(f32[1,1,16,64]{3,2,1,0:T(8,128)S(1)} %get-tuple-element.126), channel_id=1, source_target_pairs={{1,0},{2,1},{3,2},{5,4},{6,5},{7,6},{9,8},{10,9},{11,10},{13,12},{... | collective-permute-start | bytes 12296 | tf_op jit(solution)/shard_map/ppermute | solution.py:25
  22.6 37.2 %collective-permute-start.16 = (f32[1,1,16,64]{3,2,1,0:T(8,128)S(1)}, f32[1,1,16,64]{3,2,1,0:T(8,128)S(1)}, u32[]{:S(2)}, u32[]{:S(2)}) collective-permute-start(f32[1,1,16,64]{3,2,1,0:T(8,128)S(1)} %get-tuple-element.125), channel_id=1, source_target_pairs={{0,1},{1,2},{2,3},{4,5},{5,6},{6,7},{8,9},{9,10},{10,11},{12,13},{... | collective-permute-start | bytes 12296 | tf_op jit(solution)/shard_map/ppermute | solution.py:22
  25.7 28.1 %collective-permute-start.19 = (f32[1,4,1,64]{3,2,1,0:T(1,128)S(1)}, f32[1,4,1,64]{3,2,1,0:T(1,128)S(1)}, u32[]{:S(2)}, u32[]{:S(2)}) collective-permute-start(f32[1,4,1,64]{3,2,1,0:T(1,128)S(1)} %get-tuple-element.130), channel_id=1, source_target_pairs={{4,0},{8,4},{12,8},{16,12},{20,16},{24,20},{28,24},{5,1},{9,5},{13... | collective-permute-start | bytes 3080 | tf_op jit(solution)/shard_map/ppermute | solution.py:33
  27.0 31.6 %collective-permute-start.18 = (f32[1,4,1,64]{3,1,2,0:T(4,128)S(1)}, f32[1,4,1,64]{3,1,2,0:T(4,128)S(1)}, u32[]{:S(2)}, u32[]{:S(2)}) collective-permute-start(f32[1,4,1,64]{3,1,2,0:T(4,128)S(1)} %bitcast.178), channel_id=1, source_target_pairs={{0,4},{4,8},{8,12},{12,16},{16,20},{20,24},{24,28},{1,5},{5,9},{9,... | collective-permute-start | bytes 3080 | tf_op jit(solution)/shard_map/ppermute | solution.py:33
  53.7 14.2 %collective-permute-start.6 = (f32[1,8,1,128]{3,1,2,0:T(8,128)S(1)}, f32[1,8,1,128]{3,1,2,0:T(8,128)S(1)}, u32[]{:S(2)}, u32[]{:S(2)}) collective-permute-start(f32[1,8,1,128]{3,1,2,0:T(8,128)S(1)} %get-tuple-element.79), channel_id=1, source_target_pairs={{0,4},{4,8},{8,12},{12,16},{16,20},{20,24},{24,28},{1,5},{5,9},{9,... | collective-permute-start | bytes 12296 | tf_op jit(solution)/shard_map/ppermute | solution.py:33
  58.5 34.8 %collective-permute-start.5 = (f32[1,1,32,128]{3,2,1,0:T(8,128)S(1)}, f32[1,1,32,128]{3,2,1,0:T(8,128)S(1)}, u32[]{:S(2)}, u32[]{:S(2)}) collective-permute-start(f32[1,1,32,128]{3,2,1,0:T(8,128)S(1)} %bitcast.169), channel_id=1, source_target_pairs={{1,0},{2,1},{3,2},{5,4},{6,5},{7,6},{9,8},{10,9},{11,10},{13,12},{... | collective-permute-start | bytes 49160 | tf_op jit(solution)/shard_map/ppermute | solution.py:25
  61.3 16.9 %collective-permute-start.28 = (f32[1,1,8,32]{3,2,1,0:T(8,128)S(1)}, f32[1,1,8,32]{3,2,1,0:T(8,128)S(1)}, u32[]{:S(2)}, u32[]{:S(2)}) collective-permute-start(f32[1,1,8,32]{3,2,1,0:T(8,128)S(1)} %get-tuple-element.166), channel_id=1, source_target_pairs={{0,1},{1,2},{2,3},{4,5},{5,6},{6,7},{8,9},{9,10},{10,11},{12,13},{... | collective-permute-start | bytes 3080 | tf_op jit(solution)/shard_map/ppermute | solution.py:22
  65.3 12.9 %collective-permute-start.29 = (f32[1,1,8,32]{3,2,1,0:T(8,128)S(1)}, f32[1,1,8,32]{3,2,1,0:T(8,128)S(1)}, u32[]{:S(2)}, u32[]{:S(2)}) collective-permute-start(f32[1,1,8,32]{3,2,1,0:T(8,128)S(1)} %get-tuple-element.169), channel_id=1, source_target_pairs={{1,0},{2,1},{3,2},{5,4},{6,5},{7,6},{9,8},{10,9},{11,10},{13,12},{... | collective-permute-start | bytes 3080 | tf_op jit(solution)/shard_map/ppermute | solution.py:25
  74.5 18.8 %collective-permute-start.4 = (f32[1,1,32,128]{3,2,1,0:T(8,128)S(1)}, f32[1,1,32,128]{3,2,1,0:T(8,128)S(1)}, u32[]{:S(2)}, u32[]{:S(2)}) collective-permute-start(f32[1,1,32,128]{3,2,1,0:T(8,128)S(1)} %bitcast.168), channel_id=1, source_target_pairs={{0,1},{1,2},{2,3},{4,5},{5,6},{6,7},{8,9},{9,10},{10,11},{12,13},{... | collective-permute-start | bytes 49160 | tf_op jit(solution)/shard_map/ppermute | solution.py:22
  113.9 15.7 %collective-permute-start.8 = (f32[3,1,32,128]{3,1,2,0:T(1,128)S(1)}, f32[3,1,32,128]{3,1,2,0:T(1,128)S(1)}, u32[]{:S(2)}, u32[]{:S(2)}) collective-permute-start(f32[3,1,32,128]{3,1,2,0:T(1,128)S(1)} %get-tuple-element.59), channel_id=1, source_target_pairs={{0,1},{1,2},{2,3},{4,5},{5,6},{6,7},{8,9},{9,10},{10,11},{12,13},{... | collective-permute-start | bytes 147464 | tf_op jit(solution)/shard_map/ppermute | solution.py:22
  130.6 13.2 %collective-permute-start.12 = (f32[3,1,32,128]{3,1,2,0:T(1,128)S(1)}, f32[3,1,32,128]{3,1,2,0:T(1,128)S(1)}, u32[]{:S(2)}, u32[]{:S(2)}) collective-permute-start(f32[3,1,32,128]{3,1,2,0:T(1,128)S(1)} %get-tuple-element.49), channel_id=1, source_target_pairs={{0,1},{1,2},{2,3},{4,5},{5,6},{6,7},{8,9},{9,10},{10,11},{12,13},{... | collective-permute-start | bytes 147464 | tf_op jit(solution)/shard_map/ppermute | solution.py:22
  180.7 13.7 %collective-permute-start.20 = (f32[3,1,16,64]{3,2,1,0:T(8,128)S(1)}, f32[3,1,16,64]{3,2,1,0:T(8,128)S(1)}, u32[]{:S(2)}, u32[]{:S(2)}) collective-permute-start(f32[3,1,16,64]{3,2,1,0:T(8,128)S(1)} %get-tuple-element.114), channel_id=1, source_target_pairs={{0,1},{1,2},{2,3},{4,5},{5,6},{6,7},{8,9},{9,10},{10,11},{12,13},{... | collective-permute-start | bytes 36872 | tf_op jit(solution)/shard_map/ppermute | solution.py:22
  194.8 15.5 %collective-permute-start.24 = (f32[3,1,16,64]{3,2,1,0:T(8,128)S(1)}, f32[3,1,16,64]{3,2,1,0:T(8,128)S(1)}, u32[]{:S(2)}, u32[]{:S(2)}) collective-permute-start(f32[3,1,16,64]{3,2,1,0:T(8,128)S(1)} %get-tuple-element.104), channel_id=1, source_target_pairs={{0,1},{1,2},{2,3},{4,5},{5,6},{6,7},{8,9},{9,10},{10,11},{12,13},{... | collective-permute-start | bytes 36872 | tf_op jit(solution)/shard_map/ppermute | solution.py:22
  217.1 14.5 %collective-permute-start.32 = (f32[3,1,8,32]{3,2,1,0:T(8,128)S(1)}, f32[3,1,8,32]{3,2,1,0:T(8,128)S(1)}, u32[]{:S(2)}, u32[]{:S(2)}) collective-permute-start(f32[3,1,8,32]{3,2,1,0:T(8,128)S(1)} %get-tuple-element.157), channel_id=1, source_target_pairs={{0,1},{1,2},{2,3},{4,5},{5,6},{6,7},{8,9},{9,10},{10,11},{12,13},{... | collective-permute-start | bytes 9224 | tf_op jit(solution)/shard_map/ppermute | solution.py:22
  232.6 15.4 %collective-permute-start.36 = (f32[3,1,8,32]{3,2,1,0:T(8,128)S(1)}, f32[3,1,8,32]{3,2,1,0:T(8,128)S(1)}, u32[]{:S(2)}, u32[]{:S(2)}) collective-permute-start(f32[3,1,8,32]{3,2,1,0:T(8,128)S(1)} %get-tuple-element.149), channel_id=1, source_target_pairs={{0,1},{1,2},{2,3},{4,5},{5,6},{6,7},{8,9},{9,10},{10,11},{12,13},{... | collective-permute-start | bytes 9224 | tf_op jit(solution)/shard_map/ppermute | solution.py:22
  250.0 14.8 %collective-permute-start.45 = (f32[3,1,4,16]{3,2,0,1:T(4,128)S(1)}, f32[3,1,4,16]{3,2,0,1:T(4,128)S(1)}, u32[]{:S(2)}, u32[]{:S(2)}) collective-permute-start(f32[3,1,4,16]{3,2,0,1:T(4,128)S(1)} %fusion.198), channel_id=1, source_target_pairs={{1,0},{2,1},{3,2},{5,4},{6,5},{7,6},{9,8},{10,9},{11,10},{13,12},{... | collective-permute-start | bytes 2312 | tf_op jit(solution)/shard_map/ppermute | solution.py:25
  251.3 13.5 %collective-permute-start.44 = (f32[3,1,4,16]{3,2,0,1:T(4,128)S(1)}, f32[3,1,4,16]{3,2,0,1:T(4,128)S(1)}, u32[]{:S(2)}, u32[]{:S(2)}) collective-permute-start(f32[3,1,4,16]{3,2,0,1:T(4,128)S(1)} %fusion.198), channel_id=1, source_target_pairs={{0,1},{1,2},{2,3},{4,5},{5,6},{6,7},{8,9},{9,10},{10,11},{12,13},{... | collective-permute-start | bytes 2312 | tf_op jit(solution)/shard_map/ppermute | solution.py:22
  265.6 13.9 %collective-permute-start.49 = (f32[3,1,4,16]{3,2,0,1:T(4,128)S(1)}, f32[3,1,4,16]{3,2,0,1:T(4,128)S(1)}, u32[]{:S(2)}, u32[]{:S(2)}) collective-permute-start(f32[3,1,4,16]{3,2,0,1:T(4,128)S(1)} %fusion.156), channel_id=1, source_target_pairs={{1,0},{2,1},{3,2},{5,4},{6,5},{7,6},{9,8},{10,9},{11,10},{13,12},{... | collective-permute-start | bytes 2312 | tf_op jit(solution)/shard_map/ppermute | solution.py:25
  280.3 12.7 %collective-permute-start.53 = (f32[3,1,4,16]{3,2,0,1:T(4,128)S(1)}, f32[3,1,4,16]{3,2,0,1:T(4,128)S(1)}, u32[]{:S(2)}, u32[]{:S(2)}) collective-permute-start(f32[3,1,4,16]{3,2,0,1:T(4,128)S(1)} %fusion.166), channel_id=1, source_target_pairs={{1,0},{2,1},{3,2},{5,4},{6,5},{7,6},{9,8},{10,9},{11,10},{13,12},{... | collective-permute-start | bytes 2312 | tf_op jit(solution)/shard_map/ppermute | solution.py:25
  293.9 12.7 %collective-permute-start.57 = (f32[3,1,4,16]{3,2,0,1:T(4,128)S(1)}, f32[3,1,4,16]{3,2,0,1:T(4,128)S(1)}, u32[]{:S(2)}, u32[]{:S(2)}) collective-permute-start(f32[3,1,4,16]{3,2,0,1:T(4,128)S(1)} %fusion.176), channel_id=1, source_target_pairs={{1,0},{2,1},{3,2},{5,4},{6,5},{7,6},{9,8},{10,9},{11,10},{13,12},{... | collective-permute-start | bytes 2312 | tf_op jit(solution)/shard_map/ppermute | solution.py:25
  320.1 14.0 %collective-permute-start.64 = (f32[3,1,8,32]{3,2,1,0:T(8,128)S(1)}, f32[3,1,8,32]{3,2,1,0:T(8,128)S(1)}, u32[]{:S(2)}, u32[]{:S(2)}) collective-permute-start(f32[3,1,8,32]{3,2,1,0:T(8,128)S(1)} %get-tuple-element.141), channel_id=1, source_target_pairs={{0,1},{1,2},{2,3},{4,5},{5,6},{6,7},{8,9},{9,10},{10,11},{12,13},{... | collective-permute-start | bytes 9224 | tf_op jit(solution)/shard_map/ppermute | solution.py:22
  336.6 14.3 %collective-permute-start.68 = (f32[3,1,16,64]{3,2,1,0:T(8,128)S(1)}, f32[3,1,16,64]{3,2,1,0:T(8,128)S(1)}, u32[]{:S(2)}, u32[]{:S(2)}) collective-permute-start(f32[3,1,16,64]{3,2,1,0:T(8,128)S(1)} %get-tuple-element.94), channel_id=1, source_target_pairs={{0,1},{1,2},{2,3},{4,5},{5,6},{6,7},{8,9},{9,10},{10,11},{12,13},{... | collective-permute-start | bytes 36872 | tf_op jit(solution)/shard_map/ppermute | solution.py:22
  353.6 14.3 %collective-permute-start.72 = (f32[3,1,32,128]{3,1,2,0:T(1,128)S(1)}, f32[3,1,32,128]{3,1,2,0:T(1,128)S(1)}, u32[]{:S(2)}, u32[]{:S(2)}) collective-permute-start(f32[3,1,32,128]{3,1,2,0:T(1,128)S(1)} %get-tuple-element.39), channel_id=1, source_target_pairs={{0,1},{1,2},{2,3},{4,5},{5,6},{6,7},{8,9},{9,10},{10,11},{12,13},{... | collective-permute-start | bytes 147464 | tf_op jit(solution)/shard_map/ppermute | solution.py:22
  (87 other events, 3238.0 us)
where the time goes:
time: 376 us; the launch traced here: 371 us
  starting transfers between devices  194 us (52%)
  local copies, waits for them, and re-layouts  61.4 us (16%)
  waiting for transfers between devices  58.8 us (16%)
  other arithmetic  54.1 us (14%)
    ppermute x38, starting transfers between devices, passed_along(): return lax.ppermute(x, axis, pairs)  103 us
    ppermute x19, starting transfers between devices, with_halo(): lax.ppermute(lax.slice_in_dim(block, block.shape[dim] - width, None, axis...  67.2 us
    ppermute x38, waiting for transfers between devices, passed_along(): return lax.ppermute(x, axis, pairs)  56 us
    reshape x5, local copies, waits for them, and re-layouts, block_sum(): field.reshape(dims_now[0], dims_now[1] // 2, 2, dims_now[2] // 2, 2, dims...  51.2 us
    ppermute x19, starting transfers between devices, with_halo(): lax.ppermute(lax.slice_in_dim(block, 0, width, axis=dim), axis, backward)  24.5 us
    reduce_sum x13, other arithmetic, block_sum(): return shaped.sum(axis=(2, 4, 6))  20.8 us
    add x5, other arithmetic, coefficients(): low_face + high_face  10.8 us
  transfers between devices with their start and end apart: 76, of which 16 were waited for; matrix products, arithmetic and copies ran while one was open for 11% of the time, Pallas kernels for 0%

commit v1 on v0

v1 whole, which is shorter than its diff:
```python
import functools

import jax
import jax.numpy as jnp
from jax import lax
from jax.experimental import pallas as pl
from jax.experimental.pallas import tpu as pltpu
from jax.sharding import PartitionSpec as P

PENALTY = 50.0
OMEGA = 0.6
COARSE_SWEEPS = 6
LANES = 128
HALO = 9
REACH = 16
F32 = jnp.float32


def chunks(start, stop, size):
    return [(row, min(size, stop - row)) for row in range(start, stop, size)]


def lane_of(rows):
    return lax.broadcasted_iota(jnp.int32, (rows, LANES), 1)


def roll(x, shift):
    return pltpu.roll(x, shift % LANES, 1)


def rows_at(ref, layer, row, count):
    return ref[layer, pl.ds(row, count), :]


def cross_faces(s_ref, layer, row, count):
    here = rows_at(s_ref, layer, row, count)
    return here, [
        here + rows_at(s_ref, layer - 1, row, count),
        here + rows_at(s_ref, layer + 1, row, count),
        here + rows_at(s_ref, layer, row - 1, count),
        here + rows_at(s_ref, layer, row + 1, count),
    ]


def lane_faces(here, step):
    lane = lane_of(here.shape[0])
    first, last = lane < step, lane >= LANES - step
    low = here + jnp.where(first, 0.0, roll(here, step))
    high = here + jnp.where(last, 0.0, roll(here, -step))
    return low, high, jnp.where(first, 0.0, low), jnp.where(last, 0.0, high)


def neighbours(v_ref, faces, layer, row, count, step):
    here = rows_at(v_ref, layer, row, count)
    along = [
        faces[0] * rows_at(v_ref, layer - 1, row, count)
        + faces[1] * rows_at(v_ref, layer + 1, row, count),
        faces[2] * rows_at(v_ref, layer, row - 1, count)
        + faces[3] * rows_at(v_ref, layer, row + 1, count),
        faces[4] * roll(here, step) + faces[5] * roll(here, -step),
    ]
    return here, along


def total(along, component):
    return (along[0] + along[1] + along[2]) + along[component]


def safe_rate(here, doubled):
    return jnp.where(here > 0.0, OMEGA / doubled, 0.0)


def pair_lanes(x, step):
    upper = (lane_of(x.shape[0]) & step) != 0
    return x + jnp.where(upper, roll(x, step), roll(x, -step))


def pair_rows(ref, row, count):
    return ref[pl.ds(row, count, stride=2), :] + ref[pl.ds(row + 1, count, stride=2), :]


def spread_rows(ref, x):
    count = x.shape[0]
    ref[pl.ds(0, count, stride=2), :] = x
    ref[pl.ds(1, count, stride=2), :] = x


def level_setup(s_ref, p_ref, r_ref, d_ref, g_ref, y_ref, b_of, layer, row, count, step):
    here, cross = cross_faces(s_ref, layer, row, count)
    low, high, low_in, high_in = lane_faces(here, step)
    y_ref[0, layer, pl.ds(row, count), :] = low_in
    y_ref[1, layer, pl.ds(row, count), :] = high_in
    sums = [cross[0] + cross[1], cross[2] + cross[3], low + high]
    base = rows_at(p_ref, layer, row, count) + (sums[0] + sums[1] + sums[2])
    for c in range(3):
        doubled = base + sums[c]
        rate = safe_rate(here, doubled)
        d_ref[c, layer, pl.ds(row, count), :] = doubled
        r_ref[c, layer, pl.ds(row, count), :] = rate
        g_ref[c, layer, pl.ds(row, count), :] = (2.0 * rate) * b_of(c)


def all_faces(s_ref, y_ref, layer, row, count):
    _, cross = cross_faces(s_ref, layer, row, count)
    return cross + [
        y_ref[0, layer, pl.ds(row, count), :],
        y_ref[1, layer, pl.ds(row, count), :],
    ]


def first_sweep(s_ref, y_ref, r_ref, g_ref, v_ref, layer, row, count, step):
    faces = all_faces(s_ref, y_ref, layer, row, count)
    for c in range(3):
        here, along = neighbours(g_ref.at[c], faces, layer, row, count, step)
        rate = r_ref[c, layer, pl.ds(row, count), :]
        v_ref[c, layer, pl.ds(row, count), :] = (2.0 - OMEGA) * here + rate * total(along, c)


def remainder(s_ref, y_ref, b_ref, d_ref, v_ref, layer, row, count, step):
    faces = all_faces(s_ref, y_ref, layer, row, count)
    result = []
    for c in range(3):
        here, along = neighbours(v_ref.at[c], faces, layer, row, count, step)
        doubled = d_ref[c, layer, pl.ds(row, count), :]
        source = b_ref[c, layer, pl.ds(row, count), :]
        result.append(source + 0.5 * (total(along, c) - doubled * here))
    return result


def down_kernel(
    heights, tiles, bz, bx,
    x_ref, table_ref, strain_ref,
    send_ref, s0_out, y0_out, v0_out, g0_out, r0_out, s1_out, y1_out, v1_out, g1_out, r1_out,
    s, p, st, b, r, d, g, y, v, tmp, s1, p1, b1, r1, d1, g1, y1, v1, sem,
):
    h, t = lax.axis_index("height"), lax.axis_index("tile")
    nz, n1 = bz + 2 * HALO, bz // 2 + 8
    bx1, bx2 = bx // 2, bx // 4
    low, high = 8, bx + 24
    own_rows, halo_rows = (bz + 2) * bx, (bz + 2) * HALO
    before = jnp.where(t > 0, 1.0, 0.0)
    behind = jnp.where(t < tiles - 1, 1.0, 0.0)

    def read_layer(layer, carry):
        z = bz * h - HALO + layer
        inside = jnp.where((z >= 0) & (z < heights * bz), 1.0, 0.0)
        bottom = jnp.where((z >= 0) & (z < 2), 2.0 * PENALTY, 0.0)
        z_in = jnp.clip(z, 0, heights * bz - 1)
        brick, slot = z_in // bz, z_in % bz
        clamp_slot = bz + jnp.clip(z, 0, 1)
        parts = [
            (slot * bx, clamp_slot * bx, bx, 16, 1.0),
            (own_rows + slot * HALO, own_rows + clamp_slot * HALO, HALO, 16 - HALO, before),
            (own_rows + halo_rows + slot * HALO, own_rows + halo_rows + clamp_slot * HALO, HALO, 16 + bx, behind),
        ]
        for at, clamp_at, count, to, valid in parts:
            label = x_ref[brick, pl.ds(at, count), :]
            is0, is1 = label == 0, label == 1
            weight = inside * valid
            stiff = [table_ref[k] * weight for k in range(3)]
            dst = pl.ds(to, count)
            s[layer, dst, :] = jnp.where(is0, stiff[0], jnp.where(is1, stiff[1], stiff[2]))
            for c in range(3):
                e = [stiff[k] * strain_ref[k, c] for k in range(3)]
                st[c, layer, dst, :] = jnp.where(is0, e[0], jnp.where(is1, e[1], e[2]))
            joined = x_ref[0, pl.ds(clamp_at, count), :].astype(F32)
            p[layer, dst, :] = joined * (bottom * valid)
        return carry

    lax.fori_loop(0, nz, read_layer, 0)

    def setup0(layer, carry):
        for row, count in chunks(low, high, 16):
            lane = lane_of(count)
            here = st[2, layer, pl.ds(row, count), :]
            source = [
                0.5 * (rows_at(st.at[0], layer - 1, row, count) - rows_at(st.at[0], layer + 1, row, count)),
                0.5 * (rows_at(st.at[1], layer, row - 1, count) - rows_at(st.at[1], layer, row + 1, count)),
                0.5 * (jnp.where(lane < 1, 0.0, roll(here, 1)) - jnp.where(lane >= LANES - 1, 0.0, roll(here, -1))),
            ]
            for c in range(3):
                b[c, layer, pl.ds(row, count), :] = source[c]
            level_setup(s, p, r, d, g, y, lambda c: source[c], layer, row, count, 1)
        return carry

    lax.fori_loop(1, nz - 1, setup0, 0)

    def sweep0(layer, carry):
        for row, count in chunks(low, high, 16):
            first_sweep(s, y, r, g, v, layer, row, count, 1)
        return carry

    lax.fori_loop(2, nz - 2, sweep0, 0)

    own = (pl.ds(HALO, bz), pl.ds(16, bx))
    near = (pl.ds(HALO - 1, bz + 2), pl.ds(low, bx + 16))
    copies = [
        (s.at[near[0], near[1]], s0_out),
        (y.at[:, own[0], own[1]], y0_out),
        (v.at[:, near[0], near[1]], v0_out),
        (g.at[:, own[0], own[1]], g0_out),
        (r.at[:, own[0], own[1]], r0_out),
    ]
    started = []
    for k, (src, dst) in enumerate(copies):
        started.append(pltpu.make_async_copy(src, dst, sem.at[k]))
        started[-1].start()

    rows1 = bx1 + 8

    def restrict0(j, carry):
        layer = 3 + 2 * j
        for row, count in chunks(low, high, 16):
            one = remainder(s, y, b, d, v, layer, row, count, 1)
            two = remainder(s, y, b, d, v, layer + 1, row, count, 1)
            for c in range(3):
                tmp[c, pl.ds(row, count), :] = one[c] + two[c]
        for c in range(3):
            b1[c, j + 1, pl.ds(8, rows1), :] = pair_lanes(pair_rows(tmp.at[c], low, rows1), 1)
        return carry

    lax.fori_loop(0, n1 - 2, restrict0, 0)

    def coarse0(k, carry):
        for field, scale, into in ((s, 0.5, s1), (p, 1.0, p1)):
            both = [pair_rows(field.at[1 + 2 * k + i], low, rows1) for i in range(2)]
            into[k, pl.ds(8, rows1), :] = scale * pair_lanes(both[0] + both[1], 1)
        return carry

    lax.fori_loop(0, n1, coarse0, 0)

    def setup1(layer, carry):
        level_setup(
            s1, p1, r1, d1, g1, y1,
            lambda c: b1[c, layer, pl.ds(8, rows1), :], layer, 8, rows1, 2,
        )
        return carry

    lax.fori_loop(1, n1 - 1, setup1, 0)

    def sweep1(layer, carry):
        first_sweep(s1, y1, r1, g1, v1, layer, 8, rows1, 2)
        return carry

    lax.fori_loop(2, n1 - 2, sweep1, 0)

    copies = [
        (s1.at[pl.ds(2, n1 - 4), pl.ds(8, rows1)], s1_out),
        (y1.at[:, pl.ds(3, n1 - 6), pl.ds(8, rows1)], y1_out),
        (v1.at[:, pl.ds(2, n1 - 4), pl.ds(8, rows1)], v1_out),
        (g1.at[:, pl.ds(3, n1 - 6), pl.ds(8, rows1)], g1_out),
        (r1.at[:, pl.ds(3, n1 - 6), pl.ds(8, rows1)], r1_out),
    ]
    for k, (src, dst) in enumerate(copies):
        started.append(pltpu.make_async_copy(src, dst, sem.at[5 + k]))
        started[-1].start()

    lane = lane_of(bx2) & 3
    packed = []
    for m in range(bz // 4):
        layer = 4 + 2 * m
        one = remainder(s1, y1, b1, d1, v1, layer, 8, rows1, 2)
        two = remainder(s1, y1, b1, d1, v1, layer + 1, 8, rows1, 2)
        fields = []
        for c in range(3):
            tmp[c, pl.ds(0, rows1), :] = one[c] + two[c]
            fields.append(pair_lanes(pair_rows(tmp.at[c], 4, bx2), 2))
        both = [pair_rows(s1.at[layer + i], 12, bx2) for i in range(2)]
        stiff = 0.5 * pair_lanes(both[0] + both[1], 2)
        packed.append(
            jnp.where(lane == 0, fields[0], jnp.where(lane == 1, fields[1], jnp.where(lane == 2, fields[2], stiff)))
        )
    both = [pair_rows(p1.at[4 + i], 12, bx2) for i in range(2)]
    packed.append(pair_lanes(both[0] + both[1], 2))

    def fill(i, carry):
        for m, value in enumerate(packed):
            send_ref[i, m, :, :] = value
        return carry

    lax.fori_loop(0, heights * tiles, fill, 0)
    for copy in started:
        copy.wait()


def up_kernel(
    heights, tiles, bz, bx,
    recv_ref, s0_in, y0_in, v0_in, g0_in, r0_in, s1_in, y1_in, v1_in, g1_in, r1_in,
    out_ref,
    s0, y0, v0, g0, r0, s1, y1, v1, g1, r1, f1, s2, p2, b2, q2, r2, d2, g2, v2, f2, s3, p3, b3, q3, r3, g3, va, vb, tmp, sem,
):
    h, t = lax.axis_index("height"), lax.axis_index("tile")
    bx1, bx2, bz2 = bx // 2, bx // 4, bz // 4
    n1, n2, n3 = bz // 2 + 4, heights * bz // 4, heights * bz // 8
    rows1 = bx1 + 8
    near = pl.ds(8, bx + 16)
    own = pl.ds(16, bx)
    mid = pl.ds(8, rows1)
    copies = [
        (s1_in, s1.at[:, mid]), (y1_in, y1.at[:, pl.ds(1, n1 - 2), mid]), (v1_in, v1.at[:, :, mid]),
        (g1_in, g1.at[:, pl.ds(1, n1 - 2), mid]), (r1_in, r1.at[:, pl.ds(1, n1 - 2), mid]),
        (s0_in, s0.at[:, near]), (y0_in, y0.at[:, pl.ds(1, bz), own]), (v0_in, v0.at[:, :, near]),
        (g0_in, g0.at[:, pl.ds(1, bz), own]), (r0_in, r0.at[:, pl.ds(1, bz), own]),
    ]
    started = []
    for k, (src, dst) in enumerate(copies):
        started.append(pltpu.make_async_copy(src, dst, sem.at[k]))
        started[-1].start()

    for ref in (s2, p2, g2, v2, f2, s3, p3, g3, va, vb):
        ref[...] = jnp.zeros(ref.shape, F32)
    tmp[...] = jnp.zeros(tmp.shape, F32)

    side = REACH // bx2
    lane = lane_of(bx2) & 3
    for dt in range(-side, side + 1):
        other = t + dt
        valid = (other >= 0) & (other < tiles)
        other = jnp.clip(other, 0, tiles - 1)
        scale = jnp.where(valid, 1.0, 0.0)
        dst = pl.ds(8 + (dt + side) * bx2, bx2)
        for hh in range(heights):
            for m in range(bz2):
                x = recv_ref[other * heights + hh, m] * scale
                layer = 1 + hh * bz2 + m
                b2[layer, dst, :] = jnp.where(lane == 3, 0.0, x)
                s2[layer, dst, :] = jnp.where(
                    lane == 3, x, jnp.where(lane == 2, roll(x, -1), jnp.where(lane == 1, roll(x, -2), roll(x, -3)))
                )
        p2[1, dst, :] = recv_ref[other * heights, bz2] * scale

    def weights(count):
        kind = lane_of(count) & 3
        return [jnp.where(kind == c, 2.0, 1.0) for c in range(3)]

    def setup(s_ref, p_ref, b_ref, q_ref, r_ref, d_ref, g_ref, layer, row, count, step):
        here, cross = cross_faces(s_ref, layer, row, count)
        low, high, low_in, high_in = lane_faces(here, step)
        w = weights(count)
        dst = pl.ds(row, count)
        for k in range(4):
            q_ref[k, layer, dst, :] = w[k // 2] * cross[k]
        q_ref[4, layer, dst, :] = w[2] * low_in
        q_ref[5, layer, dst, :] = w[2] * high_in
        doubled = rows_at(p_ref, layer, row, count) + (
            w[0] * (cross[0] + cross[1]) + w[1] * (cross[2] + cross[3]) + w[2] * (low + high)
        )
        rate = safe_rate(here, doubled)
        r_ref[layer, dst, :] = rate
        if d_ref is not None:
            d_ref[layer, dst, :] = doubled
        g_ref[layer, dst, :] = (2.0 * rate) * rows_at(b_ref, layer, row, count)

    def packed_sum(v_ref, q_ref, layer, row, count, step):
        faces = [q_ref[k, layer, pl.ds(row, count), :] for k in range(6)]
        here, along = neighbours(v_ref, faces, layer, row, count, step)
        return here, along[0] + along[1] + along[2]

    rows2 = bx2 + 2 * REACH

    def setup2(layer, carry):
        setup(s2, p2, b2, q2, r2, d2, g2, layer, 8, rows2, 4)
        return carry

    lax.fori_loop(1, n2 + 1, setup2, 0)

    def sweep2(layer, carry):
        here, total_ = packed_sum(g2, q2, layer, 8, rows2, 4)
        v2[layer, pl.ds(8, rows2), :] = (2.0 - OMEGA) * here + rows_at(r2, layer, 8, rows2) * total_
        return carry

    lax.fori_loop(1, n2 + 1, sweep2, 0)

    rows3 = -(-(rows2 // 2) // 8) * 8

    def restrict2(j, carry):
        rest = 0.0
        for i in range(2):
            layer = 1 + 2 * j + i
            here, total_ = packed_sum(v2, q2, layer, 8, rows2, 4)
            rest = rest + rows_at(b2, layer, 8, rows2) + 0.5 * (total_ - rows_at(d2, layer, 8, rows2) * here)
        tmp[0, pl.ds(8, rows2), :] = rest
        dst = pl.ds(8, rows3)
        b3[j + 1, dst, :] = pair_lanes(pair_rows(tmp.at[0], 8, rows3), 4)
        for field, scale, into in ((s2, 0.5, s3), (p2, 1.0, p3)):
            both = [pair_rows(field.at[1 + 2 * j + i], 8, rows3) for i in range(2)]
            into[j + 1, dst, :] = scale * pair_lanes(both[0] + both[1], 4)
        return carry

    lax.fori_loop(0, n3, restrict2, 0)

    for layer in range(1, n3 + 1):
        setup(s3, p3, b3, q3, r3, None, g3, layer, 8, rows3, 8)
    source, target = g3, va
    for _ in range(COARSE_SWEEPS - 1):
        for layer in range(1, n3 + 1):
            here, total_ = packed_sum(source, q3, layer, 8, rows3, 8)
            target[layer, pl.ds(8, rows3), :] = (
                (1.0 - OMEGA) * here + rows_at(g3, layer, 8, rows3) + rows_at(r3, layer, 8, rows3) * total_
            )
        source, target = target, (vb if target is va else va)
    coarse = source

    wide2 = bx2 + 16

    def lift2(layer, carry):
        spread_rows(tmp.at[0], coarse[(layer + 1) // 2, pl.ds(12, wide2 // 2), :])
        v2[layer, pl.ds(16, wide2), :] += tmp[0, pl.ds(0, wide2), :]
        return carry

    lax.fori_loop(1, n2 + 1, lift2, 0)

    def post2(layer, carry):
        here, total_ = packed_sum(v2, q2, layer, 16, wide2, 4)
        f2[layer, pl.ds(16, wide2), :] = (
            (1.0 - OMEGA) * here + rows_at(g2, layer, 16, wide2) + rows_at(r2, layer, 16, wide2) * total_
        )
        return carry

    lax.fori_loop(1, n2 + 1, post2, 0)

    for copy in started[:5]:
        copy.wait()
    kind = lane_of(bx2 + 4) & 3

    def lift1(m, carry):
        x = f2[bz2 * h + m, pl.ds(22, bx2 + 4), :]
        moved = {shift: roll(x, shift) if shift else x for shift in range(-2, 4)}
        for c in range(3):
            part = jnp.where(
                kind == 0, moved[-c], jnp.where(kind == 1, moved[1 - c], jnp.where(kind == 2, moved[2 - c], moved[3 - c]))
            )
            spread_rows(tmp.at[c], part)
            lifted = tmp[c, pl.ds(0, rows1), :]
            for i in range(2):
                v1[c, 2 * m + i, mid, :] += lifted
        return carry

    lax.fori_loop(0, n1 // 2, lift1, 0)

    def post(s_ref, y_ref, g_ref, r_ref, v_ref, into, layer, to, row, count, step):
        faces = all_faces(s_ref, y_ref, layer, row, count)
        for c in range(3):
            here, along = neighbours(v_ref.at[c], faces, layer, row, count, step)
            dst = pl.ds(row, count)
            into(c, (1.0 - OMEGA) * here + g_ref[c, layer, dst, :] + r_ref[c, layer, dst, :] * total(along, c))

    def post1(layer, carry):
        def into(c, value):
            f1[c, layer, mid, :] = value

        post(s1, y1, g1, r1, v1, into, layer, layer, 8, rows1, 2)
        return carry

    lax.fori_loop(1, n1 - 1, post1, 0)

    for copy in started[5:]:
        copy.wait()

    for c in range(3):
        for k in range(1, n1 - 1):
            spread_rows(tmp.at[c], f1[c, k, mid, :])
            lifted = tmp[c, pl.ds(0, bx + 16), :]
            for i in (2 * k - 3, 2 * k - 2):
                if 0 <= i < bz + 2:
                    v0[c, i, near, :] += lifted

    def post0(layer, carry):
        for row, count in chunks(16, 16 + bx, 16):

            def into(c, value):
                out_ref[c, layer - 1, pl.ds(row - 16, count), :] = value

            post(s0, y0, g0, r0, v0, into, layer, layer, row, count, 1)
        return carry

    lax.fori_loop(1, bz + 1, post0, 0)


def passed_along(x, axis, by):
    size = lax.axis_size(axis)
    return lax.ppermute(x, axis, [(i, i + by) for i in range(size) if 0 <= i + by < size])


def vmem(*shape):
    return pltpu.VMEM(shape, F32)


def local(heights, tiles, material, clamped, stiffness_table, eigenstrain):
    bz, bx, _ = material.shape
    labels = jnp.concatenate([material, clamped[:2]], 0)
    after = passed_along(labels[:, bx - HALO :].reshape(-1, LANES), "tile", 1)
    ahead = passed_along(labels[:, :HALO].reshape(-1, LANES), "tile", -1)
    rows = (bz + 2) * (bx + 2 * HALO)
    pad = jnp.zeros((-rows % 8, LANES), labels.dtype)
    brick = jnp.concatenate([labels.reshape(-1, LANES), after, ahead, pad], 0)
    bricks = lax.all_gather(brick, "height")

    bx1, bx2 = bx // 2, bx // 4
    nz, n1 = bz + 2 * HALO, bz // 2 + 8
    r0, r1 = bx + 32, bx1 + 24
    rows1 = bx1 + 8
    held = pl.BlockSpec(memory_space=pltpu.VMEM)
    scalar = pl.BlockSpec(memory_space=pltpu.SMEM)
    anywhere = pl.BlockSpec(memory_space=pl.ANY)
    kept = [
        (bz + 2, bx + 16), (2, bz, bx), (3, bz + 2, bx + 16), (3, bz, bx), (3, bz, bx),
        (n1 - 4, rows1), (2, n1 - 6, rows1), (3, n1 - 4, rows1), (3, n1 - 6, rows1), (3, n1 - 6, rows1),
    ]
    kept = [jax.ShapeDtypeStruct((*shape, LANES), F32) for shape in kept]
    field0, field1 = (nz, r0, LANES), (n1, r1, LANES)
    send, *saved = pl.pallas_call(
        functools.partial(down_kernel, heights, tiles, bz, bx),
        out_shape=[jax.ShapeDtypeStruct((heights * tiles, bz // 4 + 1, bx2, LANES), F32), *kept],
        in_specs=[held, scalar, scalar],
        out_specs=[held] + [anywhere] * len(kept),
        scratch_shapes=[
            vmem(*field0), vmem(*field0), vmem(3, *field0), vmem(3, *field0), vmem(3, *field0), vmem(3, *field0),
            vmem(3, *field0), vmem(2, *field0), vmem(3, *field0), vmem(3, r0, LANES),
            vmem(*field1), vmem(*field1), vmem(3, *field1), vmem(3, *field1), vmem(3, *field1), vmem(3, *field1),
            vmem(2, *field1), vmem(3, *field1), pltpu.SemaphoreType.DMA((10,)),
        ],
        compiler_params=pltpu.CompilerParams(vmem_limit_bytes=40 * 2**20),
    )(bricks, stiffness_table, eigenstrain)

    received = lax.all_to_all(send, ("tile", "height"), 0, 0)

    rows2 = bx2 + 2 * REACH
    rows3 = -(-(rows2 // 2) // 8) * 8
    up0, up1 = (bz + 2, r0, LANES), (n1 - 4, r1, LANES)
    up2 = (heights * bz // 4 + 2, rows2 + 16, LANES)
    up3 = (heights * bz // 8 + 2, rows3 + 16, LANES)
    return pl.pallas_call(
        functools.partial(up_kernel, heights, tiles, bz, bx),
        out_shape=jax.ShapeDtypeStruct((3, bz, bx, LANES), F32),
        in_specs=[held] + [anywhere] * len(kept),
        out_specs=held,
        scratch_shapes=[
            vmem(*up0), vmem(2, *up0), vmem(3, *up0), vmem(3, *up0), vmem(3, *up0),
            vmem(*up1), vmem(2, *up1), vmem(3, *up1), vmem(3, *up1), vmem(3, *up1), vmem(3, *up1),
            vmem(*up2), vmem(*up2), vmem(*up2), vmem(6, *up2), vmem(*up2), vmem(*up2), vmem(*up2), vmem(*up2), vmem(*up2),
            vmem(*up3), vmem(*up3), vmem(*up3), vmem(6, *up3), vmem(*up3), vmem(*up3), vmem(*up3), vmem(*up3),
            vmem(3, r0, LANES), pltpu.SemaphoreType.DMA((10,)),
        ],
        compiler_params=pltpu.CompilerParams(vmem_limit_bytes=40 * 2**20),
    )(received, *saved)


def solution(mesh):
    sides = mesh.shape["height"], mesh.shape["tile"]
    in_specs = (P("height", "tile", None), P("height", "tile", None), P(), P())
    out_specs = P(None, "height", "tile", None)
    return jax.shard_map(
        functools.partial(local, *sides), mesh=mesh, in_specs=in_specs, out_specs=out_specs, check_vma=False
    )
```

time: 376 us -> 60.6 us (0.16); the launches traced: 371 us -> 60.3 us
  starting transfers between devices: 194 us -> 6.9 us
  local copies, waits for them, and re-layouts: 61.4 us -> 1.52 us
  waiting for transfers between devices: 58.8 us -> 1.61 us
  other arithmetic: 54.1 us -> 1.03 us
  blocking collectives: 0 us -> 30 us
  Pallas kernels: 0 us -> 19.1 us
    ppermute x76 -> x2, starting transfers between devices: 194 us -> 6.9 us  [passed_along(): lax.ppermute(x, axis, [(i, i + by) for i in range(size) if 0 <= i + by <...]
    ppermute x76 -> x2, waiting for transfers between devices: 58.8 us -> 1.61 us  [passed_along(): lax.ppermute(x, axis, [(i, i + by) for i in range(size) if 0 <= i + by <...]
    reshape x9 -> x2, local copies, waits for them, and re-layouts: 52.3 us -> 0.01 us  [the longest x1 0.01 us: local(): ahead = passed_along(labels[:, :HALO].reshape(-1, LANES), 'tile', -1)]
    add x21 -> x0, other arithmetic: 26.5 us -> none  [the longest x5 10.8 us: coefficients(): low_face + high_face]
    reduce_sum x13 -> x0, other arithmetic: 20.8 us -> none  [block_sum(): return shaped.sum(axis=(2, 4, 6))]
    all_to_all x0 -> x1, blocking collectives: none -> 19.5 us  [local(): received = lax.all_to_all(send, ('tile', 'height'), 0, 0)]
    pallas_call x0 -> x2, Pallas kernels: none -> 19.1 us  [the longest x1 12.5 us: local(): pl.pallas_call(functools.partial(down_kernel, heights, tiles, bz, bx), ou...]
    all_gather x0 -> x1, blocking collectives: none -> 10.5 us  [local(): bricks = lax.all_gather(brick, 'height')]
  transfers between devices with their start and end apart: 76 -> 2, of which waited for: 16 -> 1; matrix products, arithmetic and copies ran while one was open for 11% -> 0% of each run, Pallas kernels for 0% -> 0%
where the time goes in v1:
time: 60.6 us; the launch traced here: 60.3 us
  blocking collectives  30 us (50%)
  Pallas kernels  19.1 us (32%)
  starting transfers between devices  6.9 us (11%)
  waiting for transfers between devices  1.61 us (3%)
  local copies, waits for them, and re-layouts  1.52 us (3%)
  other arithmetic  1.03 us (2%)
    all_to_all x1, blocking collectives, local(): received = lax.all_to_all(send, ('tile', 'height'), 0, 0)  19.5 us
    pallas_call x1, Pallas kernels, local(): pl.pallas_call(functools.partial(down_kernel, heights, tiles, bz, bx), ou...  12.5 us
    all_gather x1, blocking collectives, local(): bricks = lax.all_gather(brick, 'height')  10.5 us
    ppermute x2, starting transfers between devices, passed_along(): lax.ppermute(x, axis, [(i, i + by) for i in range(size) if 0 <= i + by <...  6.9 us
    pallas_call x1, Pallas kernels, local(): pl.pallas_call(functools.partial(up_kernel, heights, tiles, bz, bx), out_...  6.64 us
    ppermute x2, waiting for transfers between devices, passed_along(): lax.ppermute(x, axis, [(i, i + by) for i in range(size) if 0 <= i + by <...  1.61 us
  transfers between devices with their start and end apart: 2, of which 1 were waited for; matrix products, arithmetic and copies ran while one was open for 0% of the time, Pallas kernels for 0%

profile of v1, /device:TPU:0, one launch (start us, length us, event | category | flops | bytes accessed | tf_op | source)
XLA Modules:
  0.0 60.3 jit_solution(14167514393167906348)
XLA Ops:
  0.0 0.8 %slice.9 = s32[2,32,128]{2,1,0:T(8,128)S(1)} slice(s32[8,32,128]{2,1,0:T(8,128)} %param.5), slice={[0:2], [0:32], [0:128]} | slice | bytes 65536 | tf_op jit(solution)/shard_map/slice | solution.py:491
  0.8 0.9 %fusion = (s32[10,9,128]{2,1,0:T(8,128)S(1)}, s32[10,9,128]{2,1,0:T(8,128)S(1)}) fusion(s32[8,32,128]{2,1,0:T(8,128)} %param.4, s32[2,32,128]{2,1,0:T(8,128)S(1)} %slice.9), kind=kLoop, calls=%fused_computation.6 | loop fusion | flops 23040 | bytes 256000 | tf_op jit(solution)/shard_map/concatenate | solution.py:491
  1.6 0.0 copy-start.2
  1.7 1.4 %collective-permute-start.1 = (s32[90,128]{1,0:T(8,128)S(1)}, s32[90,128]{1,0:T(8,128)S(1)}, u32[]{:S(2)}, u32[]{:S(2)}) collective-permute-start(s32[90,128]{1,0:T(8,128)S(1)} %reshape.11), channel_id=1, source_target_pairs={{4,0},{8,4},{12,8},{16,12},{20,16},{24,20},{28,24},{5,1},{9,5},{13... | collective-permute-start | bytes 138248 | tf_op jit(solution)/shard_map/ppermute | solution.py:482
  3.1 5.5 %collective-permute-start = (s32[90,128]{1,0:T(8,128)S(1)}, s32[90,128]{1,0:T(8,128)S(1)}, u32[]{:S(2)}, u32[]{:S(2)}) collective-permute-start(s32[90,128]{1,0:T(8,128)S(1)} %reshape.10), channel_id=1, source_target_pairs={{0,4},{4,8},{8,12},{12,16},{16,20},{20,24},{24,28},{1,5},{5,9},{9,... | collective-permute-start | bytes 138248 | tf_op jit(solution)/shard_map/ppermute | solution.py:482
  8.6 0.0 copy-done.2
  8.6 0.1 pad.3.clone
  8.7 0.0 collective-permute-done.1
  8.7 1.6 %collective-permute-done = s32[90,128]{1,0:T(8,128)S(1)} collective-permute-done((s32[90,128]{1,0:T(8,128)S(1)}, s32[90,128]{1,0:T(8,128)S(1)}, u32[]{:S(2)}, u32[]{:S(2)}) %collective-permute-start) | collective-permute-done | bytes 46112 | tf_op jit(solution)/shard_map/ppermute | solution.py:482
  10.3 0.1 add_add_fusion
  10.5 0.0 copy-start
  10.5 10.5 %all-gather = s32[2016,128]{1,0:T(8,128)S(1)} all-gather(s32[504,128]{1,0:T(8,128)S(1)} %add_add_fusion), channel_id=2, replica_groups=mesh['tile'=8,'height'=4] {'height'}, dimensions={0}, use_global_device_ids=true | all-gather | bytes 1290240 | tf_op jit(solution)/shard_map/all_gather | solution.py:497
  21.0 0.0 copy-start.1
  21.0 0.0 copy-done
  21.0 0.7 %copy-done.1 = f32[3]{0:T(128)S(1)} copy-done((f32[3]{0:T(128)S(1)}, f32[3]{0:T(128)}, u32[]{:S(2)}) %copy-start.1) | copy-done | bytes 36
  21.6 12.5 %shard_map.46 = (f32[32,3,8,128]{3,2,1,0:T(8,128)S(1)}, f32[10,48,128]{2,1,0:T(8,128)S(1)}, f32[2,8,32,128]{3,2,1,0:T(8,128)S(1)}, f32[3,10,48,128]{3,2,1,0:T(8,...) custom-call(s32[4,504,128]{2,1,0:T(8,128)S(1)} %bitcast.2, ...), custom_call_target="tpu_custom_call" | custom-call | tf_op jit(solution)/shard_map/pallas_call | solution.py:512
  34.1 19.5 %all_to_all.5.recv_ref = f32[32,3,8,128]{3,2,1,0:T(8,128)S(1)} all-to-all(f32[32,3,8,128]{3,2,1,0:T(8,128)S(1)} %get-tuple-element.16), channel_id=1, replica_groups=mesh['tile'=8,'height'=4] {'tile','height'}, dimensions={0} | all-to-all | bytes 786432 | tf_op jit(solution)/shard_map/all_to_all | solution.py:526
  53.6 6.6 %shard_map.47 = f32[3,8,32,128]{3,2,1,0:T(8,128)} custom-call(f32[32,3,8,128]{3,2,1,0:T(8,128)S(1)} %all_to_all.5.recv_ref, f32[10,48,128]{2,1,0:T(8,128)S(1)} %get-tuple-element.17.s0_in, f32[2,8,32,128]{3,2,1,0:T(8,128)S(1)} %get-tuple-element.18.y0_in, f32[3,10,48,128]{3,2,1,0:T(8,128)S(1)} %get-tuple-element.19.v0_in, ...), custom_call_target="tpu_custom_call" | custom-call | tf_op jit(solution)/shard_map/pallas_call | solution.py:533
  (4 shorter events, 0.0 us)
Async XLA Ops:
  1.6 7.0 %copy-start.2 = (s32[8,32,128]{2,1,0:T(8,128)S(1)}, s32[8,32,128]{2,1,0:T(8,128)}, u32[]{:S(2)}) copy-start(s32[8,32,128]{2,1,0:T(8,128)} %param.4) | copy-start | bytes 393220
  1.7 7.0 %collective-permute-start.1 = (s32[90,128]{1,0:T(8,128)S(1)}, s32[90,128]{1,0:T(8,128)S(1)}, u32[]{:S(2)}, u32[]{:S(2)}) collective-permute-start(s32[90,128]{1,0:T(8,128)S(1)} %reshape.11), channel_id=1, source_target_pairs={{4,0},{8,4},{12,8},{16,12},{20,16},{24,20},{28,24},{5,1},{9,5},{13... | collective-permute-start | bytes 138248 | tf_op jit(solution)/shard_map/ppermute | solution.py:482
  3.1 7.2 %collective-permute-start = (s32[90,128]{1,0:T(8,128)S(1)}, s32[90,128]{1,0:T(8,128)S(1)}, u32[]{:S(2)}, u32[]{:S(2)}) collective-permute-start(s32[90,128]{1,0:T(8,128)S(1)} %reshape.10), channel_id=1, source_target_pairs={{0,4},{4,8},{8,12},{12,16},{16,20},{20,24},{24,28},{1,5},{5,9},{9,... | collective-permute-start | bytes 138248 | tf_op jit(solution)/shard_map/ppermute | solution.py:482
  10.5 10.5 %copy-start = (f32[3,3]{1,0:T(4,128)S(1)}, f32[3,3]{1,0:T(4,128)}, u32[]{:S(2)}) copy-start(f32[3,3]{1,0:T(4,128)} %strain_ref.1) | copy-start | bytes 112
  21.0 0.7 %copy-start.1 = (f32[3]{0:T(128)S(1)}, f32[3]{0:T(128)}, u32[]{:S(2)}) copy-start(f32[3]{0:T(128)} %table_ref.1) | copy-start | bytes 40

commit v2 on v1

--- a/solution.py
+++ b/solution.py
@@ -13,7 +13,24 @@
 LANES = 128
 HALO = 9
 REACH = 16
+SPARE = 4
 F32 = jnp.float32
+
+
+def each(start, stop, body, step):
+    groups = (stop - start) // step
+
+    def group(i, carry):
+        for k in range(step):
+            body(start + i * step + k, 0)
+        return carry
+
+    if groups > 1:
+        lax.fori_loop(0, groups, group, 0)
+    elif groups == 1:
+        group(0, 0)
+    for layer in range(start + groups * step, stop):
+        body(layer, 0)
 
 
 def chunks(start, stop, size):
@@ -127,9 +144,36 @@
     return result
 
 
+def pack_kernel(
+    bz, bx, material_ref, clamped_ref, table_ref, strain_ref, own_ref, after_ref, ahead_ref, label, joined, table, strain, sem
+):
+    copies = [
+        pltpu.make_async_copy(material_ref, label, sem.at[0]),
+        pltpu.make_async_copy(clamped_ref.at[pl.ds(0, 2)], joined, sem.at[1]),
+        pltpu.make_async_copy(table_ref, table, sem.at[2]),
+        pltpu.make_async_copy(strain_ref, strain, sem.at[3]),
+    ]
+    for copy in copies:
+        copy.start()
+    for copy in copies:
+        copy.wait()
+    for slot in range(bz + 2):
+        src = label.at[slot] if slot < bz else joined.at[slot - bz]
+        own_ref[pl.ds(slot * bx, bx), :] = src[...].astype(F32)
+        after_ref[pl.ds(slot * HALO, HALO), :] = src[pl.ds(bx - HALO, HALO), :].astype(F32)
+        ahead_ref[pl.ds(slot * HALO, HALO), :] = src[pl.ds(0, HALO), :].astype(F32)
+    lane = lane_of(SPARE)
+    row = jnp.zeros((SPARE, LANES), F32)
+    for k in range(3):
+        row = jnp.where(lane == k, table[k], row)
+        for c in range(3):
+            row = jnp.where(lane == 3 + 3 * c + k, table[k] * strain[k, c], row)
+    own_ref[pl.ds((bz + 2) * bx, SPARE), :] = row
+
+
 def down_kernel(
     heights, tiles, bz, bx,
-    x_ref, table_ref, strain_ref,
+    x_ref,
     send_ref, s0_out, y0_out, v0_out, g0_out, r0_out, s1_out, y1_out, v1_out, g1_out, r1_out,
     s, p, st, b, r, d, g, y, v, tmp, s1, p1, b1, r1, d1, g1, y1, v1, sem,
 ):
@@ -137,7 +181,10 @@
     nz, n1 = bz + 2 * HALO, bz // 2 + 8
     bx1, bx2 = bx // 2, bx // 4
     low, high = 8, bx + 24
-    own_rows, halo_rows = (bz + 2) * bx, (bz + 2) * HALO
+    own_rows, halo_rows = (bz + 2) * bx + SPARE, (bz + 2) * HALO
+    spare = x_ref[0, pl.ds(own_rows - SPARE, 1), :]
+    table = [jnp.broadcast_to(spare[:, k : k + 1], (1, LANES)) for k in range(12)]
+    strain = [table[3 + 3 * c : 6 + 3 * c] for c in range(3)]
     before = jnp.where(t > 0, 1.0, 0.0)
     behind = jnp.where(t < tiles - 1, 1.0, 0.0)
 
@@ -155,19 +202,19 @@
         ]
         for at, clamp_at, count, to, valid in parts:
             label = x_ref[brick, pl.ds(at, count), :]
-            is0, is1 = label == 0, label == 1
+            is0, is1 = label == 0.0, label == 1.0
             weight = inside * valid
-            stiff = [table_ref[k] * weight for k in range(3)]
+            stiff = [table[k] * weight for k in range(3)]
             dst = pl.ds(to, count)
             s[layer, dst, :] = jnp.where(is0, stiff[0], jnp.where(is1, stiff[1], stiff[2]))
             for c in range(3):
-                e = [stiff[k] * strain_ref[k, c] for k in range(3)]
+                e = [strain[c][k] * weight for k in range(3)]
                 st[c, layer, dst, :] = jnp.where(is0, e[0], jnp.where(is1, e[1], e[2]))
-            joined = x_ref[0, pl.ds(clamp_at, count), :].astype(F32)
+            joined = x_ref[0, pl.ds(clamp_at, count), :]
             p[layer, dst, :] = joined * (bottom * valid)
         return carry
 
-    lax.fori_loop(0, nz, read_layer, 0)
+    each(0, nz, read_layer, 8)
 
     def setup0(layer, carry):
         for row, count in chunks(low, high, 16):
@@ -183,14 +230,14 @@
             level_setup(s, p, r, d, g, y, lambda c: source[c], layer, row, count, 1)
         return carry
 
-    lax.fori_loop(1, nz - 1, setup0, 0)
+    each(1, nz - 1, setup0, 8)
 
     def sweep0(layer, carry):
         for row, count in chunks(low, high, 16):
             first_sweep(s, y, r, g, v, layer, row, count, 1)
         return carry
 
-    lax.fori_loop(2, nz - 2, sweep0, 0)
+    each(2, nz - 2, sweep0, 8)
 
     own = (pl.ds(HALO, bz), pl.ds(16, bx))
     near = (pl.ds(HALO - 1, bz + 2), pl.ds(low, bx + 16))
@@ -219,7 +266,7 @@
             b1[c, j + 1, pl.ds(8, rows1), :] = pair_lanes(pair_rows(tmp.at[c], low, rows1), 1)
         return carry
 
-    lax.fori_loop(0, n1 - 2, restrict0, 0)
+    each(0, n1 - 2, restrict0, 8)
 
     def coarse0(k, carry):
         for field, scale, into in ((s, 0.5, s1), (p, 1.0, p1)):
@@ -227,7 +274,7 @@
             into[k, pl.ds(8, rows1), :] = scale * pair_lanes(both[0] + both[1], 1)
         return carry
 
-    lax.fori_loop(0, n1, coarse0, 0)
+    each(0, n1, coarse0, 8)
 
     def setup1(layer, carry):
         level_setup(
@@ -236,13 +283,13 @@
         )
         return carry
 
-    lax.fori_loop(1, n1 - 1, setup1, 0)
+    each(1, n1 - 1, setup1, 8)
 
     def sweep1(layer, carry):
         first_sweep(s1, y1, r1, g1, v1, layer, 8, rows1, 2)
         return carry
 
-    lax.fori_loop(2, n1 - 2, sweep1, 0)
+    each(2, n1 - 2, sweep1, 8)
 
     copies = [
         (s1.at[pl.ds(2, n1 - 4), pl.ds(8, rows1)], s1_out),
@@ -271,14 +318,19 @@
             jnp.where(lane == 0, fields[0], jnp.where(lane == 1, fields[1], jnp.where(lane == 2, fields[2], stiff)))
         )
     both = [pair_rows(p1.at[4 + i], 12, bx2) for i in range(2)]
-    packed.append(pair_lanes(both[0] + both[1], 2))
+    tmp[0, pl.ds(0, bx2), :] = pair_lanes(both[0] + both[1], 2)
+    quarter = bx2 // 4
+    part = [tmp[0, pl.ds(j, quarter, stride=4), :] for j in range(4)]
+    lane = lane_of(quarter) & 3
+    packed.append(jnp.where(lane == 0, part[0], jnp.where(lane == 1, part[1], jnp.where(lane == 2, part[2], part[3]))))
 
     def fill(i, carry):
         for m, value in enumerate(packed):
-            send_ref[i, m, :, :] = value
-        return carry
-
-    lax.fori_loop(0, heights * tiles, fill, 0)
+            for k in range(value.shape[0] // 2):
+                send_ref[i, m * bx2 // 2 + k, :, :] = value[2 * k : 2 * k + 2]
+        return carry
+
+    each(0, heights * tiles, fill, 8)
     for copy in started:
         copy.wait()
 
@@ -321,13 +373,20 @@
         dst = pl.ds(8 + (dt + side) * bx2, bx2)
         for hh in range(heights):
             for m in range(bz2):
-                x = recv_ref[other * heights + hh, m] * scale
+                x = recv_ref[other * heights + hh, pl.ds(m * bx2 // 2, bx2 // 2)].reshape(bx2, LANES) * scale
                 layer = 1 + hh * bz2 + m
                 b2[layer, dst, :] = jnp.where(lane == 3, 0.0, x)
                 s2[layer, dst, :] = jnp.where(
                     lane == 3, x, jnp.where(lane == 2, roll(x, -1), jnp.where(lane == 1, roll(x, -2), roll(x, -3)))
                 )
-        p2[1, dst, :] = recv_ref[other * heights, bz2] * scale
+        quarter = bx2 // 4
+        x = recv_ref[other * heights, pl.ds(bz2 * bx2 // 2, quarter // 2)].reshape(quarter, LANES) * scale
+        moved = {shift: roll(x, shift) if shift else x for shift in range(-3, 4)}
+        small = lane_of(quarter) & 3
+        for j in range(4):
+            p2[1, pl.ds(8 + (dt + side) * bx2 + j, quarter, stride=4), :] = jnp.where(
+                small == 0, moved[-j], jnp.where(small == 1, moved[1 - j], jnp.where(small == 2, moved[2 - j], moved[3 - j]))
+            )
 
     def weights(count):
         kind = lane_of(count) & 3
@@ -362,14 +421,14 @@
         setup(s2, p2, b2, q2, r2, d2, g2, layer, 8, rows2, 4)
         return carry
 
-    lax.fori_loop(1, n2 + 1, setup2, 0)
+    each(1, n2 + 1, setup2, 8)
 
     def sweep2(layer, carry):
         here, total_ = packed_sum(g2, q2, layer, 8, rows2, 4)
         v2[layer, pl.ds(8, rows2), :] = (2.0 - OMEGA) * here + rows_at(r2, layer, 8, rows2) * total_
         return carry
 
-    lax.fori_loop(1, n2 + 1, sweep2, 0)
+    each(1, n2 + 1, sweep2, 8)
 
     rows3 = -(-(rows2 // 2) // 8) * 8
 
@@ -387,7 +446,7 @@
             into[j + 1, dst, :] = scale * pair_lanes(both[0] + both[1], 4)
         return carry
 
-    lax.fori_loop(0, n3, restrict2, 0)
+    each(0, n3, restrict2, 8)
 
     for layer in range(1, n3 + 1):
         setup(s3, p3, b3, q3, r3, None, g3, layer, 8, rows3, 8)
@@ -408,7 +467,7 @@
         v2[layer, pl.ds(16, wide2), :] += tmp[0, pl.ds(0, wide2), :]
         return carry
 
-    lax.fori_loop(1, n2 + 1, lift2, 0)
+    each(1, n2 + 1, lift2, 8)
 
     def post2(layer, carry):
         here, total_ = packed_sum(v2, q2, layer, 16, wide2, 4)
@@ -417,7 +476,7 @@
         )
         return carry
 
-    lax.fori_loop(1, n2 + 1, post2, 0)
+    each(1, n2 + 1, post2, 8)
 
     for copy in started[:5]:
         copy.wait()
@@ -436,7 +495,7 @@
                 v1[c, 2 * m + i, mid, :] += lifted
         return carry
 
-    lax.fori_loop(0, n1 // 2, lift1, 0)
+    each(0, n1 // 2, lift1, 8)
 
     def post(s_ref, y_ref, g_ref, r_ref, v_ref, into, layer, to, row, count, step):
         faces = all_faces(s_ref, y_ref, layer, row, count)
@@ -452,7 +511,7 @@
         post(s1, y1, g1, r1, v1, into, layer, layer, 8, rows1, 2)
         return carry
 
-    lax.fori_loop(1, n1 - 1, post1, 0)
+    each(1, n1 - 1, post1, 8)
 
     for copy in started[5:]:
         copy.wait()
@@ -474,7 +533,7 @@
             post(s0, y0, g0, r0, v0, into, layer, layer, row, count, 1)
         return carry
 
-    lax.fori_loop(1, bz + 1, post0, 0)
+    each(1, bz + 1, post0, 8)
 
 
 def passed_along(x, axis, by):
@@ -488,21 +547,31 @@
 
 def local(heights, tiles, material, clamped, stiffness_table, eigenstrain):
     bz, bx, _ = material.shape
-    labels = jnp.concatenate([material, clamped[:2]], 0)
-    after = passed_along(labels[:, bx - HALO :].reshape(-1, LANES), "tile", 1)
-    ahead = passed_along(labels[:, :HALO].reshape(-1, LANES), "tile", -1)
-    rows = (bz + 2) * (bx + 2 * HALO)
-    pad = jnp.zeros((-rows % 8, LANES), labels.dtype)
-    brick = jnp.concatenate([labels.reshape(-1, LANES), after, ahead, pad], 0)
-    bricks = lax.all_gather(brick, "height")
+
+    held = pl.BlockSpec(memory_space=pltpu.VMEM)
+    anywhere = pl.BlockSpec(memory_space=pl.ANY)
+    outside = pl.BlockSpec(memory_space=pltpu.HBM)
+    slots = bz + 2
+    own, after, ahead = pl.pallas_call(
+        functools.partial(pack_kernel, bz, bx),
+        out_shape=[
+            pltpu.VMEM((rows, LANES), F32)
+            for rows in (slots * bx + SPARE, slots * HALO, slots * HALO)
+        ],
+        in_specs=[outside] * 4,
+        out_specs=[held] * 3,
+        scratch_shapes=[
+            pltpu.VMEM((bz, bx, LANES), jnp.int32), pltpu.VMEM((2, bx, LANES), jnp.int32),
+            pltpu.SMEM((3,), F32), pltpu.SMEM((3, 3), F32), pltpu.SemaphoreType.DMA((4,)),
+        ],
+    )(material, clamped, stiffness_table, eigenstrain)
+    after, ahead = passed_along(after, "tile", 1), passed_along(ahead, "tile", -1)
+    bricks = lax.all_gather(jnp.concatenate([own, after, ahead], 0), "height")
 
     bx1, bx2 = bx // 2, bx // 4
     nz, n1 = bz + 2 * HALO, bz // 2 + 8
     r0, r1 = bx + 32, bx1 + 24
     rows1 = bx1 + 8
-    held = pl.BlockSpec(memory_space=pltpu.VMEM)
-    scalar = pl.BlockSpec(memory_space=pltpu.SMEM)
-    anywhere = pl.BlockSpec(memory_space=pl.ANY)
     kept = [
         (bz + 2, bx + 16), (2, bz, bx), (3, bz + 2, bx + 16), (3, bz, bx), (3, bz, bx),
         (n1 - 4, rows1), (2, n1 - 6, rows1), (3, n1 - 4, rows1), (3, n1 - 6, rows1), (3, n1 - 6, rows1),
@@ -511,8 +580,8 @@
     field0, field1 = (nz, r0, LANES), (n1, r1, LANES)
     send, *saved = pl.pallas_call(
         functools.partial(down_kernel, heights, tiles, bz, bx),
-        out_shape=[jax.ShapeDtypeStruct((heights * tiles, bz // 4 + 1, bx2, LANES), F32), *kept],
-        in_specs=[held, scalar, scalar],
+        out_shape=[jax.ShapeDtypeStruct((heights * tiles, (bz // 4 * bx2 + bx2 // 4) // 2, 2, LANES), F32), *kept],
+        in_specs=[held],
         out_specs=[held] + [anywhere] * len(kept),
         scratch_shapes=[
             vmem(*field0), vmem(*field0), vmem(3, *field0), vmem(3, *field0), vmem(3, *field0), vmem(3, *field0),
@@ -521,7 +590,7 @@
             vmem(2, *field1), vmem(3, *field1), pltpu.SemaphoreType.DMA((10,)),
         ],
         compiler_params=pltpu.CompilerParams(vmem_limit_bytes=40 * 2**20),
-    )(bricks, stiffness_table, eigenstrain)
+    )(bricks)
 
     received = lax.all_to_all(send, ("tile", "height"), 0, 0)
 

time: 60.6 us -> 46.6 us (0.77)
  Pallas kernels: 19.1 us -> 9.54 us
  blocking collectives: 30 us -> 26 us
  waiting for transfers between devices: 1.61 us -> 4.68 us
  local copies, waits for them, and re-layouts: 1.52 us -> 0 us
  other arithmetic: 1.03 us -> 0.02 us
  starting transfers between devices: 6.9 us -> 6.14 us
    pallas_call x1, Pallas kernels: 12.5 us -> 5.65 us  [local(): pl.pallas_call(functools.partial(down_kernel, heights, tiles, bz, bx), ou...]
    pallas_call x1, Pallas kernels: 6.64 us -> 2.9 us  [local(): pl.pallas_call(functools.partial(up_kernel, heights, tiles, bz, bx), out_...]
    all_to_all x1, blocking collectives: 19.5 us -> 16 us  [local(): received = lax.all_to_all(send, ('tile', 'height'), 0, 0)]
    ppermute x2, waiting for transfers between devices: 1.61 us -> 4.68 us  [passed_along(): lax.ppermute(x, axis, [(i, i + by) for i in range(size) if 0 <= i + by <...]
    concatenate x3 -> x1, other arithmetic: 1.03 us -> 0.02 us  [local(): bricks = lax.all_gather(jnp.concatenate([own, after, ahead], 0), 'height')]
    pallas_call x0 -> x1, Pallas kernels: none -> 0.98 us  [local(): pl.pallas_call(functools.partial(pack_kernel, bz, bx), out_shape=[pltpu.V...]
    slice x1 -> x0, local copies, waits for them, and re-layouts: 0.76 us -> none  [local(): labels = jnp.concatenate([material, clamped[:2]], 0)]
    ppermute x2, starting transfers between devices: 6.9 us -> 6.14 us  [passed_along(): lax.ppermute(x, axis, [(i, i + by) for i in range(size) if 0 <= i + by <...]
  transfers between devices with their start and end apart: 2 -> 2, of which waited for: 1 -> 2; matrix products, arithmetic and copies ran while one was open for 0% -> 0% of each run, Pallas kernels for 0% -> 0%
where the time goes in v2:
time: 46.6 us; the launch traced here: 46.4 us
  blocking collectives  26 us (56%)
  Pallas kernels  9.54 us (20%)
  starting transfers between devices  6.14 us (13%)
  waiting for transfers between devices  4.68 us (10%)
    all_to_all x1, blocking collectives, local(): received = lax.all_to_all(send, ('tile', 'height'), 0, 0)  16 us
    all_gather x1, blocking collectives, local(): bricks = lax.all_gather(jnp.concatenate([own, after, ahead], 0), 'height')  9.96 us
    ppermute x2, starting transfers between devices, passed_along(): lax.ppermute(x, axis, [(i, i + by) for i in range(size) if 0 <= i + by <...  6.14 us
    pallas_call x1, Pallas kernels, local(): pl.pallas_call(functools.partial(down_kernel, heights, tiles, bz, bx), ou...  5.65 us
    ppermute x2, waiting for transfers between devices, passed_along(): lax.ppermute(x, axis, [(i, i + by) for i in range(size) if 0 <= i + by <...  4.68 us
    pallas_call x1, Pallas kernels, local(): pl.pallas_call(functools.partial(up_kernel, heights, tiles, bz, bx), out_...  2.9 us
    pallas_call x1, Pallas kernels, local(): pl.pallas_call(functools.partial(pack_kernel, bz, bx), out_shape=[pltpu.V...  0.98 us
  transfers between devices with their start and end apart: 2, of which 2 were waited for; matrix products, arithmetic and copies ran while one was open for 0% of the time, Pallas kernels for 0%

profile of v2, /device:TPU:0, one launch (start us, length us, event | category | flops | bytes accessed | tf_op | source)
XLA Modules:
  0.0 46.4 jit_solution(17217425218923816422)
XLA Ops:
  0.0 1.0 %shard_map.46 = (f32[324,128]{1,0:T(8,128)S(1)}, f32[90,128]{1,0:T(8,128)S(1)}, f32[90,128]{1,0:T(8,128)S(1)}) custom-call(s32[8,32,128]{2,1,0:T(8,128)} %material_ref.1, s32[8,32,128]{2,1,0:T(8,128)} %clamped_ref.1, f32[3]{0:T(128)} %table_ref.1, f32[3,3]{1,0:T(4,128)} %strain_ref.1), custom_call_target="tpu_custom_call" | custom-call | tf_op jit(solution)/shard_map/pallas_call | solution.py:555
  1.0 4.8 %collective-permute-start = (f32[90,128]{1,0:T(8,128)S(1)}, f32[90,128]{1,0:T(8,128)S(1)}, u32[]{:S(2)}, u32[]{:S(2)}) collective-permute-start(f32[90,128]{1,0:T(8,128)S(1)} %get-tuple-element.20), channel_id=1, source_target_pairs={{0,4},{4,8},{8,12},{12,16},{16,20},{20,24},{24,28},{1,5},{5,9},{9,... | collective-permute-start | bytes 138248 | tf_op jit(solution)/shard_map/ppermute | solution.py:541
  5.8 1.3 %collective-permute-start.1 = (f32[90,128]{1,0:T(8,128)S(1)}, f32[90,128]{1,0:T(8,128)S(1)}, u32[]{:S(2)}, u32[]{:S(2)}) collective-permute-start(f32[90,128]{1,0:T(8,128)S(1)} %get-tuple-element.21), channel_id=1, source_target_pairs={{4,0},{8,4},{12,8},{16,12},{20,16},{24,20},{28,24},{5,1},{9,5},{13... | collective-permute-start | bytes 138248 | tf_op jit(solution)/shard_map/ppermute | solution.py:541
  7.1 0.4 collective-permute-done
  7.6 4.3 %collective-permute-done.1 = f32[90,128]{1,0:T(8,128)S(1)} collective-permute-done((f32[90,128]{1,0:T(8,128)S(1)}, f32[90,128]{1,0:T(8,128)S(1)}, u32[]{:S(2)}, u32[]{:S(2)}) %collective-permute-start.1) | collective-permute-done | bytes 46112 | tf_op jit(solution)/shard_map/ppermute | solution.py:541
  11.8 10.0 %all-gather = f32[2016,128]{1,0:T(8,128)S(1)} all-gather(f32[504,128]{1,0:T(8,128)S(1)} %pad_maximum_fusion), channel_id=2, replica_groups=mesh['tile'=8,'height'=4] {'height'}, dimensions={0}, use_global_device_ids=true | all-gather | bytes 1290240 | tf_op jit(solution)/shard_map/all_gather | solution.py:569
  21.8 5.7 %shard_map.47 = (f32[32,9,2,128]{3,2,1,0:T(2,128)S(1)}, f32[10,48,128]{2,1,0:T(8,128)S(1)}, f32[2,8,32,128]{3,2,1,0:T(8,128)S(1)}, f32[3,10,48,128]{3,2,1,0:T(8,...) custom-call(f32[4,504,128]{2,1,0:T(8,128)S(1)} %bitcast.1), custom_call_target="tpu_custom_call" | custom-call | tf_op jit(solution)/shard_map/pallas_call | solution.py:581
  27.5 16.0 %all_to_all.5.recv_ref = f32[32,9,2,128]{3,2,1,0:T(2,128)S(1)} all-to-all(f32[32,9,2,128]{3,2,1,0:T(2,128)S(1)} %get-tuple-element.22), channel_id=1, replica_groups=mesh['tile'=8,'height'=4] {'tile','height'}, dimensions={0} | all-to-all | bytes 589824 | tf_op jit(solution)/shard_map/all_to_all | solution.py:595
  43.5 2.9 %shard_map.48 = f32[3,8,32,128]{3,2,1,0:T(8,128)} custom-call(f32[32,9,2,128]{3,2,1,0:T(2,128)S(1)} %all_to_all.5.recv_ref, f32[10,48,128]{2,1,0:T(8,128)S(1)} %get-tuple-element.23.s0_in, f32[2,8,32,128]{3,2,1,0:T(8,128)S(1)} %get-tuple-element.24.y0_in, f32[3,10,48,128]{3,2,1,0:T(8,128)S(1)} %get-tuple-element.25.v0_in, ...), custom_call_target="tpu_custom_call" | custom-call | tf_op jit(solution)/shard_map/pallas_call | solution.py:602
  (1 shorter events, 0.0 us)
Async XLA Ops:
  1.0 6.6 %collective-permute-start = (f32[90,128]{1,0:T(8,128)S(1)}, f32[90,128]{1,0:T(8,128)S(1)}, u32[]{:S(2)}, u32[]{:S(2)}) collective-permute-start(f32[90,128]{1,0:T(8,128)S(1)} %get-tuple-element.20), channel_id=1, source_target_pairs={{0,4},{4,8},{8,12},{12,16},{16,20},{20,24},{24,28},{1,5},{5,9},{9,... | collective-permute-start | bytes 138248 | tf_op jit(solution)/shard_map/ppermute | solution.py:541
  5.8 6.0 %collective-permute-start.1 = (f32[90,128]{1,0:T(8,128)S(1)}, f32[90,128]{1,0:T(8,128)S(1)}, u32[]{:S(2)}, u32[]{:S(2)}) collective-permute-start(f32[90,128]{1,0:T(8,128)S(1)} %get-tuple-element.21), channel_id=1, source_target_pairs={{4,0},{8,4},{12,8},{16,12},{20,16},{24,20},{28,24},{5,1},{9,5},{13... | collective-permute-start | bytes 138248 | tf_op jit(solution)/shard_map/ppermute | solution.py:541

commit v3 on v2

--- a/solution.py
+++ b/solution.py
@@ -145,7 +145,7 @@
 
 
 def pack_kernel(
-    bz, bx, material_ref, clamped_ref, table_ref, strain_ref, own_ref, after_ref, ahead_ref, label, joined, table, strain, sem
+    bz, bx, material_ref, clamped_ref, table_ref, strain_ref, own_ref, near_ref, far_ref, label, joined, table, strain, sem
 ):
     copies = [
         pltpu.make_async_copy(material_ref, label, sem.at[0]),
@@ -157,11 +157,14 @@
         copy.start()
     for copy in copies:
         copy.wait()
+    odd = (lax.axis_index("tile") & 1) == 1
     for slot in range(bz + 2):
         src = label.at[slot] if slot < bz else joined.at[slot - bz]
         own_ref[pl.ds(slot * bx, bx), :] = src[...].astype(F32)
-        after_ref[pl.ds(slot * HALO, HALO), :] = src[pl.ds(bx - HALO, HALO), :].astype(F32)
-        ahead_ref[pl.ds(slot * HALO, HALO), :] = src[pl.ds(0, HALO), :].astype(F32)
+        first = src[pl.ds(0, HALO), :].astype(F32)
+        last = src[pl.ds(bx - HALO, HALO), :].astype(F32)
+        near_ref[pl.ds(slot * HALO, HALO), :] = jnp.where(odd, first, last)
+        far_ref[pl.ds(slot * HALO, HALO), :] = jnp.where(odd, last, first)
     lane = lane_of(SPARE)
     row = jnp.zeros((SPARE, LANES), F32)
     for k in range(3):
@@ -182,6 +185,8 @@
     bx1, bx2 = bx // 2, bx // 4
     low, high = 8, bx + 24
     own_rows, halo_rows = (bz + 2) * bx + SPARE, (bz + 2) * HALO
+    low_rows = own_rows + jnp.where((t & 1) == 1, 0, halo_rows)
+    high_rows = own_rows + jnp.where((t & 1) == 1, halo_rows, 0)
     spare = x_ref[0, pl.ds(own_rows - SPARE, 1), :]
     table = [jnp.broadcast_to(spare[:, k : k + 1], (1, LANES)) for k in range(12)]
     strain = [table[3 + 3 * c : 6 + 3 * c] for c in range(3)]
@@ -197,8 +202,8 @@
         clamp_slot = bz + jnp.clip(z, 0, 1)
         parts = [
             (slot * bx, clamp_slot * bx, bx, 16, 1.0),
-            (own_rows + slot * HALO, own_rows + clamp_slot * HALO, HALO, 16 - HALO, before),
-            (own_rows + halo_rows + slot * HALO, own_rows + halo_rows + clamp_slot * HALO, HALO, 16 + bx, behind),
+            (low_rows + slot * HALO, low_rows + clamp_slot * HALO, HALO, 16 - HALO, before),
+            (high_rows + slot * HALO, high_rows + clamp_slot * HALO, HALO, 16 + bx, behind),
         ]
         for at, clamp_at, count, to, valid in parts:
             label = x_ref[brick, pl.ds(at, count), :]
@@ -261,9 +266,9 @@
             one = remainder(s, y, b, d, v, layer, row, count, 1)
             two = remainder(s, y, b, d, v, layer + 1, row, count, 1)
             for c in range(3):
-                tmp[c, pl.ds(row, count), :] = one[c] + two[c]
+                tmp[j, c, pl.ds(row, count), :] = one[c] + two[c]
         for c in range(3):
-            b1[c, j + 1, pl.ds(8, rows1), :] = pair_lanes(pair_rows(tmp.at[c], low, rows1), 1)
+            b1[c, j + 1, pl.ds(8, rows1), :] = pair_lanes(pair_rows(tmp.at[j, c], low, rows1), 1)
         return carry
 
     each(0, n1 - 2, restrict0, 8)
@@ -310,17 +315,17 @@
         two = remainder(s1, y1, b1, d1, v1, layer + 1, 8, rows1, 2)
         fields = []
         for c in range(3):
-            tmp[c, pl.ds(0, rows1), :] = one[c] + two[c]
-            fields.append(pair_lanes(pair_rows(tmp.at[c], 4, bx2), 2))
+            tmp[m, c, pl.ds(0, rows1), :] = one[c] + two[c]
+            fields.append(pair_lanes(pair_rows(tmp.at[m, c], 4, bx2), 2))
         both = [pair_rows(s1.at[layer + i], 12, bx2) for i in range(2)]
         stiff = 0.5 * pair_lanes(both[0] + both[1], 2)
         packed.append(
             jnp.where(lane == 0, fields[0], jnp.where(lane == 1, fields[1], jnp.where(lane == 2, fields[2], stiff)))
         )
     both = [pair_rows(p1.at[4 + i], 12, bx2) for i in range(2)]
-    tmp[0, pl.ds(0, bx2), :] = pair_lanes(both[0] + both[1], 2)
+    tmp[2, 0, pl.ds(0, bx2), :] = pair_lanes(both[0] + both[1], 2)
     quarter = bx2 // 4
-    part = [tmp[0, pl.ds(j, quarter, stride=4), :] for j in range(4)]
+    part = [tmp[2, 0, pl.ds(j, quarter, stride=4), :] for j in range(4)]
     lane = lane_of(quarter) & 3
     packed.append(jnp.where(lane == 0, part[0], jnp.where(lane == 1, part[1], jnp.where(lane == 2, part[2], part[3]))))
 
@@ -339,7 +344,7 @@
     heights, tiles, bz, bx,
     recv_ref, s0_in, y0_in, v0_in, g0_in, r0_in, s1_in, y1_in, v1_in, g1_in, r1_in,
     out_ref,
-    s0, y0, v0, g0, r0, s1, y1, v1, g1, r1, f1, s2, p2, b2, q2, r2, d2, g2, v2, f2, s3, p3, b3, q3, r3, g3, va, vb, tmp, sem,
+    s0, y0, v0, g0, r0, s1, y1, v1, g1, r1, f1, s2, p2, b2, q2, r2, d2, g2, v2, f2, s3, p3, b3, q3, r3, g3, va, vb, rest2, tmp, sem,
 ):
     h, t = lax.axis_index("height"), lax.axis_index("tile")
     bx1, bx2, bz2 = bx // 2, bx // 4, bz // 4
@@ -361,7 +366,7 @@
 
     for ref in (s2, p2, g2, v2, f2, s3, p3, g3, va, vb):
         ref[...] = jnp.zeros(ref.shape, F32)
-    tmp[...] = jnp.zeros(tmp.shape, F32)
+    rest2[...] = jnp.zeros(rest2.shape, F32)
 
     side = REACH // bx2
     lane = lane_of(bx2) & 3
@@ -438,9 +443,9 @@
             layer = 1 + 2 * j + i
             here, total_ = packed_sum(v2, q2, layer, 8, rows2, 4)
             rest = rest + rows_at(b2, layer, 8, rows2) + 0.5 * (total_ - rows_at(d2, layer, 8, rows2) * here)
-        tmp[0, pl.ds(8, rows2), :] = rest
+        rest2[j, pl.ds(8, rows2), :] = rest
         dst = pl.ds(8, rows3)
-        b3[j + 1, dst, :] = pair_lanes(pair_rows(tmp.at[0], 8, rows3), 4)
+        b3[j + 1, dst, :] = pair_lanes(pair_rows(rest2.at[j], 8, rows3), 4)
         for field, scale, into in ((s2, 0.5, s3), (p2, 1.0, p3)):
             both = [pair_rows(field.at[1 + 2 * j + i], 8, rows3) for i in range(2)]
             into[j + 1, dst, :] = scale * pair_lanes(both[0] + both[1], 4)
@@ -463,8 +468,8 @@
     wide2 = bx2 + 16
 
     def lift2(layer, carry):
-        spread_rows(tmp.at[0], coarse[(layer + 1) // 2, pl.ds(12, wide2 // 2), :])
-        v2[layer, pl.ds(16, wide2), :] += tmp[0, pl.ds(0, wide2), :]
+        spread_rows(tmp.at[layer - 1], coarse[(layer + 1) // 2, pl.ds(12, wide2 // 2), :])
+        v2[layer, pl.ds(16, wide2), :] += tmp[layer - 1, pl.ds(0, wide2), :]
         return carry
 
     each(1, n2 + 1, lift2, 8)
@@ -489,8 +494,8 @@
             part = jnp.where(
                 kind == 0, moved[-c], jnp.where(kind == 1, moved[1 - c], jnp.where(kind == 2, moved[2 - c], moved[3 - c]))
             )
-            spread_rows(tmp.at[c], part)
-            lifted = tmp[c, pl.ds(0, rows1), :]
+            spread_rows(tmp.at[3 * m + c], part)
+            lifted = tmp[3 * m + c, pl.ds(0, rows1), :]
             for i in range(2):
                 v1[c, 2 * m + i, mid, :] += lifted
         return carry
@@ -518,8 +523,9 @@
 
     for c in range(3):
         for k in range(1, n1 - 1):
-            spread_rows(tmp.at[c], f1[c, k, mid, :])
-            lifted = tmp[c, pl.ds(0, bx + 16), :]
+            slot = 3 * (k - 1) + c
+            spread_rows(tmp.at[slot], f1[c, k, mid, :])
+            lifted = tmp[slot, pl.ds(0, bx + 16), :]
             for i in (2 * k - 3, 2 * k - 2):
                 if 0 <= i < bz + 2:
                     v0[c, i, near, :] += lifted
@@ -536,9 +542,9 @@
     each(1, bz + 1, post0, 8)
 
 
-def passed_along(x, axis, by):
-    size = lax.axis_size(axis)
-    return lax.ppermute(x, axis, [(i, i + by) for i in range(size) if 0 <= i + by < size])
+def swapped(x, axis, start):
+    pairs = [(i, i + 1) for i in range(start, lax.axis_size(axis) - 1, 2)]
+    return lax.ppermute(x, axis, pairs + [(j, i) for i, j in pairs])
 
 
 def vmem(*shape):
@@ -552,7 +558,7 @@
     anywhere = pl.BlockSpec(memory_space=pl.ANY)
     outside = pl.BlockSpec(memory_space=pltpu.HBM)
     slots = bz + 2
-    own, after, ahead = pl.pallas_call(
+    own, near, far = pl.pallas_call(
         functools.partial(pack_kernel, bz, bx),
         out_shape=[
             pltpu.VMEM((rows, LANES), F32)
@@ -565,8 +571,9 @@
             pltpu.SMEM((3,), F32), pltpu.SMEM((3, 3), F32), pltpu.SemaphoreType.DMA((4,)),
         ],
     )(material, clamped, stiffness_table, eigenstrain)
-    after, ahead = passed_along(after, "tile", 1), passed_along(ahead, "tile", -1)
-    bricks = lax.all_gather(jnp.concatenate([own, after, ahead], 0), "height")
+    far = swapped(far, "tile", 1)
+    near = swapped(near, "tile", 0)
+    bricks = lax.all_gather(jnp.concatenate([own, near, far], 0), "height")
 
     bx1, bx2 = bx // 2, bx // 4
     nz, n1 = bz + 2 * HALO, bz // 2 + 8
@@ -585,7 +592,7 @@
         out_specs=[held] + [anywhere] * len(kept),
         scratch_shapes=[
             vmem(*field0), vmem(*field0), vmem(3, *field0), vmem(3, *field0), vmem(3, *field0), vmem(3, *field0),
-            vmem(3, *field0), vmem(2, *field0), vmem(3, *field0), vmem(3, r0, LANES),
+            vmem(3, *field0), vmem(2, *field0), vmem(3, *field0), vmem(n1 - 2, 3, r0, LANES),
             vmem(*field1), vmem(*field1), vmem(3, *field1), vmem(3, *field1), vmem(3, *field1), vmem(3, *field1),
             vmem(2, *field1), vmem(3, *field1), pltpu.SemaphoreType.DMA((10,)),
         ],
@@ -609,7 +616,7 @@
             vmem(*up1), vmem(2, *up1), vmem(3, *up1), vmem(3, *up1), vmem(3, *up1), vmem(3, *up1),
             vmem(*up2), vmem(*up2), vmem(*up2), vmem(6, *up2), vmem(*up2), vmem(*up2), vmem(*up2), vmem(*up2), vmem(*up2),
             vmem(*up3), vmem(*up3), vmem(*up3), vmem(6, *up3), vmem(*up3), vmem(*up3), vmem(*up3), vmem(*up3),
-            vmem(3, r0, LANES), pltpu.SemaphoreType.DMA((10,)),
+            vmem(heights * bz // 8, rows2 + 24, LANES), vmem(max(heights * bz // 4, 3 * (n1 - 6)), r0, LANES), pltpu.SemaphoreType.DMA((10,)),
         ],
         compiler_params=pltpu.CompilerParams(vmem_limit_bytes=40 * 2**20),
     )(received, *saved)

time: 46.6 us -> 44.8 us (0.961)
  blocking collectives: 26 us -> 29.9 us
  waiting for transfers between devices: 4.68 us -> 1.41 us
  starting transfers between devices: 6.14 us -> 3.66 us
    all_to_all x1, blocking collectives: 16 us -> 19.4 us  [local(): received = lax.all_to_all(send, ('tile', 'height'), 0, 0)]
    ppermute x2, waiting for transfers between devices: 4.68 us -> 1.41 us  [swapped(): return lax.ppermute(x, axis, pairs + [(j, i) for i, j in pairs])]
    ppermute x2, starting transfers between devices: 6.14 us -> 3.66 us  [swapped(): return lax.ppermute(x, axis, pairs + [(j, i) for i, j in pairs])]
    all_gather x1, blocking collectives: 9.96 us -> 10.5 us  [local(): bricks = lax.all_gather(jnp.concatenate([own, near, far], 0), 'height')]
  transfers between devices with their start and end apart: 2 -> 2, of which waited for: 2 -> 1; matrix products, arithmetic and copies ran while one was open for 0% -> 0% of each run, Pallas kernels for 0% -> 0%
where the time goes in v3:
time: 44.8 us; the launch traced here: 44.6 us
  blocking collectives  29.9 us (67%)
  Pallas kernels  9.56 us (21%)
  starting transfers between devices  3.66 us (8%)
  waiting for transfers between devices  1.41 us (3%)
    all_to_all x1, blocking collectives, local(): received = lax.all_to_all(send, ('tile', 'height'), 0, 0)  19.4 us
    all_gather x1, blocking collectives, local(): bricks = lax.all_gather(jnp.concatenate([own, near, far], 0), 'height')  10.5 us
    pallas_call x1, Pallas kernels, local(): pl.pallas_call(functools.partial(down_kernel, heights, tiles, bz, bx), ou...  5.66 us
    ppermute x2, starting transfers between devices, swapped(): return lax.ppermute(x, axis, pairs + [(j, i) for i, j in pairs])  3.66 us
    pallas_call x1, Pallas kernels, local(): pl.pallas_call(functools.partial(up_kernel, heights, tiles, bz, bx), out_...  2.92 us
    ppermute x2, waiting for transfers between devices, swapped(): return lax.ppermute(x, axis, pairs + [(j, i) for i, j in pairs])  1.41 us
    pallas_call x1, Pallas kernels, local(): pl.pallas_call(functools.partial(pack_kernel, bz, bx), out_shape=[pltpu.V...  0.98 us
  transfers between devices with their start and end apart: 2, of which 1 were waited for; matrix products, arithmetic and copies ran while one was open for 0% of the time, Pallas kernels for 0%

profile of v3, /device:TPU:0, one launch (start us, length us, event | category | flops | bytes accessed | tf_op | source)
XLA Modules:
  0.0 44.6 jit_solution(5879290015421263612)
XLA Ops:
  0.0 1.0 %shard_map.46 = (f32[324,128]{1,0:T(8,128)S(1)}, f32[90,128]{1,0:T(8,128)S(1)}, f32[90,128]{1,0:T(8,128)S(1)}) custom-call(s32[8,32,128]{2,1,0:T(8,128)} %material_ref.1, s32[8,32,128]{2,1,0:T(8,128)} %clamped_ref.1, f32[3]{0:T(128)} %table_ref.1, f32[3,3]{1,0:T(4,128)} %strain_ref.1), custom_call_target="tpu_custom_call" | custom-call | tf_op jit(solution)/shard_map/pallas_call | solution.py:561
  1.0 3.0 %collective-permute-start = (f32[90,128]{1,0:T(8,128)S(1)}, f32[90,128]{1,0:T(8,128)S(1)}, u32[]{:S(2)}, u32[]{:S(2)}) collective-permute-start(f32[90,128]{1,0:T(8,128)S(1)} %get-tuple-element.20), channel_id=1, source_target_pairs={{0,4},{8,12},{16,20},{24,28},{4,0},{12,8},{20,16},{28,24},{1,5},{9... | collective-permute-start | bytes 138248 | tf_op jit(solution)/shard_map/ppermute | solution.py:547
  4.0 0.7 %collective-permute-start.1 = (f32[90,128]{1,0:T(8,128)S(1)}, f32[90,128]{1,0:T(8,128)S(1)}, u32[]{:S(2)}, u32[]{:S(2)}) collective-permute-start(f32[90,128]{1,0:T(8,128)S(1)} %get-tuple-element.21), channel_id=1, source_target_pairs={{4,8},{12,16},{20,24},{8,4},{16,12},{24,20},{5,9},{13,17},{21,25},... | collective-permute-start | bytes 138248 | tf_op jit(solution)/shard_map/ppermute | solution.py:547
  4.7 1.4 %collective-permute-done = f32[90,128]{1,0:T(8,128)S(1)} collective-permute-done((f32[90,128]{1,0:T(8,128)S(1)}, f32[90,128]{1,0:T(8,128)S(1)}, u32[]{:S(2)}, u32[]{:S(2)}) %collective-permute-start) | collective-permute-done | bytes 46112 | tf_op jit(solution)/shard_map/ppermute | solution.py:547
  6.1 0.0 collective-permute-done.1
  6.1 10.5 %all-gather = f32[2016,128]{1,0:T(8,128)S(1)} all-gather(f32[504,128]{1,0:T(8,128)S(1)} %pad_maximum_fusion), channel_id=2, replica_groups=mesh['tile'=8,'height'=4] {'height'}, dimensions={0}, use_global_device_ids=true | all-gather | bytes 1290240 | tf_op jit(solution)/shard_map/all_gather | solution.py:576
  16.6 5.7 %shard_map.47 = (f32[32,9,2,128]{3,2,1,0:T(2,128)S(1)}, f32[10,48,128]{2,1,0:T(8,128)S(1)}, f32[2,8,32,128]{3,2,1,0:T(8,128)S(1)}, f32[3,10,48,128]{3,2,1,0:T(8,...) custom-call(f32[4,504,128]{2,1,0:T(8,128)S(1)} %bitcast.1), custom_call_target="tpu_custom_call" | custom-call | tf_op jit(solution)/shard_map/pallas_call | solution.py:588
  22.3 19.4 %all_to_all.5.recv_ref = f32[32,9,2,128]{3,2,1,0:T(2,128)S(1)} all-to-all(f32[32,9,2,128]{3,2,1,0:T(2,128)S(1)} %get-tuple-element.22), channel_id=1, replica_groups=mesh['tile'=8,'height'=4] {'tile','height'}, dimensions={0} | all-to-all | bytes 589824 | tf_op jit(solution)/shard_map/all_to_all | solution.py:602
  41.7 2.9 %shard_map.48 = f32[3,8,32,128]{3,2,1,0:T(8,128)} custom-call(f32[32,9,2,128]{3,2,1,0:T(2,128)S(1)} %all_to_all.5.recv_ref, f32[10,48,128]{2,1,0:T(8,128)S(1)} %get-tuple-element.23.s0_in, f32[2,8,32,128]{3,2,1,0:T(8,128)S(1)} %get-tuple-element.24.y0_in, f32[3,10,48,128]{3,2,1,0:T(8,128)S(1)} %get-tuple-element.25.v0_in, ...), custom_call_target="tpu_custom_call" | custom-call | tf_op jit(solution)/shard_map/pallas_call | solution.py:609
  (1 shorter events, 0.0 us)
Async XLA Ops:
  1.0 5.1 %collective-permute-start = (f32[90,128]{1,0:T(8,128)S(1)}, f32[90,128]{1,0:T(8,128)S(1)}, u32[]{:S(2)}, u32[]{:S(2)}) collective-permute-start(f32[90,128]{1,0:T(8,128)S(1)} %get-tuple-element.20), channel_id=1, source_target_pairs={{0,4},{8,12},{16,20},{24,28},{4,0},{12,8},{20,16},{28,24},{1,5},{9... | collective-permute-start | bytes 138248 | tf_op jit(solution)/shard_map/ppermute | solution.py:547
  4.0 2.1 %collective-permute-start.1 = (f32[90,128]{1,0:T(8,128)S(1)}, f32[90,128]{1,0:T(8,128)S(1)}, u32[]{:S(2)}, u32[]{:S(2)}) collective-permute-start(f32[90,128]{1,0:T(8,128)S(1)} %get-tuple-element.21), channel_id=1, source_target_pairs={{4,8},{12,16},{20,24},{8,4},{16,12},{24,20},{5,9},{13,17},{21,25},... | collective-permute-start | bytes 138248 | tf_op jit(solution)/shard_map/ppermute | solution.py:547

commit v4 on v3

--- a/solution.py
+++ b/solution.py
@@ -144,9 +144,13 @@
     return result
 
 
-def pack_kernel(
-    bz, bx, material_ref, clamped_ref, table_ref, strain_ref, own_ref, near_ref, far_ref, label, joined, table, strain, sem
-):
+def strips(bz):
+    counts = [min(layer, HALO, bz + 2 * HALO - 1 - layer) for layer in range(bz + 2 * HALO)]
+    starts = [sum(counts[:layer]) for layer in range(len(counts))]
+    return counts, starts, sum(counts)
+
+
+def pack_kernel(bz, bx, material_ref, clamped_ref, table_ref, strain_ref, own_ref, label, joined, table, strain, sem):
     copies = [
         pltpu.make_async_copy(material_ref, label, sem.at[0]),
         pltpu.make_async_copy(clamped_ref.at[pl.ds(0, 2)], joined, sem.at[1]),
@@ -157,14 +161,9 @@
         copy.start()
     for copy in copies:
         copy.wait()
-    odd = (lax.axis_index("tile") & 1) == 1
     for slot in range(bz + 2):
         src = label.at[slot] if slot < bz else joined.at[slot - bz]
         own_ref[pl.ds(slot * bx, bx), :] = src[...].astype(F32)
-        first = src[pl.ds(0, HALO), :].astype(F32)
-        last = src[pl.ds(bx - HALO, HALO), :].astype(F32)
-        near_ref[pl.ds(slot * HALO, HALO), :] = jnp.where(odd, first, last)
-        far_ref[pl.ds(slot * HALO, HALO), :] = jnp.where(odd, last, first)
     lane = lane_of(SPARE)
     row = jnp.zeros((SPARE, LANES), F32)
     for k in range(3):
@@ -174,75 +173,135 @@
     own_ref[pl.ds((bz + 2) * bx, SPARE), :] = row
 
 
+def place(heights, bz, layer):
+    z = bz * lax.axis_index("height") - HALO + layer
+    z_in = jnp.clip(z, 0, heights * bz - 1)
+    return z, z_in // bz, z_in % bz
+
+
+def strip_kernel(heights, bz, bx, x_ref, near_ref, far_ref):
+    odd = (lax.axis_index("tile") & 1) == 1
+    counts, starts, end = strips(bz)
+    wanted = [(place(heights, bz, layer)[1:], count, start) for layer, (count, start) in enumerate(zip(counts, starts))]
+    wanted += [((0, bz + k), HALO, end + HALO * k) for k in range(2)]
+    for (brick, slot), count, start in wanted:
+        if count:
+            first = x_ref[brick, pl.ds(slot * bx, count), :]
+            last = x_ref[brick, pl.ds(slot * bx + bx - count, count), :]
+            near_ref[pl.ds(start, count), :] = jnp.where(odd, first, last)
+            far_ref[pl.ds(start, count), :] = jnp.where(odd, last, first)
+
+
+def tables_of(x_ref, row):
+    spare = x_ref[0, pl.ds(row, 1), :]
+    table = [jnp.broadcast_to(spare[:, k : k + 1], (1, LANES)) for k in range(12)]
+    return table[:3], [table[3 + 3 * c : 6 + 3 * c] for c in range(3)]
+
+
+def store_layer(s, st, label, layer, to, weight, tables):
+    is0, is1 = label == 0.0, label == 1.0
+    dst = pl.ds(to, label.shape[0])
+    for ref, values in zip((s, *(st.at[c] for c in range(3))), (tables[0], *tables[1])):
+        a, b, c = (value * weight for value in values)
+        ref[layer, dst, :] = jnp.where(is0, a, jnp.where(is1, b, c))
+
+
+def store_strip(s, st, p, strip_ref, heights, bz, layer, far_side, valid, bx, tables):
+    counts, starts, end = strips(bz)
+    z, _, _ = place(heights, bz, layer)
+    weight = jnp.where((z >= 0) & (z < heights * bz), valid, 0.0)
+    count = counts[layer]
+    if count:
+        to = jnp.where(far_side, 16 + bx, 16 - count)
+        store_layer(s, st, strip_ref[pl.ds(starts[layer], count), :], layer, to, weight, tables)
+    joined = strip_ref[pl.ds(end + HALO * jnp.clip(z, 0, 1), HALO), :]
+    to = jnp.where(far_side, 16 + bx, 16 - HALO)
+    p[layer, pl.ds(to, HALO), :] = joined * jnp.where((z >= 0) & (z < 2), 2.0 * PENALTY * valid, 0.0)
+
+
+def fine_setup(s, p, st, b, r, d, g, y, layer, row, count):
+    lane = lane_of(count)
+    here = st[2, layer, pl.ds(row, count), :]
+    source = [
+        0.5 * (rows_at(st.at[0], layer - 1, row, count) - rows_at(st.at[0], layer + 1, row, count)),
+        0.5 * (rows_at(st.at[1], layer, row - 1, count) - rows_at(st.at[1], layer, row + 1, count)),
+        0.5 * (jnp.where(lane < 1, 0.0, roll(here, 1)) - jnp.where(lane >= LANES - 1, 0.0, roll(here, -1))),
+    ]
+    for c in range(3):
+        b[c, layer, pl.ds(row, count), :] = source[c]
+    level_setup(s, p, r, d, g, y, lambda c: source[c], layer, row, count, 1)
+
+
+def fine_down(bz, s, p, st, b, r, d, g, y, v, rest, rows, step):
+    nz = bz + 2 * HALO
+
+    def setup0(layer, carry):
+        for row in rows[0]:
+            fine_setup(s, p, st, b, r, d, g, y, layer, row, 16)
+        return carry
+
+    def sweep0(layer, carry):
+        for row in rows[1]:
+            first_sweep(s, y, r, g, v, layer, row, 16, 1)
+        return carry
+
+    def restrict0(j, carry):
+        layer = 3 + 2 * j
+        for row in rows[2]:
+            one = remainder(s, y, b, d, v, layer, row, 16, 1)
+            two = remainder(s, y, b, d, v, layer + 1, row, 16, 1)
+            for c in range(3):
+                rest[j, c, pl.ds(row, 16), :] = one[c] + two[c]
+        return carry
+
+    each(1, nz - 1, setup0, step)
+    each(2, nz - 2, sweep0, step)
+    each(0, bz // 2 + 6, restrict0, step)
+
+
+def inner_kernel(heights, tiles, bz, bx, x_ref, near_ref, s, p, st, b, r, d, g, y, v, rest):
+    t = lax.axis_index("tile")
+    odd = (t & 1) == 1
+    tables = tables_of(x_ref, (bz + 2) * bx)
+    valid = jnp.where(odd | (t < tiles - 1), 1.0, 0.0)
+
+    def read_layer(layer, carry):
+        z, brick, slot = place(heights, bz, layer)
+        inside = jnp.where((z >= 0) & (z < heights * bz), 1.0, 0.0)
+        store_layer(s, st, x_ref[brick, pl.ds(slot * bx, bx), :], layer, 16, inside, tables)
+        bottom = jnp.where((z >= 0) & (z < 2), 2.0 * PENALTY, 0.0)
+        p[layer, pl.ds(16, bx), :] = x_ref[0, pl.ds((bz + jnp.clip(z, 0, 1)) * bx, bx), :] * bottom
+        store_strip(s, st, p, near_ref, heights, bz, layer, jnp.logical_not(odd), valid, bx, tables)
+        return carry
+
+    each(0, bz + 2 * HALO, read_layer, bz + 2 * HALO + 1)
+    rows = [[jnp.where(odd, 8 - k, 24 + k) + at for at in range(0, bx, 16)] for k in range(3)]
+    fine_down(bz, s, p, st, b, r, d, g, y, v, rest, rows, 8)
+
+
 def down_kernel(
     heights, tiles, bz, bx,
-    x_ref,
-    send_ref, s0_out, y0_out, v0_out, g0_out, r0_out, s1_out, y1_out, v1_out, g1_out, r1_out,
-    s, p, st, b, r, d, g, y, v, tmp, s1, p1, b1, r1, d1, g1, y1, v1, sem,
+    x_ref, far_ref, *refs,
 ):
-    h, t = lax.axis_index("height"), lax.axis_index("tile")
-    nz, n1 = bz + 2 * HALO, bz // 2 + 8
+    (
+        send_ref, s0_out, y0_out, v0_out, g0_out, r0_out, s1_out, y1_out, v1_out, g1_out, r1_out,
+        s, p, st, b, r, d, g, y, v, rest, tmp, s1, p1, b1, r1, d1, g1, y1, v1, sem,
+    ) = refs[10:]
+    t = lax.axis_index("tile")
+    odd = (t & 1) == 1
+    n1 = bz // 2 + 8
     bx1, bx2 = bx // 2, bx // 4
-    low, high = 8, bx + 24
-    own_rows, halo_rows = (bz + 2) * bx + SPARE, (bz + 2) * HALO
-    low_rows = own_rows + jnp.where((t & 1) == 1, 0, halo_rows)
-    high_rows = own_rows + jnp.where((t & 1) == 1, halo_rows, 0)
-    spare = x_ref[0, pl.ds(own_rows - SPARE, 1), :]
-    table = [jnp.broadcast_to(spare[:, k : k + 1], (1, LANES)) for k in range(12)]
-    strain = [table[3 + 3 * c : 6 + 3 * c] for c in range(3)]
-    before = jnp.where(t > 0, 1.0, 0.0)
-    behind = jnp.where(t < tiles - 1, 1.0, 0.0)
+    low = 8
+    tables = tables_of(x_ref, (bz + 2) * bx)
+    valid = jnp.where(jnp.where(odd, t < tiles - 1, t > 0), 1.0, 0.0)
 
     def read_layer(layer, carry):
-        z = bz * h - HALO + layer
-        inside = jnp.where((z >= 0) & (z < heights * bz), 1.0, 0.0)
-        bottom = jnp.where((z >= 0) & (z < 2), 2.0 * PENALTY, 0.0)
-        z_in = jnp.clip(z, 0, heights * bz - 1)
-        brick, slot = z_in // bz, z_in % bz
-        clamp_slot = bz + jnp.clip(z, 0, 1)
-        parts = [
-            (slot * bx, clamp_slot * bx, bx, 16, 1.0),
-            (low_rows + slot * HALO, low_rows + clamp_slot * HALO, HALO, 16 - HALO, before),
-            (high_rows + slot * HALO, high_rows + clamp_slot * HALO, HALO, 16 + bx, behind),
-        ]
-        for at, clamp_at, count, to, valid in parts:
-            label = x_ref[brick, pl.ds(at, count), :]
-            is0, is1 = label == 0.0, label == 1.0
-            weight = inside * valid
-            stiff = [table[k] * weight for k in range(3)]
-            dst = pl.ds(to, count)
-            s[layer, dst, :] = jnp.where(is0, stiff[0], jnp.where(is1, stiff[1], stiff[2]))
-            for c in range(3):
-                e = [strain[c][k] * weight for k in range(3)]
-                st[c, layer, dst, :] = jnp.where(is0, e[0], jnp.where(is1, e[1], e[2]))
-            joined = x_ref[0, pl.ds(clamp_at, count), :]
-            p[layer, dst, :] = joined * (bottom * valid)
-        return carry
-
-    each(0, nz, read_layer, 8)
-
-    def setup0(layer, carry):
-        for row, count in chunks(low, high, 16):
-            lane = lane_of(count)
-            here = st[2, layer, pl.ds(row, count), :]
-            source = [
-                0.5 * (rows_at(st.at[0], layer - 1, row, count) - rows_at(st.at[0], layer + 1, row, count)),
-                0.5 * (rows_at(st.at[1], layer, row - 1, count) - rows_at(st.at[1], layer, row + 1, count)),
-                0.5 * (jnp.where(lane < 1, 0.0, roll(here, 1)) - jnp.where(lane >= LANES - 1, 0.0, roll(here, -1))),
-            ]
-            for c in range(3):
-                b[c, layer, pl.ds(row, count), :] = source[c]
-            level_setup(s, p, r, d, g, y, lambda c: source[c], layer, row, count, 1)
-        return carry
-
-    each(1, nz - 1, setup0, 8)
-
-    def sweep0(layer, carry):
-        for row, count in chunks(low, high, 16):
-            first_sweep(s, y, r, g, v, layer, row, count, 1)
-        return carry
-
-    each(2, nz - 2, sweep0, 8)
+        store_strip(s, st, p, far_ref, heights, bz, layer, odd, valid, bx, tables)
+        return carry
+
+    each(0, bz + 2 * HALO, read_layer, bz + 2 * HALO + 1)
+    rows = [[jnp.where(odd, bx + 8 - k, 8 + k)] for k in range(3)]
+    fine_down(bz, s, p, st, b, r, d, g, y, v, rest, rows, 24)
 
     own = (pl.ds(HALO, bz), pl.ds(16, bx))
     near = (pl.ds(HALO - 1, bz + 2), pl.ds(low, bx + 16))
@@ -261,14 +320,8 @@
     rows1 = bx1 + 8
 
     def restrict0(j, carry):
-        layer = 3 + 2 * j
-        for row, count in chunks(low, high, 16):
-            one = remainder(s, y, b, d, v, layer, row, count, 1)
-            two = remainder(s, y, b, d, v, layer + 1, row, count, 1)
-            for c in range(3):
-                tmp[j, c, pl.ds(row, count), :] = one[c] + two[c]
         for c in range(3):
-            b1[c, j + 1, pl.ds(8, rows1), :] = pair_lanes(pair_rows(tmp.at[j, c], low, rows1), 1)
+            b1[c, j + 1, pl.ds(8, rows1), :] = pair_lanes(pair_rows(rest.at[j, c], low, rows1), 1)
         return carry
 
     each(0, n1 - 2, restrict0, 8)
@@ -557,23 +610,27 @@
     held = pl.BlockSpec(memory_space=pltpu.VMEM)
     anywhere = pl.BlockSpec(memory_space=pl.ANY)
     outside = pl.BlockSpec(memory_space=pltpu.HBM)
-    slots = bz + 2
-    own, near, far = pl.pallas_call(
+    own = pl.pallas_call(
         functools.partial(pack_kernel, bz, bx),
-        out_shape=[
-            pltpu.VMEM((rows, LANES), F32)
-            for rows in (slots * bx + SPARE, slots * HALO, slots * HALO)
-        ],
+        out_shape=pltpu.VMEM(((bz + 2) * bx + SPARE, LANES), F32),
         in_specs=[outside] * 4,
-        out_specs=[held] * 3,
+        out_specs=held,
         scratch_shapes=[
             pltpu.VMEM((bz, bx, LANES), jnp.int32), pltpu.VMEM((2, bx, LANES), jnp.int32),
             pltpu.SMEM((3,), F32), pltpu.SMEM((3, 3), F32), pltpu.SemaphoreType.DMA((4,)),
         ],
     )(material, clamped, stiffness_table, eigenstrain)
+    bricks = lax.all_gather(own, "height")
+    strip = pltpu.VMEM((-(-(strips(bz)[2] + 2 * HALO) // 8) * 8, LANES), F32)
+    near, far = pl.pallas_call(
+        functools.partial(strip_kernel, heights, bz, bx),
+        out_shape=[strip, strip],
+        in_specs=[held],
+        out_specs=[held, held],
+        compiler_params=pltpu.CompilerParams(vmem_limit_bytes=4 * 2**20),
+    )(bricks)
     far = swapped(far, "tile", 1)
     near = swapped(near, "tile", 0)
-    bricks = lax.all_gather(jnp.concatenate([own, near, far], 0), "height")
 
     bx1, bx2 = bx // 2, bx // 4
     nz, n1 = bz + 2 * HALO, bz // 2 + 8
@@ -585,19 +642,33 @@
     ]
     kept = [jax.ShapeDtypeStruct((*shape, LANES), F32) for shape in kept]
     field0, field1 = (nz, r0, LANES), (n1, r1, LANES)
+    fields = [field0, field0, (3, *field0), (3, *field0), (3, *field0), (3, *field0), (3, *field0), (2, *field0), (3, *field0)]
+    fields = [pltpu.VMEM(shape, F32) for shape in [*fields, (n1 - 2, 3, r0, LANES)]]
+    work = 24 * 6 * 3 * 1024
+    inner = pl.pallas_call(
+        functools.partial(inner_kernel, heights, tiles, bz, bx),
+        out_shape=fields,
+        in_specs=[held] * 2,
+        out_specs=[held] * len(fields),
+        cost_estimate=pl.CostEstimate(flops=work * 60, bytes_accessed=work * 40, transcendentals=0),
+        compiler_params=pltpu.CompilerParams(vmem_limit_bytes=4 * 2**20),
+    )(bricks, near)
     send, *saved = pl.pallas_call(
         functools.partial(down_kernel, heights, tiles, bz, bx),
-        out_shape=[jax.ShapeDtypeStruct((heights * tiles, (bz // 4 * bx2 + bx2 // 4) // 2, 2, LANES), F32), *kept],
-        in_specs=[held],
-        out_specs=[held] + [anywhere] * len(kept),
+        out_shape=[
+            jax.ShapeDtypeStruct((heights * tiles, (bz // 4 * bx2 + bx2 // 4) // 2, 2, LANES), F32), *kept, *fields
+        ],
+        in_specs=[held] * (2 + len(fields)),
+        out_specs=[held] + [anywhere] * len(kept) + [held] * len(fields),
+        input_output_aliases={2 + k: 1 + len(kept) + k for k in range(len(fields))},
         scratch_shapes=[
-            vmem(*field0), vmem(*field0), vmem(3, *field0), vmem(3, *field0), vmem(3, *field0), vmem(3, *field0),
-            vmem(3, *field0), vmem(2, *field0), vmem(3, *field0), vmem(n1 - 2, 3, r0, LANES),
+            vmem(n1 - 2, 3, r0, LANES),
             vmem(*field1), vmem(*field1), vmem(3, *field1), vmem(3, *field1), vmem(3, *field1), vmem(3, *field1),
             vmem(2, *field1), vmem(3, *field1), pltpu.SemaphoreType.DMA((10,)),
         ],
-        compiler_params=pltpu.CompilerParams(vmem_limit_bytes=40 * 2**20),
-    )(bricks)
+        compiler_params=pltpu.CompilerParams(vmem_limit_bytes=12 * 2**20),
+    )(bricks, far, *inner)
+    saved = saved[: len(kept)]
 
     received = lax.all_to_all(send, ("tile", "height"), 0, 0)
 
@@ -618,7 +689,7 @@
             vmem(*up3), vmem(*up3), vmem(*up3), vmem(6, *up3), vmem(*up3), vmem(*up3), vmem(*up3), vmem(*up3),
             vmem(heights * bz // 8, rows2 + 24, LANES), vmem(max(heights * bz // 4, 3 * (n1 - 6)), r0, LANES), pltpu.SemaphoreType.DMA((10,)),
         ],
-        compiler_params=pltpu.CompilerParams(vmem_limit_bytes=40 * 2**20),
+        compiler_params=pltpu.CompilerParams(vmem_limit_bytes=16 * 2**20),
     )(received, *saved)
 
 

time: 44.8 us -> 41 us (0.915)
  blocking collectives: 29.9 us -> 26.2 us
  starting transfers between devices: 3.66 us -> 2.21 us
  waiting for transfers between devices: 1.41 us -> 2.64 us
    pallas_call x1 -> x3, Pallas kernels: 0.98 us -> 3.96 us  [the longest x1 2.88 us: local(): pl.pallas_call(functools.partial(inner_kernel, heights, tiles, bz, bx), o...]
    pallas_call x1, Pallas kernels: 5.66 us -> 2.83 us  [local(): pl.pallas_call(functools.partial(down_kernel, heights, tiles, bz, bx), ou...]
    all_to_all x1, blocking collectives: 19.4 us -> 16.8 us  [local(): received = lax.all_to_all(send, ('tile', 'height'), 0, 0)]
    ppermute x2, starting transfers between devices: 3.66 us -> 2.21 us  [swapped(): return lax.ppermute(x, axis, pairs + [(j, i) for i, j in pairs])]
    ppermute x2, waiting for transfers between devices: 1.41 us -> 2.64 us  [swapped(): return lax.ppermute(x, axis, pairs + [(j, i) for i, j in pairs])]
    all_gather x1, blocking collectives: 10.5 us -> 9.45 us  [local(): bricks = lax.all_gather(own, 'height')]
  transfers between devices with their start and end apart: 2 -> 2, of which waited for: 1 -> 1; matrix products, arithmetic and copies ran while one was open for 0% -> 0% of each run, Pallas kernels for 0% -> 7%
where the time goes in v4:
time: 41 us; the launch traced here: 40.8 us
  blocking collectives  26.2 us (64%)
  Pallas kernels  9.7 us (24%)
  waiting for transfers between devices  2.64 us (6%)
  starting transfers between devices  2.21 us (5%)
    all_to_all x1, blocking collectives, local(): received = lax.all_to_all(send, ('tile', 'height'), 0, 0)  16.8 us
    all_gather x1, blocking collectives, local(): bricks = lax.all_gather(own, 'height')  9.45 us
    pallas_call x1, Pallas kernels, local(): pl.pallas_call(functools.partial(up_kernel, heights, tiles, bz, bx), out_...  2.92 us
    pallas_call x1, Pallas kernels, local(): pl.pallas_call(functools.partial(inner_kernel, heights, tiles, bz, bx), o...  2.88 us
    pallas_call x1, Pallas kernels, local(): pl.pallas_call(functools.partial(down_kernel, heights, tiles, bz, bx), ou...  2.83 us
    ppermute x2, waiting for transfers between devices, swapped(): return lax.ppermute(x, axis, pairs + [(j, i) for i, j in pairs])  2.64 us
    ppermute x2, starting transfers between devices, swapped(): return lax.ppermute(x, axis, pairs + [(j, i) for i, j in pairs])  2.21 us
    pallas_call x1, Pallas kernels, local(): pl.pallas_call(functools.partial(pack_kernel, bz, bx), out_shape=pltpu.VM...  0.97 us
  transfers between devices with their start and end apart: 2, of which 1 were waited for; matrix products, arithmetic and copies ran while one was open for 0% of the time, Pallas kernels for 7%

profile of v4, /device:TPU:0, one launch (start us, length us, event | category | flops | bytes accessed | tf_op | source)
XLA Modules:
  0.0 40.8 jit_solution(14313103729794441536)
XLA Ops:
  0.0 1.0 %shard_map.46 = f32[324,128]{1,0:T(8,128)S(1)} custom-call(s32[8,32,128]{2,1,0:T(8,128)} %material_ref.1, s32[8,32,128]{2,1,0:T(8,128)} %clamped_ref.1, f32[3]{0:T(128)} %table_ref.1, f32[3,3]{1,0:T(4,128)} %strain_ref.1), custom_call_target="tpu_custom_call" | custom-call | tf_op jit(solution)/shard_map/pallas_call | solution.py:613
  1.0 9.4 %all-gather.1.x_ref = f32[4,324,128]{2,1,0:T(8,128)S(1)} all-gather(f32[1,324,128]{2,1,0:T(8,128)S(1)} %bitcast.1), channel_id=2, replica_groups=mesh['tile'=8,'height'=4] {'height'}, dimensions={0}, use_global_device_ids=true | all-gather | bytes 829440 | tf_op jit(solution)/shard_map/all_gather | solution.py:623
  10.4 0.1 shard_map.47
  10.5 1.6 %collective-permute-start.1 = (f32[168,128]{1,0:T(8,128)S(1)}, f32[168,128]{1,0:T(8,128)S(1)}, u32[]{:S(2)}, u32[]{:S(2)}) collective-permute-start(f32[168,128]{1,0:T(8,128)S(1)} %get-tuple-element.29), channel_id=1, source_target_pairs={{0,4},{8,12},{16,20},{24,28},{4,0},{12,8},{20,16},{28,24},{1,5},{9... | collective-permute-start | bytes 258056 | tf_op jit(solution)/shard_map/ppermute | solution.py:600
  12.1 0.7 %collective-permute-start = (f32[168,128]{1,0:T(8,128)S(1)}, f32[168,128]{1,0:T(8,128)S(1)}, u32[]{:S(2)}, u32[]{:S(2)}) collective-permute-start(f32[168,128]{1,0:T(8,128)S(1)} %get-tuple-element.28), channel_id=1, source_target_pairs={{4,8},{12,16},{20,24},{8,4},{16,12},{24,20},{5,9},{13,17},{21,25},... | collective-permute-start | bytes 258056 | tf_op jit(solution)/shard_map/ppermute | solution.py:600
  12.8 2.6 %collective-permute-done.1.near_ref = f32[168,128]{1,0:T(8,128)S(1)} collective-permute-done((f32[168,128]{1,0:T(8,128)S(1)}, f32[168,128]{1,0:T(8,128)S(1)}, u32[]{:S(2)}, u32[]{:S(2)}) %collective-permute-start.1) | collective-permute-done | bytes 86048 | tf_op jit(solution)/shard_map/ppermute | solution.py:600
  15.4 2.9 %shard_map.48 = (f32[26,64,128]{2,1,0:T(8,128)S(1)}, f32[26,64,128]{2,1,0:T(8,128)S(1)}, f32[3,26,64,128]{3,2,1,0:T(8,128)S(1)}, f32[3,26,64,128]{3,2,1,0:T(8,12...) custom-call(f32[4,324,128]{2,1,0:T(8,128)S(1)} %all-gather.1.x_ref, ...), custom_call_target="tpu_custom_call" | custom-call | flops 26542080 | bytes 17694720 | tf_op jit(solution)/shard_map/pallas_call | solution.py:648
  18.3 0.0 collective-permute-done.far_ref
  18.3 2.8 %shard_map.49 = (f32[32,9,2,128]{3,2,1,0:T(2,128)S(1)}, f32[10,48,128]{2,1,0:T(8,128)S(1)}, f32[2,8,32,128]{3,2,1,0:T(8,128)S(1)}, f32[3,10,48,128]{3,2,1,0:T(8,...) custom-call(f32[4,324,128]{2,1,0:T(8,128)S(1)} %all-gather.1.x_ref, ...), custom_call_target="tpu_custom_call", output_to_operand_aliasing={{11}: (2, {}), {12}: (3, {}), {13}: (4, {}), {14}: (5, {}),... | custom-call | tf_op jit(solution)/shard_map/pallas_call | solution.py:656
  21.1 16.8 %all_to_all.5.recv_ref = f32[32,9,2,128]{3,2,1,0:T(2,128)S(1)} all-to-all(f32[32,9,2,128]{3,2,1,0:T(2,128)S(1)} %get-tuple-element.40), channel_id=1, replica_groups=mesh['tile'=8,'height'=4] {'tile','height'}, dimensions={0} | all-to-all | bytes 589824 | tf_op jit(solution)/shard_map/all_to_all | solution.py:673
  37.9 2.9 %shard_map.50 = f32[3,8,32,128]{3,2,1,0:T(8,128)} custom-call(f32[32,9,2,128]{3,2,1,0:T(2,128)S(1)} %all_to_all.5.recv_ref, f32[10,48,128]{2,1,0:T(8,128)S(1)} %get-tuple-element.41.s0_in, f32[2,8,32,128]{3,2,1,0:T(8,128)S(1)} %get-tuple-element.42.y0_in, f32[3,10,48,128]{3,2,1,0:T(8,128)S(1)} %get-tuple-element.43.v0_in, ...), custom_call_target="tpu_custom_call" | custom-call | tf_op jit(solution)/shard_map/pallas_call | solution.py:680
Async XLA Ops:
  10.5 4.9 %collective-permute-start.1 = (f32[168,128]{1,0:T(8,128)S(1)}, f32[168,128]{1,0:T(8,128)S(1)}, u32[]{:S(2)}, u32[]{:S(2)}) collective-permute-start(f32[168,128]{1,0:T(8,128)S(1)} %get-tuple-element.29), channel_id=1, source_target_pairs={{0,4},{8,12},{16,20},{24,28},{4,0},{12,8},{20,16},{28,24},{1,5},{9... | collective-permute-start | bytes 258056 | tf_op jit(solution)/shard_map/ppermute | solution.py:600
  12.1 6.2 %collective-permute-start = (f32[168,128]{1,0:T(8,128)S(1)}, f32[168,128]{1,0:T(8,128)S(1)}, u32[]{:S(2)}, u32[]{:S(2)}) collective-permute-start(f32[168,128]{1,0:T(8,128)S(1)} %get-tuple-element.28), channel_id=1, source_target_pairs={{4,8},{12,16},{20,24},{8,4},{16,12},{24,20},{5,9},{13,17},{21,25},... | collective-permute-start | bytes 258056 | tf_op jit(solution)/shard_map/ppermute | solution.py:600

commit v5 on v4

--- a/solution.py
+++ b/solution.py
@@ -283,11 +283,8 @@
     heights, tiles, bz, bx,
     x_ref, far_ref, *refs,
 ):
-    (
-        send_ref, s0_out, y0_out, v0_out, g0_out, r0_out, s1_out, y1_out, v1_out, g1_out, r1_out,
-        s, p, st, b, r, d, g, y, v, rest, tmp, s1, p1, b1, r1, d1, g1, y1, v1, sem,
-    ) = refs[10:]
-    t = lax.axis_index("tile")
+    send_ref, s1, y1, v1, g1, r1, s, p, st, b, r, d, g, y, v, rest, tmp, p1, b1, d1 = refs[10:]
+    h, t = lax.axis_index("height"), lax.axis_index("tile")
     odd = (t & 1) == 1
     n1 = bz // 2 + 8
     bx1, bx2 = bx // 2, bx // 4
@@ -303,20 +300,6 @@
     rows = [[jnp.where(odd, bx + 8 - k, 8 + k)] for k in range(3)]
     fine_down(bz, s, p, st, b, r, d, g, y, v, rest, rows, 24)
 
-    own = (pl.ds(HALO, bz), pl.ds(16, bx))
-    near = (pl.ds(HALO - 1, bz + 2), pl.ds(low, bx + 16))
-    copies = [
-        (s.at[near[0], near[1]], s0_out),
-        (y.at[:, own[0], own[1]], y0_out),
-        (v.at[:, near[0], near[1]], v0_out),
-        (g.at[:, own[0], own[1]], g0_out),
-        (r.at[:, own[0], own[1]], r0_out),
-    ]
-    started = []
-    for k, (src, dst) in enumerate(copies):
-        started.append(pltpu.make_async_copy(src, dst, sem.at[k]))
-        started[-1].start()
-
     rows1 = bx1 + 8
 
     def restrict0(j, carry):
@@ -348,17 +331,6 @@
         return carry
 
     each(2, n1 - 2, sweep1, 8)
-
-    copies = [
-        (s1.at[pl.ds(2, n1 - 4), pl.ds(8, rows1)], s1_out),
-        (y1.at[:, pl.ds(3, n1 - 6), pl.ds(8, rows1)], y1_out),
-        (v1.at[:, pl.ds(2, n1 - 4), pl.ds(8, rows1)], v1_out),
-        (g1.at[:, pl.ds(3, n1 - 6), pl.ds(8, rows1)], g1_out),
-        (r1.at[:, pl.ds(3, n1 - 6), pl.ds(8, rows1)], r1_out),
-    ]
-    for k, (src, dst) in enumerate(copies):
-        started.append(pltpu.make_async_copy(src, dst, sem.at[5 + k]))
-        started[-1].start()
 
     lane = lane_of(bx2) & 3
     packed = []
@@ -375,53 +347,44 @@
         packed.append(
             jnp.where(lane == 0, fields[0], jnp.where(lane == 1, fields[1], jnp.where(lane == 2, fields[2], stiff)))
         )
-    both = [pair_rows(p1.at[4 + i], 12, bx2) for i in range(2)]
+    bottom = jnp.maximum(bz // 2 * (1 - h), 0)
+    both = [pair_rows(p1.at[bottom + i], 12, bx2) for i in range(2)]
     tmp[2, 0, pl.ds(0, bx2), :] = pair_lanes(both[0] + both[1], 2)
-    quarter = bx2 // 4
-    part = [tmp[2, 0, pl.ds(j, quarter, stride=4), :] for j in range(4)]
+    quarter = bx2 // 8
+    first = jnp.minimum(h, 1) * (bx2 // 2)
+    part = [tmp[2, 0, pl.ds(first + j, quarter, stride=4), :] for j in range(4)]
     lane = lane_of(quarter) & 3
     packed.append(jnp.where(lane == 0, part[0], jnp.where(lane == 1, part[1], jnp.where(lane == 2, part[2], part[3]))))
+    size = sum(value.shape[0] for value in packed)
 
     def fill(i, carry):
-        for m, value in enumerate(packed):
-            for k in range(value.shape[0] // 2):
-                send_ref[i, m * bx2 // 2 + k, :, :] = value[2 * k : 2 * k + 2]
+        at = i * size
+        for value in packed:
+            send_ref[pl.ds(at, value.shape[0]), :] = value
+            at = at + value.shape[0]
         return carry
 
     each(0, heights * tiles, fill, 8)
-    for copy in started:
-        copy.wait()
 
 
 def up_kernel(
     heights, tiles, bz, bx,
-    recv_ref, s0_in, y0_in, v0_in, g0_in, r0_in, s1_in, y1_in, v1_in, g1_in, r1_in,
-    out_ref,
-    s0, y0, v0, g0, r0, s1, y1, v1, g1, r1, f1, s2, p2, b2, q2, r2, d2, g2, v2, f2, s3, p3, b3, q3, r3, g3, va, vb, rest2, tmp, sem,
+    recv_ref, s0, y0, v0, g0, r0, s1, y1, v1, g1, r1, out_ref,
+    w0, w1, f1, s2, p2, b2, q2, r2, d2, g2, v2, f2, s3, p3, b3, q3, r3, g3, va, vb, rest2, tmp, done, sem,
 ):
     h, t = lax.axis_index("height"), lax.axis_index("tile")
     bx1, bx2, bz2 = bx // 2, bx // 4, bz // 4
-    n1, n2, n3 = bz // 2 + 4, heights * bz // 4, heights * bz // 8
+    n1, n2, n3 = bz // 2 + 8, heights * bz // 4, heights * bz // 8
     rows1 = bx1 + 8
     near = pl.ds(8, bx + 16)
-    own = pl.ds(16, bx)
     mid = pl.ds(8, rows1)
-    copies = [
-        (s1_in, s1.at[:, mid]), (y1_in, y1.at[:, pl.ds(1, n1 - 2), mid]), (v1_in, v1.at[:, :, mid]),
-        (g1_in, g1.at[:, pl.ds(1, n1 - 2), mid]), (r1_in, r1.at[:, pl.ds(1, n1 - 2), mid]),
-        (s0_in, s0.at[:, near]), (y0_in, y0.at[:, pl.ds(1, bz), own]), (v0_in, v0.at[:, :, near]),
-        (g0_in, g0.at[:, pl.ds(1, bz), own]), (r0_in, r0.at[:, pl.ds(1, bz), own]),
-    ]
-    started = []
-    for k, (src, dst) in enumerate(copies):
-        started.append(pltpu.make_async_copy(src, dst, sem.at[k]))
-        started[-1].start()
 
     for ref in (s2, p2, g2, v2, f2, s3, p3, g3, va, vb):
         ref[...] = jnp.zeros(ref.shape, F32)
     rest2[...] = jnp.zeros(rest2.shape, F32)
 
     side = REACH // bx2
+    size = bz2 * bx2 + bx2 // 8
     lane = lane_of(bx2) & 3
     for dt in range(-side, side + 1):
         other = t + dt
@@ -431,20 +394,22 @@
         dst = pl.ds(8 + (dt + side) * bx2, bx2)
         for hh in range(heights):
             for m in range(bz2):
-                x = recv_ref[other * heights + hh, pl.ds(m * bx2 // 2, bx2 // 2)].reshape(bx2, LANES) * scale
+                x = recv_ref[pl.ds((other * heights + hh) * size + m * bx2, bx2), :] * scale
                 layer = 1 + hh * bz2 + m
                 b2[layer, dst, :] = jnp.where(lane == 3, 0.0, x)
                 s2[layer, dst, :] = jnp.where(
                     lane == 3, x, jnp.where(lane == 2, roll(x, -1), jnp.where(lane == 1, roll(x, -2), roll(x, -3)))
                 )
-        quarter = bx2 // 4
-        x = recv_ref[other * heights, pl.ds(bz2 * bx2 // 2, quarter // 2)].reshape(quarter, LANES) * scale
-        moved = {shift: roll(x, shift) if shift else x for shift in range(-3, 4)}
+        quarter = bx2 // 8
         small = lane_of(quarter) & 3
-        for j in range(4):
-            p2[1, pl.ds(8 + (dt + side) * bx2 + j, quarter, stride=4), :] = jnp.where(
-                small == 0, moved[-j], jnp.where(small == 1, moved[1 - j], jnp.where(small == 2, moved[2 - j], moved[3 - j]))
-            )
+        for hh in range(2):
+            x = recv_ref[pl.ds((other * heights + hh) * size + bz2 * bx2, quarter), :] * scale
+            moved = {shift: roll(x, shift) if shift else x for shift in range(-3, 4)}
+            for j in range(4):
+                row = 8 + (dt + side) * bx2 + hh * (bx2 // 2) + j
+                p2[1, pl.ds(row, quarter, stride=4), :] = jnp.where(
+                    small == 0, moved[-j], jnp.where(small == 1, moved[1 - j], jnp.where(small == 2, moved[2 - j], moved[3 - j]))
+                )
 
     def weights(count):
         kind = lane_of(count) & 3
@@ -536,8 +501,6 @@
 
     each(1, n2 + 1, post2, 8)
 
-    for copy in started[:5]:
-        copy.wait()
     kind = lane_of(bx2 + 4) & 3
 
     def lift1(m, carry):
@@ -550,12 +513,12 @@
             spread_rows(tmp.at[3 * m + c], part)
             lifted = tmp[3 * m + c, pl.ds(0, rows1), :]
             for i in range(2):
-                v1[c, 2 * m + i, mid, :] += lifted
-        return carry
-
-    each(0, n1 // 2, lift1, 8)
-
-    def post(s_ref, y_ref, g_ref, r_ref, v_ref, into, layer, to, row, count, step):
+                w1[c, 2 + 2 * m + i, mid, :] = v1[c, 2 + 2 * m + i, mid, :] + lifted
+        return carry
+
+    each(0, n1 // 2 - 2, lift1, 8)
+
+    def post(s_ref, y_ref, g_ref, r_ref, v_ref, into, layer, row, count, step):
         faces = all_faces(s_ref, y_ref, layer, row, count)
         for c in range(3):
             here, along = neighbours(v_ref.at[c], faces, layer, row, count, step)
@@ -566,33 +529,33 @@
         def into(c, value):
             f1[c, layer, mid, :] = value
 
-        post(s1, y1, g1, r1, v1, into, layer, layer, 8, rows1, 2)
-        return carry
-
-    each(1, n1 - 1, post1, 8)
-
-    for copy in started[5:]:
-        copy.wait()
-
-    for c in range(3):
-        for k in range(1, n1 - 1):
-            slot = 3 * (k - 1) + c
+        post(s1, y1, g1, r1, w1, into, layer, 8, rows1, 2)
+        return carry
+
+    each(3, n1 - 3, post1, 8)
+
+    for k in range(3, n1 - 3):
+        for c in range(3):
+            slot = 3 * (k - 3) + c
             spread_rows(tmp.at[slot], f1[c, k, mid, :])
             lifted = tmp[slot, pl.ds(0, bx + 16), :]
-            for i in (2 * k - 3, 2 * k - 2):
-                if 0 <= i < bz + 2:
-                    v0[c, i, near, :] += lifted
-
-    def post0(layer, carry):
+            for layer in (2 * k + 1, 2 * k + 2):
+                if HALO - 1 <= layer <= HALO + bz:
+                    w0[c, layer, near, :] = v0[c, layer, near, :] + lifted
+
+    started = []
+    for layer in range(HALO, HALO + bz):
+        z = layer - HALO
         for row, count in chunks(16, 16 + bx, 16):
 
             def into(c, value):
-                out_ref[c, layer - 1, pl.ds(row - 16, count), :] = value
-
-            post(s0, y0, g0, r0, v0, into, layer, layer, row, count, 1)
-        return carry
-
-    each(1, bz + 1, post0, 8)
+                done[c, z, pl.ds(row - 16, count), :] = value
+
+            post(s0, y0, g0, r0, w0, into, layer, row, count, 1)
+        started.append(pltpu.make_async_copy(done.at[:, z], out_ref.at[:, z], sem.at[z]))
+        started[-1].start()
+    for copy in started:
+        copy.wait()
 
 
 def swapped(x, axis, start):
@@ -608,7 +571,6 @@
     bz, bx, _ = material.shape
 
     held = pl.BlockSpec(memory_space=pltpu.VMEM)
-    anywhere = pl.BlockSpec(memory_space=pl.ANY)
     outside = pl.BlockSpec(memory_space=pltpu.HBM)
     own = pl.pallas_call(
         functools.partial(pack_kernel, bz, bx),
@@ -636,11 +598,6 @@
     nz, n1 = bz + 2 * HALO, bz // 2 + 8
     r0, r1 = bx + 32, bx1 + 24
     rows1 = bx1 + 8
-    kept = [
-        (bz + 2, bx + 16), (2, bz, bx), (3, bz + 2, bx + 16), (3, bz, bx), (3, bz, bx),
-        (n1 - 4, rows1), (2, n1 - 6, rows1), (3, n1 - 4, rows1), (3, n1 - 6, rows1), (3, n1 - 6, rows1),
-    ]
-    kept = [jax.ShapeDtypeStruct((*shape, LANES), F32) for shape in kept]
     field0, field1 = (nz, r0, LANES), (n1, r1, LANES)
     fields = [field0, field0, (3, *field0), (3, *field0), (3, *field0), (3, *field0), (3, *field0), (2, *field0), (3, *field0)]
     fields = [pltpu.VMEM(shape, F32) for shape in [*fields, (n1 - 2, 3, r0, LANES)]]
@@ -653,44 +610,41 @@
         cost_estimate=pl.CostEstimate(flops=work * 60, bytes_accessed=work * 40, transcendentals=0),
         compiler_params=pltpu.CompilerParams(vmem_limit_bytes=4 * 2**20),
     )(bricks, near)
-    send, *saved = pl.pallas_call(
+    kept = [field1, (2, *field1), (3, *field1), (3, *field1), (3, *field1)]
+    kept = [pltpu.VMEM(shape, F32) for shape in kept]
+    send, s1, y1, v1, g1, r1_, s, _, _, _, r, _, g, y, v, _ = pl.pallas_call(
         functools.partial(down_kernel, heights, tiles, bz, bx),
         out_shape=[
-            jax.ShapeDtypeStruct((heights * tiles, (bz // 4 * bx2 + bx2 // 4) // 2, 2, LANES), F32), *kept, *fields
+            pltpu.VMEM((heights * tiles * (bz // 4 * bx2 + bx2 // 8), LANES), F32), *kept, *fields
         ],
         in_specs=[held] * (2 + len(fields)),
-        out_specs=[held] + [anywhere] * len(kept) + [held] * len(fields),
+        out_specs=[held] * (1 + len(kept) + len(fields)),
         input_output_aliases={2 + k: 1 + len(kept) + k for k in range(len(fields))},
-        scratch_shapes=[
-            vmem(n1 - 2, 3, r0, LANES),
-            vmem(*field1), vmem(*field1), vmem(3, *field1), vmem(3, *field1), vmem(3, *field1), vmem(3, *field1),
-            vmem(2, *field1), vmem(3, *field1), pltpu.SemaphoreType.DMA((10,)),
-        ],
-        compiler_params=pltpu.CompilerParams(vmem_limit_bytes=12 * 2**20),
+        scratch_shapes=[vmem(n1 - 2, 3, r0, LANES), vmem(*field1), vmem(3, *field1), vmem(3, *field1)],
+        compiler_params=pltpu.CompilerParams(vmem_limit_bytes=8 * 2**20),
     )(bricks, far, *inner)
-    saved = saved[: len(kept)]
-
-    received = lax.all_to_all(send, ("tile", "height"), 0, 0)
+
+    blocks = send.reshape(heights * tiles, -1, 1, LANES)
+    received = lax.all_to_all(blocks, ("tile", "height"), 0, 0).reshape(send.shape)
 
     rows2 = bx2 + 2 * REACH
     rows3 = -(-(rows2 // 2) // 8) * 8
-    up0, up1 = (bz + 2, r0, LANES), (n1 - 4, r1, LANES)
     up2 = (heights * bz // 4 + 2, rows2 + 16, LANES)
     up3 = (heights * bz // 8 + 2, rows3 + 16, LANES)
     return pl.pallas_call(
         functools.partial(up_kernel, heights, tiles, bz, bx),
         out_shape=jax.ShapeDtypeStruct((3, bz, bx, LANES), F32),
-        in_specs=[held] + [anywhere] * len(kept),
-        out_specs=held,
+        in_specs=[held] * 11,
+        out_specs=outside,
         scratch_shapes=[
-            vmem(*up0), vmem(2, *up0), vmem(3, *up0), vmem(3, *up0), vmem(3, *up0),
-            vmem(*up1), vmem(2, *up1), vmem(3, *up1), vmem(3, *up1), vmem(3, *up1), vmem(3, *up1),
+            vmem(3, *field0), vmem(3, *field1), vmem(3, *field1),
             vmem(*up2), vmem(*up2), vmem(*up2), vmem(6, *up2), vmem(*up2), vmem(*up2), vmem(*up2), vmem(*up2), vmem(*up2),
             vmem(*up3), vmem(*up3), vmem(*up3), vmem(6, *up3), vmem(*up3), vmem(*up3), vmem(*up3), vmem(*up3),
-            vmem(heights * bz // 8, rows2 + 24, LANES), vmem(max(heights * bz // 4, 3 * (n1 - 6)), r0, LANES), pltpu.SemaphoreType.DMA((10,)),
+            vmem(heights * bz // 8, rows2 + 24, LANES), vmem(max(heights * bz // 4, 3 * (n1 - 6)), r0, LANES),
+            vmem(3, bz, bx, LANES), pltpu.SemaphoreType.DMA((bz,)),
         ],
         compiler_params=pltpu.CompilerParams(vmem_limit_bytes=16 * 2**20),
-    )(received, *saved)
+    )(received, s, y, v, g, r, s1, y1, v1, g1, r1_)
 
 
 def solution(mesh):

time: 41 us -> 40.5 us (0.988)
  no operation moved by 1% of the time
where the time goes in v5:
time: 40.5 us; the launch traced here: 40.4 us
  blocking collectives  25.9 us (64%)
  Pallas kernels  9.58 us (24%)
  waiting for transfers between devices  2.64 us (7%)
  starting transfers between devices  2.21 us (5%)
    all_to_all x1, blocking collectives, local(): lax.all_to_all(blocks, ('tile', 'height'), 0, 0).reshape(send.shape)  16.4 us
    all_gather x1, blocking collectives, local(): bricks = lax.all_gather(own, 'height')  9.45 us
    pallas_call x1, Pallas kernels, local(): pl.pallas_call(functools.partial(inner_kernel, heights, tiles, bz, bx), o...  2.93 us
    pallas_call x1, Pallas kernels, local(): pl.pallas_call(functools.partial(up_kernel, heights, tiles, bz, bx), out_...  2.89 us
    pallas_call x1, Pallas kernels, local(): pl.pallas_call(functools.partial(down_kernel, heights, tiles, bz, bx), ou...  2.69 us
    ppermute x2, waiting for transfers between devices, swapped(): return lax.ppermute(x, axis, pairs + [(j, i) for i, j in pairs])  2.64 us
    ppermute x2, starting transfers between devices, swapped(): return lax.ppermute(x, axis, pairs + [(j, i) for i, j in pairs])  2.21 us
    pallas_call x1, Pallas kernels, local(): pl.pallas_call(functools.partial(pack_kernel, bz, bx), out_shape=pltpu.VM...  0.97 us
  transfers between devices with their start and end apart: 2, of which 1 were waited for; matrix products, arithmetic and copies ran while one was open for 0% of the time, Pallas kernels for 7%

profile of v5, /device:TPU:0, one launch (start us, length us, event | category | flops | bytes accessed | tf_op | source)
XLA Modules:
  0.0 40.4 jit_solution(1583008435115023611)
XLA Ops:
  0.0 1.0 %shard_map.46 = f32[324,128]{1,0:T(8,128)S(1)} custom-call(s32[8,32,128]{2,1,0:T(8,128)} %material_ref.1, s32[8,32,128]{2,1,0:T(8,128)} %clamped_ref.1, f32[3]{0:T(128)} %table_ref.1, f32[3,3]{1,0:T(4,128)} %strain_ref.1), custom_call_target="tpu_custom_call" | custom-call | tf_op jit(solution)/shard_map/pallas_call | solution.py:575
  1.0 9.4 %all-gather.1.x_ref = f32[4,324,128]{2,1,0:T(8,128)S(1)} all-gather(f32[1,324,128]{2,1,0:T(8,128)S(1)} %bitcast.4), channel_id=2, replica_groups=mesh['tile'=8,'height'=4] {'height'}, dimensions={0}, use_global_device_ids=true | all-gather | bytes 829440 | tf_op jit(solution)/shard_map/all_gather | solution.py:585
  10.4 0.1 shard_map.47
  10.5 1.6 %collective-permute-start.1 = (f32[168,128]{1,0:T(8,128)S(1)}, f32[168,128]{1,0:T(8,128)S(1)}, u32[]{:S(2)}, u32[]{:S(2)}) collective-permute-start(f32[168,128]{1,0:T(8,128)S(1)} %get-tuple-element.29), channel_id=1, source_target_pairs={{0,4},{8,12},{16,20},{24,28},{4,0},{12,8},{20,16},{28,24},{1,5},{9... | collective-permute-start | bytes 258056 | tf_op jit(solution)/shard_map/ppermute | solution.py:563
  12.1 0.7 %collective-permute-start = (f32[168,128]{1,0:T(8,128)S(1)}, f32[168,128]{1,0:T(8,128)S(1)}, u32[]{:S(2)}, u32[]{:S(2)}) collective-permute-start(f32[168,128]{1,0:T(8,128)S(1)} %get-tuple-element.28), channel_id=1, source_target_pairs={{4,8},{12,16},{20,24},{8,4},{16,12},{24,20},{5,9},{13,17},{21,25},... | collective-permute-start | bytes 258056 | tf_op jit(solution)/shard_map/ppermute | solution.py:563
  12.8 2.6 %collective-permute-done.1.near_ref = f32[168,128]{1,0:T(8,128)S(1)} collective-permute-done((f32[168,128]{1,0:T(8,128)S(1)}, f32[168,128]{1,0:T(8,128)S(1)}, u32[]{:S(2)}, u32[]{:S(2)}) %collective-permute-start.1) | collective-permute-done | bytes 86048 | tf_op jit(solution)/shard_map/ppermute | solution.py:563
  15.4 2.9 %shard_map.48 = (f32[26,64,128]{2,1,0:T(8,128)S(1)}, f32[26,64,128]{2,1,0:T(8,128)S(1)}, f32[3,26,64,128]{3,2,1,0:T(8,128)S(1)}, f32[3,26,64,128]{3,2,1,0:T(8,12...) custom-call(f32[4,324,128]{2,1,0:T(8,128)S(1)} %all-gather.1.x_ref, ...), custom_call_target="tpu_custom_call" | custom-call | flops 26542080 | bytes 17694720 | tf_op jit(solution)/shard_map/pallas_call | solution.py:605
  18.3 0.0 collective-permute-done.far_ref
  18.3 2.7 %shard_map.49 = (f32[544,128]{1,0:T(8,128)S(1)}, f32[12,40,128]{2,1,0:T(8,128)S(1)}, f32[2,12,40,128]{3,2,1,0:T(8,128)S(1)}, f32[3,12,40,128]{3,2,1,0:T(8,128)S(...) custom-call(f32[4,324,128]{2,1,0:T(8,128)S(1)} %all-gather.1.x_ref, ...), custom_call_target="tpu_custom_call", output_to_operand_aliasing={{6}: (2, {}), {7}: (3, {}), {8}: (4, {}), {9}: (5, {}), {10... | custom-call | tf_op jit(solution)/shard_map/pallas_call | solution.py:615
  21.0 16.4 %all_to_all.5 = f32[32,17,1,128]{3,2,1,0:T(1,128)S(1)} all-to-all(f32[32,17,1,128]{3,2,1,0:T(1,128)S(1)} %bitcast.5), channel_id=1, replica_groups=mesh['tile'=8,'height'=4] {'tile','height'}, dimensions={0} | all-to-all | bytes 557056 | tf_op jit(solution)/shard_map/all_to_all | solution.py:628
  37.5 2.9 %shard_map.50 = f32[3,8,32,128]{3,2,1,0:T(8,128)} custom-call(f32[544,128]{1,0:T(8,128)S(1)} %bitcast.3, f32[26,64,128]{2,1,0:T(8,128)S(1)} %get-tuple-element.41.s0, f32[2,26,64,128]{3,2,1,0:T(8,128)S(1)} %get-tuple-element.42.y0, f32[3,26,64,128]{3,2,1,0:T(8,128)S(1)} %get-tuple-element.43.v0, f32[3,26,64,128]{3,2,1,0:T(8,128)S(1)} %get-tuple-element.44.g0, ...), custom_call_target="tpu_custom_call" | custom-call | tf_op jit(solution)/shard_map/pallas_call | solution.py:634
Async XLA Ops:
  10.5 4.9 %collective-permute-start.1 = (f32[168,128]{1,0:T(8,128)S(1)}, f32[168,128]{1,0:T(8,128)S(1)}, u32[]{:S(2)}, u32[]{:S(2)}) collective-permute-start(f32[168,128]{1,0:T(8,128)S(1)} %get-tuple-element.29), channel_id=1, source_target_pairs={{0,4},{8,12},{16,20},{24,28},{4,0},{12,8},{20,16},{28,24},{1,5},{9... | collective-permute-start | bytes 258056 | tf_op jit(solution)/shard_map/ppermute | solution.py:563
  12.1 6.2 %collective-permute-start = (f32[168,128]{1,0:T(8,128)S(1)}, f32[168,128]{1,0:T(8,128)S(1)}, u32[]{:S(2)}, u32[]{:S(2)}) collective-permute-start(f32[168,128]{1,0:T(8,128)S(1)} %get-tuple-element.28), channel_id=1, source_target_pairs={{4,8},{12,16},{20,24},{8,4},{16,12},{24,20},{5,9},{13,17},{21,25},... | collective-permute-start | bytes 258056 | tf_op jit(solution)/shard_map/ppermute | solution.py:563

commit v6 on v5

--- a/solution.py
+++ b/solution.py
@@ -114,7 +114,7 @@
         rate = safe_rate(here, doubled)
         d_ref[c, layer, pl.ds(row, count), :] = doubled
         r_ref[c, layer, pl.ds(row, count), :] = rate
-        g_ref[c, layer, pl.ds(row, count), :] = (2.0 * rate) * b_of(c)
+        g_ref[c, layer, pl.ds(row, count), :] = rate * b_of(c)
 
 
 def all_faces(s_ref, y_ref, layer, row, count):
@@ -140,7 +140,7 @@
         here, along = neighbours(v_ref.at[c], faces, layer, row, count, step)
         doubled = d_ref[c, layer, pl.ds(row, count), :]
         source = b_ref[c, layer, pl.ds(row, count), :]
-        result.append(source + 0.5 * (total(along, c) - doubled * here))
+        result.append(source + (total(along, c) - doubled * here))
     return result
 
 
@@ -150,7 +150,9 @@
     return counts, starts, sum(counts)
 
 
-def pack_kernel(bz, bx, material_ref, clamped_ref, table_ref, strain_ref, own_ref, label, joined, table, strain, sem):
+def pack_kernel(
+    heights, bz, bx, material_ref, clamped_ref, table_ref, strain_ref, own_ref, brick_ref, edge_ref, label, joined, table, strain, sem
+):
     copies = [
         pltpu.make_async_copy(material_ref, label, sem.at[0]),
         pltpu.make_async_copy(clamped_ref.at[pl.ds(0, 2)], joined, sem.at[1]),
@@ -163,7 +165,12 @@
         copy.wait()
     for slot in range(bz + 2):
         src = label.at[slot] if slot < bz else joined.at[slot - bz]
-        own_ref[pl.ds(slot * bx, bx), :] = src[...].astype(F32)
+        value = src[...].astype(F32)
+        own_ref[pl.ds(slot * bx, bx), :] = value
+        if slot < bz:
+            brick_ref[pl.ds(slot * bx, bx), :] = value
+    lower = lax.axis_index("height") < heights // 2
+    edge_ref[...] = jnp.where(lower, label[bz - 1], label[0]).astype(F32)
     lane = lane_of(SPARE)
     row = jnp.zeros((SPARE, LANES), F32)
     for k in range(3):
@@ -173,27 +180,42 @@
     own_ref[pl.ds((bz + 2) * bx, SPARE), :] = row
 
 
-def place(heights, bz, layer):
-    z = bz * lax.axis_index("height") - HALO + layer
+def gathered_rows(bz, bx):
+    whole, brick = (bz + 2) * bx + SPARE, bz * bx
+    return [0, whole, 2 * whole, 2 * whole + brick]
+
+
+def place(heights, bz, bx, layer):
+    h = lax.axis_index("height")
+    z = bz * h - HALO + layer
     z_in = jnp.clip(z, 0, heights * bz - 1)
-    return z, z_in // bz, z_in % bz
+    brick, slot = z_in // bz, z_in % bz
+    starts = gathered_rows(bz, bx)
+    apart = jnp.abs(brick - h)
+    paired = (brick // 2) == (h // 2)
+    inner = jnp.where(apart == 0, starts[0], jnp.where(paired, starts[1], starts[2])) + slot * bx
+    return z, jnp.where(apart > 1, starts[3], inner)
+
+
+def spring_row(bz, bx):
+    return jnp.where(lax.axis_index("height") == 0, 0, gathered_rows(bz, bx)[1]) + bz * bx
 
 
 def strip_kernel(heights, bz, bx, x_ref, near_ref, far_ref):
     odd = (lax.axis_index("tile") & 1) == 1
     counts, starts, end = strips(bz)
-    wanted = [(place(heights, bz, layer)[1:], count, start) for layer, (count, start) in enumerate(zip(counts, starts))]
-    wanted += [((0, bz + k), HALO, end + HALO * k) for k in range(2)]
-    for (brick, slot), count, start in wanted:
+    wanted = [(place(heights, bz, bx, layer)[1], count, start) for layer, (count, start) in enumerate(zip(counts, starts))]
+    wanted += [(spring_row(bz, bx) + bx * k, HALO, end + HALO * k) for k in range(2)]
+    for row, count, start in wanted:
         if count:
-            first = x_ref[brick, pl.ds(slot * bx, count), :]
-            last = x_ref[brick, pl.ds(slot * bx + bx - count, count), :]
+            first = x_ref[pl.ds(row, count), :]
+            last = x_ref[pl.ds(row + bx - count, count), :]
             near_ref[pl.ds(start, count), :] = jnp.where(odd, first, last)
             far_ref[pl.ds(start, count), :] = jnp.where(odd, last, first)
 
 
 def tables_of(x_ref, row):
-    spare = x_ref[0, pl.ds(row, 1), :]
+    spare = x_ref[pl.ds(row, 1), :]
     table = [jnp.broadcast_to(spare[:, k : k + 1], (1, LANES)) for k in range(12)]
     return table[:3], [table[3 + 3 * c : 6 + 3 * c] for c in range(3)]
 
@@ -208,7 +230,7 @@
 
 def store_strip(s, st, p, strip_ref, heights, bz, layer, far_side, valid, bx, tables):
     counts, starts, end = strips(bz)
-    z, _, _ = place(heights, bz, layer)
+    z, _ = place(heights, bz, bx, layer)
     weight = jnp.where((z >= 0) & (z < heights * bz), valid, 0.0)
     count = counts[layer]
     if count:
@@ -223,9 +245,9 @@
     lane = lane_of(count)
     here = st[2, layer, pl.ds(row, count), :]
     source = [
-        0.5 * (rows_at(st.at[0], layer - 1, row, count) - rows_at(st.at[0], layer + 1, row, count)),
-        0.5 * (rows_at(st.at[1], layer, row - 1, count) - rows_at(st.at[1], layer, row + 1, count)),
-        0.5 * (jnp.where(lane < 1, 0.0, roll(here, 1)) - jnp.where(lane >= LANES - 1, 0.0, roll(here, -1))),
+        (rows_at(st.at[0], layer - 1, row, count) - rows_at(st.at[0], layer + 1, row, count)),
+        (rows_at(st.at[1], layer, row - 1, count) - rows_at(st.at[1], layer, row + 1, count)),
+        (jnp.where(lane < 1, 0.0, roll(here, 1)) - jnp.where(lane >= LANES - 1, 0.0, roll(here, -1))),
     ]
     for c in range(3):
         b[c, layer, pl.ds(row, count), :] = source[c]
@@ -266,11 +288,11 @@
     valid = jnp.where(odd | (t < tiles - 1), 1.0, 0.0)
 
     def read_layer(layer, carry):
-        z, brick, slot = place(heights, bz, layer)
+        z, row = place(heights, bz, bx, layer)
         inside = jnp.where((z >= 0) & (z < heights * bz), 1.0, 0.0)
-        store_layer(s, st, x_ref[brick, pl.ds(slot * bx, bx), :], layer, 16, inside, tables)
+        store_layer(s, st, x_ref[pl.ds(row, bx), :], layer, 16, inside, tables)
         bottom = jnp.where((z >= 0) & (z < 2), 2.0 * PENALTY, 0.0)
-        p[layer, pl.ds(16, bx), :] = x_ref[0, pl.ds((bz + jnp.clip(z, 0, 1)) * bx, bx), :] * bottom
+        p[layer, pl.ds(16, bx), :] = x_ref[pl.ds(spring_row(bz, bx) + jnp.clip(z, 0, 1) * bx, bx), :] * bottom
         store_strip(s, st, p, near_ref, heights, bz, layer, jnp.logical_not(odd), valid, bx, tables)
         return carry
 
@@ -431,7 +453,7 @@
         r_ref[layer, dst, :] = rate
         if d_ref is not None:
             d_ref[layer, dst, :] = doubled
-        g_ref[layer, dst, :] = (2.0 * rate) * rows_at(b_ref, layer, row, count)
+        g_ref[layer, dst, :] = rate * rows_at(b_ref, layer, row, count)
 
     def packed_sum(v_ref, q_ref, layer, row, count, step):
         faces = [q_ref[k, layer, pl.ds(row, count), :] for k in range(6)]
@@ -460,7 +482,7 @@
         for i in range(2):
             layer = 1 + 2 * j + i
             here, total_ = packed_sum(v2, q2, layer, 8, rows2, 4)
-            rest = rest + rows_at(b2, layer, 8, rows2) + 0.5 * (total_ - rows_at(d2, layer, 8, rows2) * here)
+            rest = rest + rows_at(b2, layer, 8, rows2) + (total_ - rows_at(d2, layer, 8, rows2) * here)
         rest2[j, pl.ds(8, rows2), :] = rest
         dst = pl.ds(8, rows3)
         b3[j + 1, dst, :] = pair_lanes(pair_rows(rest2.at[j], 8, rows3), 4)
@@ -572,17 +594,20 @@
 
     held = pl.BlockSpec(memory_space=pltpu.VMEM)
     outside = pl.BlockSpec(memory_space=pltpu.HBM)
-    own = pl.pallas_call(
-        functools.partial(pack_kernel, bz, bx),
-        out_shape=pltpu.VMEM(((bz + 2) * bx + SPARE, LANES), F32),
+    own, brick, edge = pl.pallas_call(
+        functools.partial(pack_kernel, heights, bz, bx),
+        out_shape=[pltpu.VMEM((rows, LANES), F32) for rows in ((bz + 2) * bx + SPARE, bz * bx, bx)],
         in_specs=[outside] * 4,
-        out_specs=held,
+        out_specs=[held] * 3,
         scratch_shapes=[
             pltpu.VMEM((bz, bx, LANES), jnp.int32), pltpu.VMEM((2, bx, LANES), jnp.int32),
             pltpu.SMEM((3,), F32), pltpu.SMEM((3, 3), F32), pltpu.SemaphoreType.DMA((4,)),
         ],
     )(material, clamped, stiffness_table, eigenstrain)
-    bricks = lax.all_gather(own, "height")
+    beside = swapped(brick, "height", 1)
+    beyond = lax.ppermute(edge, "height", [(i, (i + 2) % heights) for i in range(heights)])
+    paired = swapped(own, "height", 0)
+    bricks = jnp.concatenate([own, paired, beside, beyond], 0)
     strip = pltpu.VMEM((-(-(strips(bz)[2] + 2 * HALO) // 8) * 8, LANES), F32)
     near, far = pl.pallas_call(
         functools.partial(strip_kernel, heights, bz, bx),

time: 40.5 us -> 39.7 us (0.980)
  blocking collectives: 25.9 us -> 16.8 us
  starting transfers between devices: 2.21 us -> 7.83 us
  waiting for transfers between devices: 2.64 us -> 5.02 us
    all_gather x1 -> x0, blocking collectives: 9.45 us -> none  [local(): bricks = lax.all_gather(own, 'height')]
    ppermute x0 -> x1, starting transfers between devices: none -> 3.86 us  [local(): lax.ppermute(edge, 'height', [(i, (i + 2) % heights) for i in range(heigh...]
    ppermute x0 -> x1, waiting for transfers between devices: none -> 3.2 us  [local(): lax.ppermute(edge, 'height', [(i, (i + 2) % heights) for i in range(heigh...]
    ppermute x2 -> x4, starting transfers between devices: 2.21 us -> 3.97 us  [swapped(): return lax.ppermute(x, axis, pairs + [(j, i) for i, j in pairs])]
    ppermute x2 -> x4, waiting for transfers between devices: 2.64 us -> 1.81 us  [swapped(): return lax.ppermute(x, axis, pairs + [(j, i) for i, j in pairs])]
  transfers between devices with their start and end apart: 2 -> 5, of which waited for: 1 -> 2; matrix products, arithmetic and copies ran while one was open for 0% -> 0% of each run, Pallas kernels for 7% -> 8%
where the time goes in v6:
time: 39.7 us; the launch traced here: 39.5 us
  blocking collectives  16.8 us (42%)
  Pallas kernels  9.76 us (25%)
  starting transfers between devices  7.83 us (20%)
  waiting for transfers between devices  5.02 us (13%)
    all_to_all x1, blocking collectives, local(): lax.all_to_all(blocks, ('tile', 'height'), 0, 0).reshape(send.shape)  16.8 us
    ppermute x4, starting transfers between devices, swapped(): return lax.ppermute(x, axis, pairs + [(j, i) for i, j in pairs])  3.97 us
    ppermute x1, starting transfers between devices, local(): lax.ppermute(edge, 'height', [(i, (i + 2) % heights) for i in range(heigh...  3.86 us
    ppermute x1, waiting for transfers between devices, local(): lax.ppermute(edge, 'height', [(i, (i + 2) % heights) for i in range(heigh...  3.2 us
    pallas_call x1, Pallas kernels, local(): pl.pallas_call(functools.partial(inner_kernel, heights, tiles, bz, bx), o...  3 us
    pallas_call x1, Pallas kernels, local(): pl.pallas_call(functools.partial(up_kernel, heights, tiles, bz, bx), out_...  2.9 us
    pallas_call x1, Pallas kernels, local(): pl.pallas_call(functools.partial(down_kernel, heights, tiles, bz, bx), ou...  2.58 us
    ppermute x4, waiting for transfers between devices, swapped(): return lax.ppermute(x, axis, pairs + [(j, i) for i, j in pairs])  1.81 us
  transfers between devices with their start and end apart: 5, of which 2 were waited for; matrix products, arithmetic and copies ran while one was open for 0% of the time, Pallas kernels for 8%

profile of v6, /device:TPU:0, one launch (start us, length us, event | category | flops | bytes accessed | tf_op | source)
XLA Modules:
  0.0 39.5 jit_solution(2556590827093398)
XLA Ops:
  0.0 1.0 %shard_map.46 = (f32[324,128]{1,0:T(8,128)S(1)}, f32[256,128]{1,0:T(8,128)S(1)}, f32[32,128]{1,0:T(8,128)S(1)}) custom-call(s32[8,32,128]{2,1,0:T(8,128)} %material_ref.1, s32[8,32,128]{2,1,0:T(8,128)} %clamped_ref.1, f32[3]{0:T(128)} %table_ref.1, f32[3,3]{1,0:T(4,128)} %strain_ref.1), custom_call_target="tpu_custom_call" | custom-call | tf_op jit(solution)/shard_map/pallas_call | solution.py:597
  1.0 0.5 %collective-permute-start = (f32[324,128]{1,0:T(8,128)S(1)}, f32[324,128]{1,0:T(8,128)S(1)}, u32[]{:S(2)}, u32[]{:S(2)}) collective-permute-start(f32[324,128]{1,0:T(8,128)S(1)} %get-tuple-element.31), channel_id=1, source_target_pairs={{0,1},{2,3},{1,0},{3,2},{4,5},{6,7},{5,4},{7,6},{8,9},{10,11},{9,8... | collective-permute-start | bytes 497672 | tf_op jit(solution)/shard_map/ppermute | solution.py:585
  1.5 0.7 %collective-permute-start.1 = (f32[256,128]{1,0:T(8,128)S(1)}, f32[256,128]{1,0:T(8,128)S(1)}, u32[]{:S(2)}, u32[]{:S(2)}) collective-permute-start(f32[256,128]{1,0:T(8,128)S(1)} %get-tuple-element.32), channel_id=1, source_target_pairs={{1,2},{2,1},{5,6},{6,5},{9,10},{10,9},{13,14},{14,13},{17,18},{18,... | collective-permute-start | bytes 393224 | tf_op jit(solution)/shard_map/ppermute | solution.py:585
  2.2 3.9 %collective-permute-start.2 = (f32[32,128]{1,0:T(8,128)S(1)}, f32[32,128]{1,0:T(8,128)S(1)}, u32[]{:S(2)}, u32[]{:S(2)}) collective-permute-start(f32[32,128]{1,0:T(8,128)S(1)} %get-tuple-element.33), channel_id=1, source_target_pairs={{0,2},{1,3},{2,0},{3,1},{4,6},{5,7},{6,4},{7,5},{8,10},{9,11},{10,... | collective-permute-start | bytes 49160 | tf_op jit(solution)/shard_map/ppermute | solution.py:608
  6.0 3.2 %collective-permute-done.2 = f32[32,128]{1,0:T(8,128)S(1)} collective-permute-done((f32[32,128]{1,0:T(8,128)S(1)}, f32[32,128]{1,0:T(8,128)S(1)}, u32[]{:S(2)}, u32[]{:S(2)}) %collective-permute-start.2) | collective-permute-done | bytes 16416 | tf_op jit(solution)/shard_map/ppermute | solution.py:608
  9.2 0.0 collective-permute-done.1
  9.2 0.0 collective-permute-done
  9.3 0.3 shard_map.47
  9.6 2.1 %collective-permute-start.4 = (f32[168,128]{1,0:T(8,128)S(1)}, f32[168,128]{1,0:T(8,128)S(1)}, u32[]{:S(2)}, u32[]{:S(2)}) collective-permute-start(f32[168,128]{1,0:T(8,128)S(1)} %get-tuple-element.35), channel_id=1, source_target_pairs={{0,4},{8,12},{16,20},{24,28},{4,0},{12,8},{20,16},{28,24},{1,5},{9... | collective-permute-start | bytes 258056 | tf_op jit(solution)/shard_map/ppermute | solution.py:585
  11.7 0.7 %collective-permute-start.3 = (f32[168,128]{1,0:T(8,128)S(1)}, f32[168,128]{1,0:T(8,128)S(1)}, u32[]{:S(2)}, u32[]{:S(2)}) collective-permute-start(f32[168,128]{1,0:T(8,128)S(1)} %get-tuple-element.34), channel_id=1, source_target_pairs={{4,8},{12,16},{20,24},{8,4},{16,12},{24,20},{5,9},{13,17},{21,25},... | collective-permute-start | bytes 258056 | tf_op jit(solution)/shard_map/ppermute | solution.py:585
  12.4 1.8 %collective-permute-done.4.near_ref = f32[168,128]{1,0:T(8,128)S(1)} collective-permute-done((f32[168,128]{1,0:T(8,128)S(1)}, f32[168,128]{1,0:T(8,128)S(1)}, u32[]{:S(2)}, u32[]{:S(2)}) %collective-permute-start.4) | collective-permute-done | bytes 86048 | tf_op jit(solution)/shard_map/ppermute | solution.py:585
  14.2 3.0 %shard_map.48 = (f32[26,64,128]{2,1,0:T(8,128)S(1)}, f32[26,64,128]{2,1,0:T(8,128)S(1)}, f32[3,26,64,128]{3,2,1,0:T(8,128)S(1)}, f32[3,26,64,128]{3,2,1,0:T(8,12...) custom-call(f32[936,128]{1,0:T(8,128)S(1)} %pad_maximum_fusion.x_ref, ...), custom_call_target="tpu_custom_call" | custom-call | flops 26542080 | bytes 17694720 | tf_op jit(solution)/shard_map/pallas_call | solution.py:630
  17.2 0.0 collective-permute-done.3.far_ref
  17.2 2.6 %shard_map.49 = (f32[544,128]{1,0:T(8,128)S(1)}, f32[12,40,128]{2,1,0:T(8,128)S(1)}, f32[2,12,40,128]{3,2,1,0:T(8,128)S(1)}, f32[3,12,40,128]{3,2,1,0:T(8,128)S(...) custom-call(f32[936,128]{1,0:T(8,128)S(1)} %pad_maximum_fusion.x_ref, ...), custom_call_target="tpu_custom_call", output_to_operand_aliasing={{6}: (2, {}), {7}: (3, {}), {8}: (4, {}), {9}: (5, {}), {10... | custom-call | tf_op jit(solution)/shard_map/pallas_call | solution.py:640
  19.8 16.8 %all_to_all.5 = f32[32,17,1,128]{3,2,1,0:T(1,128)S(1)} all-to-all(f32[32,17,1,128]{3,2,1,0:T(1,128)S(1)} %bitcast.3), channel_id=1, replica_groups=mesh['tile'=8,'height'=4] {'tile','height'}, dimensions={0} | all-to-all | bytes 557056 | tf_op jit(solution)/shard_map/all_to_all | solution.py:653
  36.6 2.9 %shard_map.50 = f32[3,8,32,128]{3,2,1,0:T(8,128)} custom-call(f32[544,128]{1,0:T(8,128)S(1)} %bitcast.2, f32[26,64,128]{2,1,0:T(8,128)S(1)} %get-tuple-element.47.s0, f32[2,26,64,128]{3,2,1,0:T(8,128)S(1)} %get-tuple-element.48.y0, f32[3,26,64,128]{3,2,1,0:T(8,128)S(1)} %get-tuple-element.49.v0, f32[3,26,64,128]{3,2,1,0:T(8,128)S(1)} %get-tuple-element.50.g0, ...), custom_call_target="tpu_custom_call" | custom-call | tf_op jit(solution)/shard_map/pallas_call | solution.py:659
  (1 shorter events, 0.0 us)
Async XLA Ops:
  1.0 8.3 %collective-permute-start = (f32[324,128]{1,0:T(8,128)S(1)}, f32[324,128]{1,0:T(8,128)S(1)}, u32[]{:S(2)}, u32[]{:S(2)}) collective-permute-start(f32[324,128]{1,0:T(8,128)S(1)} %get-tuple-element.31), channel_id=1, source_target_pairs={{0,1},{2,3},{1,0},{3,2},{4,5},{6,7},{5,4},{7,6},{8,9},{10,11},{9,8... | collective-permute-start | bytes 497672 | tf_op jit(solution)/shard_map/ppermute | solution.py:585
  1.5 7.7 %collective-permute-start.1 = (f32[256,128]{1,0:T(8,128)S(1)}, f32[256,128]{1,0:T(8,128)S(1)}, u32[]{:S(2)}, u32[]{:S(2)}) collective-permute-start(f32[256,128]{1,0:T(8,128)S(1)} %get-tuple-element.32), channel_id=1, source_target_pairs={{1,2},{2,1},{5,6},{6,5},{9,10},{10,9},{13,14},{14,13},{17,18},{18,... | collective-permute-start | bytes 393224 | tf_op jit(solution)/shard_map/ppermute | solution.py:585
  2.2 7.1 %collective-permute-start.2 = (f32[32,128]{1,0:T(8,128)S(1)}, f32[32,128]{1,0:T(8,128)S(1)}, u32[]{:S(2)}, u32[]{:S(2)}) collective-permute-start(f32[32,128]{1,0:T(8,128)S(1)} %get-tuple-element.33), channel_id=1, source_target_pairs={{0,2},{1,3},{2,0},{3,1},{4,6},{5,7},{6,4},{7,5},{8,10},{9,11},{10,... | collective-permute-start | bytes 49160 | tf_op jit(solution)/shard_map/ppermute | solution.py:608
  9.6 4.6 %collective-permute-start.4 = (f32[168,128]{1,0:T(8,128)S(1)}, f32[168,128]{1,0:T(8,128)S(1)}, u32[]{:S(2)}, u32[]{:S(2)}) collective-permute-start(f32[168,128]{1,0:T(8,128)S(1)} %get-tuple-element.35), channel_id=1, source_target_pairs={{0,4},{8,12},{16,20},{24,28},{4,0},{12,8},{20,16},{28,24},{1,5},{9... | collective-permute-start | bytes 258056 | tf_op jit(solution)/shard_map/ppermute | solution.py:585
  11.7 5.5 %collective-permute-start.3 = (f32[168,128]{1,0:T(8,128)S(1)}, f32[168,128]{1,0:T(8,128)S(1)}, u32[]{:S(2)}, u32[]{:S(2)}) collective-permute-start(f32[168,128]{1,0:T(8,128)S(1)} %get-tuple-element.34), channel_id=1, source_target_pairs={{4,8},{12,16},{20,24},{8,4},{16,12},{24,20},{5,9},{13,17},{21,25},... | collective-permute-start | bytes 258056 | tf_op jit(solution)/shard_map/ppermute | solution.py:585

commit v7 on v6

--- a/solution.py
+++ b/solution.py
@@ -185,16 +185,19 @@
     return [0, whole, 2 * whole, 2 * whole + brick]
 
 
-def place(heights, bz, bx, layer):
+def place(bz, bx, layer):
     h = lax.axis_index("height")
-    z = bz * h - HALO + layer
-    z_in = jnp.clip(z, 0, heights * bz - 1)
-    brick, slot = z_in // bz, z_in % bz
-    starts = gathered_rows(bz, bx)
-    apart = jnp.abs(brick - h)
-    paired = (brick // 2) == (h // 2)
-    inner = jnp.where(apart == 0, starts[0], jnp.where(paired, starts[1], starts[2])) + slot * bx
-    return z, jnp.where(apart > 1, starts[3], inner)
+    own, paired, beside, beyond = gathered_rows(bz, bx)
+    even = (h & 1) == 0
+    if layer in (0, bz + 2 * HALO - 1):
+        row = beyond
+    elif layer < HALO:
+        row = jnp.where(even, beside, paired) + (bz - HALO + layer) * bx
+    elif layer < HALO + bz:
+        row = own + (layer - HALO) * bx
+    else:
+        row = jnp.where(even, paired, beside) + (layer - HALO - bz) * bx
+    return bz * h - HALO + layer, row
 
 
 def spring_row(bz, bx):
@@ -204,7 +207,7 @@
 def strip_kernel(heights, bz, bx, x_ref, near_ref, far_ref):
     odd = (lax.axis_index("tile") & 1) == 1
     counts, starts, end = strips(bz)
-    wanted = [(place(heights, bz, bx, layer)[1], count, start) for layer, (count, start) in enumerate(zip(counts, starts))]
+    wanted = [(place(bz, bx, layer)[1], count, start) for layer, (count, start) in enumerate(zip(counts, starts))]
     wanted += [(spring_row(bz, bx) + bx * k, HALO, end + HALO * k) for k in range(2)]
     for row, count, start in wanted:
         if count:
@@ -230,7 +233,7 @@
 
 def store_strip(s, st, p, strip_ref, heights, bz, layer, far_side, valid, bx, tables):
     counts, starts, end = strips(bz)
-    z, _ = place(heights, bz, bx, layer)
+    z, _ = place(bz, bx, layer)
     weight = jnp.where((z >= 0) & (z < heights * bz), valid, 0.0)
     count = counts[layer]
     if count:
@@ -276,9 +279,9 @@
                 rest[j, c, pl.ds(row, 16), :] = one[c] + two[c]
         return carry
 
-    each(1, nz - 1, setup0, step)
-    each(2, nz - 2, sweep0, step)
-    each(0, bz // 2 + 6, restrict0, step)
+    each(1, nz - 1, setup0, step or 12)
+    each(2, nz - 2, sweep0, step or 11)
+    each(0, bz // 2 + 6, restrict0, step or 5)
 
 
 def inner_kernel(heights, tiles, bz, bx, x_ref, near_ref, s, p, st, b, r, d, g, y, v, rest):
@@ -288,7 +291,7 @@
     valid = jnp.where(odd | (t < tiles - 1), 1.0, 0.0)
 
     def read_layer(layer, carry):
-        z, row = place(heights, bz, bx, layer)
+        z, row = place(bz, bx, layer)
         inside = jnp.where((z >= 0) & (z < heights * bz), 1.0, 0.0)
         store_layer(s, st, x_ref[pl.ds(row, bx), :], layer, 16, inside, tables)
         bottom = jnp.where((z >= 0) & (z < 2), 2.0 * PENALTY, 0.0)
@@ -298,7 +301,7 @@
 
     each(0, bz + 2 * HALO, read_layer, bz + 2 * HALO + 1)
     rows = [[jnp.where(odd, 8 - k, 24 + k) + at for at in range(0, bx, 16)] for k in range(3)]
-    fine_down(bz, s, p, st, b, r, d, g, y, v, rest, rows, 8)
+    fine_down(bz, s, p, st, b, r, d, g, y, v, rest, rows, 0)
 
 
 def down_kernel(
@@ -320,7 +323,7 @@
 
     each(0, bz + 2 * HALO, read_layer, bz + 2 * HALO + 1)
     rows = [[jnp.where(odd, bx + 8 - k, 8 + k)] for k in range(3)]
-    fine_down(bz, s, p, st, b, r, d, g, y, v, rest, rows, 24)
+    fine_down(bz, s, p, st, b, r, d, g, y, v, rest, rows, 12)
 
     rows1 = bx1 + 8
 

time: 39.7 us -> 39.4 us (level)
  Pallas kernels: 9.76 us -> 9.31 us
  transfers between devices with their start and end apart: 5 -> 5, of which waited for: 2 -> 2; matrix products, arithmetic and copies ran while one was open for 0% -> 0% of each run, Pallas kernels for 8% -> 7%
where the time goes in v7:
time: 39.4 us; the launch traced here: 39.2 us
  blocking collectives  17 us (43%)
  Pallas kernels  9.31 us (24%)
  starting transfers between devices  7.83 us (20%)
  waiting for transfers between devices  5.02 us (13%)
    all_to_all x1, blocking collectives, local(): lax.all_to_all(blocks, ('tile', 'height'), 0, 0).reshape(send.shape)  17 us
    ppermute x4, starting transfers between devices, swapped(): return lax.ppermute(x, axis, pairs + [(j, i) for i, j in pairs])  3.97 us
    ppermute x1, starting transfers between devices, local(): lax.ppermute(edge, 'height', [(i, (i + 2) % heights) for i in range(heigh...  3.86 us
    ppermute x1, waiting for transfers between devices, local(): lax.ppermute(edge, 'height', [(i, (i + 2) % heights) for i in range(heigh...  3.2 us
    pallas_call x1, Pallas kernels, local(): pl.pallas_call(functools.partial(up_kernel, heights, tiles, bz, bx), out_...  2.9 us
    pallas_call x1, Pallas kernels, local(): pl.pallas_call(functools.partial(inner_kernel, heights, tiles, bz, bx), o...  2.86 us
    pallas_call x1, Pallas kernels, local(): pl.pallas_call(functools.partial(down_kernel, heights, tiles, bz, bx), ou...  2.54 us
    ppermute x4, waiting for transfers between devices, swapped(): return lax.ppermute(x, axis, pairs + [(j, i) for i, j in pairs])  1.81 us
  transfers between devices with their start and end apart: 5, of which 2 were waited for; matrix products, arithmetic and copies ran while one was open for 0% of the time, Pallas kernels for 7%

profile of v7, /device:TPU:0, one launch (start us, length us, event | category | flops | bytes accessed | tf_op | source)
XLA Modules:
  0.0 39.2 jit_solution(4887132089585956422)
XLA Ops:
  0.0 1.0 %shard_map.46 = (f32[324,128]{1,0:T(8,128)S(1)}, f32[256,128]{1,0:T(8,128)S(1)}, f32[32,128]{1,0:T(8,128)S(1)}) custom-call(s32[8,32,128]{2,1,0:T(8,128)} %material_ref.1, s32[8,32,128]{2,1,0:T(8,128)} %clamped_ref.1, f32[3]{0:T(128)} %table_ref.1, f32[3,3]{1,0:T(4,128)} %strain_ref.1), custom_call_target="tpu_custom_call" | custom-call | tf_op jit(solution)/shard_map/pallas_call | solution.py:600
  1.0 0.5 %collective-permute-start = (f32[324,128]{1,0:T(8,128)S(1)}, f32[324,128]{1,0:T(8,128)S(1)}, u32[]{:S(2)}, u32[]{:S(2)}) collective-permute-start(f32[324,128]{1,0:T(8,128)S(1)} %get-tuple-element.31), channel_id=1, source_target_pairs={{0,1},{2,3},{1,0},{3,2},{4,5},{6,7},{5,4},{7,6},{8,9},{10,11},{9,8... | collective-permute-start | bytes 497672 | tf_op jit(solution)/shard_map/ppermute | solution.py:588
  1.5 0.7 %collective-permute-start.1 = (f32[256,128]{1,0:T(8,128)S(1)}, f32[256,128]{1,0:T(8,128)S(1)}, u32[]{:S(2)}, u32[]{:S(2)}) collective-permute-start(f32[256,128]{1,0:T(8,128)S(1)} %get-tuple-element.32), channel_id=1, source_target_pairs={{1,2},{2,1},{5,6},{6,5},{9,10},{10,9},{13,14},{14,13},{17,18},{18,... | collective-permute-start | bytes 393224 | tf_op jit(solution)/shard_map/ppermute | solution.py:588
  2.2 3.9 %collective-permute-start.2 = (f32[32,128]{1,0:T(8,128)S(1)}, f32[32,128]{1,0:T(8,128)S(1)}, u32[]{:S(2)}, u32[]{:S(2)}) collective-permute-start(f32[32,128]{1,0:T(8,128)S(1)} %get-tuple-element.33), channel_id=1, source_target_pairs={{0,2},{1,3},{2,0},{3,1},{4,6},{5,7},{6,4},{7,5},{8,10},{9,11},{10,... | collective-permute-start | bytes 49160 | tf_op jit(solution)/shard_map/ppermute | solution.py:611
  6.0 3.2 %collective-permute-done.2 = f32[32,128]{1,0:T(8,128)S(1)} collective-permute-done((f32[32,128]{1,0:T(8,128)S(1)}, f32[32,128]{1,0:T(8,128)S(1)}, u32[]{:S(2)}, u32[]{:S(2)}) %collective-permute-start.2) | collective-permute-done | bytes 16416 | tf_op jit(solution)/shard_map/ppermute | solution.py:611
  9.2 0.0 collective-permute-done.1
  9.2 0.0 collective-permute-done
  9.3 2.1 %collective-permute-start.4 = (f32[168,128]{1,0:T(8,128)S(1)}, f32[168,128]{1,0:T(8,128)S(1)}, u32[]{:S(2)}, u32[]{:S(2)}) collective-permute-start(f32[168,128]{1,0:T(8,128)S(1)} %get-tuple-element.35), channel_id=1, source_target_pairs={{0,4},{8,12},{16,20},{24,28},{4,0},{12,8},{20,16},{28,24},{1,5},{9... | collective-permute-start | bytes 258056 | tf_op jit(solution)/shard_map/ppermute | solution.py:588
  11.5 0.7 %collective-permute-start.3 = (f32[168,128]{1,0:T(8,128)S(1)}, f32[168,128]{1,0:T(8,128)S(1)}, u32[]{:S(2)}, u32[]{:S(2)}) collective-permute-start(f32[168,128]{1,0:T(8,128)S(1)} %get-tuple-element.34), channel_id=1, source_target_pairs={{4,8},{12,16},{20,24},{8,4},{16,12},{24,20},{5,9},{13,17},{21,25},... | collective-permute-start | bytes 258056 | tf_op jit(solution)/shard_map/ppermute | solution.py:588
  12.1 1.8 %collective-permute-done.4.near_ref = f32[168,128]{1,0:T(8,128)S(1)} collective-permute-done((f32[168,128]{1,0:T(8,128)S(1)}, f32[168,128]{1,0:T(8,128)S(1)}, u32[]{:S(2)}, u32[]{:S(2)}) %collective-permute-start.4) | collective-permute-done | bytes 86048 | tf_op jit(solution)/shard_map/ppermute | solution.py:588
  13.9 2.9 %shard_map.48 = (f32[26,64,128]{2,1,0:T(8,128)S(1)}, f32[26,64,128]{2,1,0:T(8,128)S(1)}, f32[3,26,64,128]{3,2,1,0:T(8,128)S(1)}, f32[3,26,64,128]{3,2,1,0:T(8,12...) custom-call(f32[936,128]{1,0:T(8,128)S(1)} %pad_maximum_fusion.x_ref, ...), custom_call_target="tpu_custom_call" | custom-call | flops 26542080 | bytes 17694720 | tf_op jit(solution)/shard_map/pallas_call | solution.py:633
  16.8 0.0 collective-permute-done.3.far_ref
  16.8 2.5 %shard_map.49 = (f32[544,128]{1,0:T(8,128)S(1)}, f32[12,40,128]{2,1,0:T(8,128)S(1)}, f32[2,12,40,128]{3,2,1,0:T(8,128)S(1)}, f32[3,12,40,128]{3,2,1,0:T(8,128)S(...) custom-call(f32[936,128]{1,0:T(8,128)S(1)} %pad_maximum_fusion.x_ref, ...), custom_call_target="tpu_custom_call", output_to_operand_aliasing={{6}: (2, {}), {7}: (3, {}), {8}: (4, {}), {9}: (5, {}), {10... | custom-call | tf_op jit(solution)/shard_map/pallas_call | solution.py:643
  19.4 17.0 %all_to_all.5 = f32[32,17,1,128]{3,2,1,0:T(1,128)S(1)} all-to-all(f32[32,17,1,128]{3,2,1,0:T(1,128)S(1)} %bitcast.3), channel_id=1, replica_groups=mesh['tile'=8,'height'=4] {'tile','height'}, dimensions={0} | all-to-all | bytes 557056 | tf_op jit(solution)/shard_map/all_to_all | solution.py:656
  36.3 2.9 %shard_map.50 = f32[3,8,32,128]{3,2,1,0:T(8,128)} custom-call(f32[544,128]{1,0:T(8,128)S(1)} %bitcast.2, f32[26,64,128]{2,1,0:T(8,128)S(1)} %get-tuple-element.47.s0, f32[2,26,64,128]{3,2,1,0:T(8,128)S(1)} %get-tuple-element.48.y0, f32[3,26,64,128]{3,2,1,0:T(8,128)S(1)} %get-tuple-element.49.v0, f32[3,26,64,128]{3,2,1,0:T(8,128)S(1)} %get-tuple-element.50.g0, ...), custom_call_target="tpu_custom_call" | custom-call | tf_op jit(solution)/shard_map/pallas_call | solution.py:662
  (2 shorter events, 0.1 us)
Async XLA Ops:
  1.0 8.3 %collective-permute-start = (f32[324,128]{1,0:T(8,128)S(1)}, f32[324,128]{1,0:T(8,128)S(1)}, u32[]{:S(2)}, u32[]{:S(2)}) collective-permute-start(f32[324,128]{1,0:T(8,128)S(1)} %get-tuple-element.31), channel_id=1, source_target_pairs={{0,1},{2,3},{1,0},{3,2},{4,5},{6,7},{5,4},{7,6},{8,9},{10,11},{9,8... | collective-permute-start | bytes 497672 | tf_op jit(solution)/shard_map/ppermute | solution.py:588
  1.5 7.7 %collective-permute-start.1 = (f32[256,128]{1,0:T(8,128)S(1)}, f32[256,128]{1,0:T(8,128)S(1)}, u32[]{:S(2)}, u32[]{:S(2)}) collective-permute-start(f32[256,128]{1,0:T(8,128)S(1)} %get-tuple-element.32), channel_id=1, source_target_pairs={{1,2},{2,1},{5,6},{6,5},{9,10},{10,9},{13,14},{14,13},{17,18},{18,... | collective-permute-start | bytes 393224 | tf_op jit(solution)/shard_map/ppermute | solution.py:588
  2.2 7.1 %collective-permute-start.2 = (f32[32,128]{1,0:T(8,128)S(1)}, f32[32,128]{1,0:T(8,128)S(1)}, u32[]{:S(2)}, u32[]{:S(2)}) collective-permute-start(f32[32,128]{1,0:T(8,128)S(1)} %get-tuple-element.33), channel_id=1, source_target_pairs={{0,2},{1,3},{2,0},{3,1},{4,6},{5,7},{6,4},{7,5},{8,10},{9,11},{10,... | collective-permute-start | bytes 49160 | tf_op jit(solution)/shard_map/ppermute | solution.py:611
  9.3 4.6 %collective-permute-start.4 = (f32[168,128]{1,0:T(8,128)S(1)}, f32[168,128]{1,0:T(8,128)S(1)}, u32[]{:S(2)}, u32[]{:S(2)}) collective-permute-start(f32[168,128]{1,0:T(8,128)S(1)} %get-tuple-element.35), channel_id=1, source_target_pairs={{0,4},{8,12},{16,20},{24,28},{4,0},{12,8},{20,16},{28,24},{1,5},{9... | collective-permute-start | bytes 258056 | tf_op jit(solution)/shard_map/ppermute | solution.py:588
  11.5 5.3 %collective-permute-start.3 = (f32[168,128]{1,0:T(8,128)S(1)}, f32[168,128]{1,0:T(8,128)S(1)}, u32[]{:S(2)}, u32[]{:S(2)}) collective-permute-start(f32[168,128]{1,0:T(8,128)S(1)} %get-tuple-element.34), channel_id=1, source_target_pairs={{4,8},{12,16},{20,24},{8,4},{16,12},{24,20},{5,9},{13,17},{21,25},... | collective-permute-start | bytes 258056 | tf_op jit(solution)/shard_map/ppermute | solution.py:588

commit v8 on v7

--- a/solution.py
+++ b/solution.py
@@ -180,6 +180,11 @@
     own_ref[pl.ds((bz + 2) * bx, SPARE), :] = row
 
 
+def spring_layers(heights, bz):
+    layers = {HALO - bz * h + k for h in range(heights) for k in range(2)}
+    return {layer for layer in layers if 0 <= layer < bz + 2 * HALO}
+
+
 def gathered_rows(bz, bx):
     whole, brick = (bz + 2) * bx + SPARE, bz * bx
     return [0, whole, 2 * whole, 2 * whole + brick]
@@ -208,7 +213,7 @@
     odd = (lax.axis_index("tile") & 1) == 1
     counts, starts, end = strips(bz)
     wanted = [(place(bz, bx, layer)[1], count, start) for layer, (count, start) in enumerate(zip(counts, starts))]
-    wanted += [(spring_row(bz, bx) + bx * k, HALO, end + HALO * k) for k in range(2)]
+    wanted += [(spring_row(bz, bx) + bx * k, HALO - 1, end + (HALO - 1) * k) for k in range(2)]
     for row, count, start in wanted:
         if count:
             first = x_ref[pl.ds(row, count), :]
@@ -239,9 +244,12 @@
     if count:
         to = jnp.where(far_side, 16 + bx, 16 - count)
         store_layer(s, st, strip_ref[pl.ds(starts[layer], count), :], layer, to, weight, tables)
-    joined = strip_ref[pl.ds(end + HALO * jnp.clip(z, 0, 1), HALO), :]
-    to = jnp.where(far_side, 16 + bx, 16 - HALO)
-    p[layer, pl.ds(to, HALO), :] = joined * jnp.where((z >= 0) & (z < 2), 2.0 * PENALTY * valid, 0.0)
+    if layer not in spring_layers(heights, bz):
+        return
+    reach = HALO - 1
+    joined = strip_ref[pl.ds(end + reach * jnp.clip(z, 0, 1), reach), :]
+    to = jnp.where(far_side, 16 + bx, 16 - reach)
+    p[layer, pl.ds(to, reach), :] = joined * jnp.where((z >= 0) & (z < 2), 2.0 * PENALTY * valid, 0.0)
 
 
 def fine_setup(s, p, st, b, r, d, g, y, layer, row, count):
@@ -294,8 +302,11 @@
         z, row = place(bz, bx, layer)
         inside = jnp.where((z >= 0) & (z < heights * bz), 1.0, 0.0)
         store_layer(s, st, x_ref[pl.ds(row, bx), :], layer, 16, inside, tables)
-        bottom = jnp.where((z >= 0) & (z < 2), 2.0 * PENALTY, 0.0)
-        p[layer, pl.ds(16, bx), :] = x_ref[pl.ds(spring_row(bz, bx) + jnp.clip(z, 0, 1) * bx, bx), :] * bottom
+        if layer in spring_layers(heights, bz):
+            bottom = jnp.where((z >= 0) & (z < 2), 2.0 * PENALTY, 0.0)
+            p[layer, pl.ds(16, bx), :] = x_ref[pl.ds(spring_row(bz, bx) + jnp.clip(z, 0, 1) * bx, bx), :] * bottom
+        else:
+            p[layer, :, :] = jnp.zeros(p.shape[1:], F32)
         store_strip(s, st, p, near_ref, heights, bz, layer, jnp.logical_not(odd), valid, bx, tables)
         return carry
 
@@ -335,12 +346,17 @@
     each(0, n1 - 2, restrict0, 8)
 
     def coarse0(k, carry):
-        for field, scale, into in ((s, 0.5, s1), (p, 1.0, p1)):
-            both = [pair_rows(field.at[1 + 2 * k + i], low, rows1) for i in range(2)]
-            into[k, pl.ds(8, rows1), :] = scale * pair_lanes(both[0] + both[1], 1)
-        return carry
-
-    each(0, n1, coarse0, 8)
+        pair = (1 + 2 * k, 2 + 2 * k)
+        both = [pair_rows(s.at[layer], low, rows1) for layer in pair]
+        s1[k, pl.ds(8, rows1), :] = 0.5 * pair_lanes(both[0] + both[1], 1)
+        if spring_layers(heights, bz).isdisjoint(pair):
+            p1[k, pl.ds(8, rows1), :] = jnp.zeros((rows1, LANES), F32)
+        else:
+            both = [pair_rows(p.at[layer], low, rows1) for layer in pair]
+            p1[k, pl.ds(8, rows1), :] = pair_lanes(both[0] + both[1], 1)
+        return carry
+
+    each(0, n1, coarse0, n1 + 1)
 
     def setup1(layer, carry):
         level_setup(
@@ -611,7 +627,7 @@
     beyond = lax.ppermute(edge, "height", [(i, (i + 2) % heights) for i in range(heights)])
     paired = swapped(own, "height", 0)
     bricks = jnp.concatenate([own, paired, beside, beyond], 0)
-    strip = pltpu.VMEM((-(-(strips(bz)[2] + 2 * HALO) // 8) * 8, LANES), F32)
+    strip = pltpu.VMEM((-(-(strips(bz)[2] + 2 * (HALO - 1)) // 8) * 8, LANES), F32)
     near, far = pl.pallas_call(
         functools.partial(strip_kernel, heights, bz, bx),
         out_shape=[strip, strip],

time: 39.4 us -> 39.3 us (level)
  no operation moved by 1% of the time
where the time goes in v8:
time: 39.3 us; the launch traced here: 39.1 us
  blocking collectives  17.2 us (44%)
  Pallas kernels  8.94 us (23%)
  starting transfers between devices  7.82 us (20%)
  waiting for transfers between devices  4.97 us (13%)
    all_to_all x1, blocking collectives, local(): lax.all_to_all(blocks, ('tile', 'height'), 0, 0).reshape(send.shape)  17.2 us
    ppermute x4, starting transfers between devices, swapped(): return lax.ppermute(x, axis, pairs + [(j, i) for i, j in pairs])  3.97 us
    ppermute x1, starting transfers between devices, local(): lax.ppermute(edge, 'height', [(i, (i + 2) % heights) for i in range(heigh...  3.86 us
    ppermute x1, waiting for transfers between devices, local(): lax.ppermute(edge, 'height', [(i, (i + 2) % heights) for i in range(heigh...  3.2 us
    pallas_call x1, Pallas kernels, local(): pl.pallas_call(functools.partial(up_kernel, heights, tiles, bz, bx), out_...  2.88 us
    pallas_call x1, Pallas kernels, local(): pl.pallas_call(functools.partial(inner_kernel, heights, tiles, bz, bx), o...  2.57 us
    pallas_call x1, Pallas kernels, local(): pl.pallas_call(functools.partial(down_kernel, heights, tiles, bz, bx), ou...  2.47 us
    ppermute x4, waiting for transfers between devices, swapped(): return lax.ppermute(x, axis, pairs + [(j, i) for i, j in pairs])  1.77 us
  transfers between devices with their start and end apart: 5, of which 2 were waited for; matrix products, arithmetic and copies ran while one was open for 0% of the time, Pallas kernels for 7%

profile of v8, /device:TPU:0, one launch (start us, length us, event | category | flops | bytes accessed | tf_op | source)
XLA Modules:
  0.0 39.1 jit_solution(17249793062812112504)
XLA Ops:
  0.0 1.0 %shard_map.46 = (f32[324,128]{1,0:T(8,128)S(1)}, f32[256,128]{1,0:T(8,128)S(1)}, f32[32,128]{1,0:T(8,128)S(1)}) custom-call(s32[8,32,128]{2,1,0:T(8,128)} %material_ref.1, s32[8,32,128]{2,1,0:T(8,128)} %clamped_ref.1, f32[3]{0:T(128)} %table_ref.1, f32[3,3]{1,0:T(4,128)} %strain_ref.1), custom_call_target="tpu_custom_call" | custom-call | tf_op jit(solution)/shard_map/pallas_call | solution.py:616
  1.0 0.5 %collective-permute-start = (f32[324,128]{1,0:T(8,128)S(1)}, f32[324,128]{1,0:T(8,128)S(1)}, u32[]{:S(2)}, u32[]{:S(2)}) collective-permute-start(f32[324,128]{1,0:T(8,128)S(1)} %get-tuple-element.31), channel_id=1, source_target_pairs={{0,1},{2,3},{1,0},{3,2},{4,5},{6,7},{5,4},{7,6},{8,9},{10,11},{9,8... | collective-permute-start | bytes 497672 | tf_op jit(solution)/shard_map/ppermute | solution.py:604
  1.5 0.7 %collective-permute-start.1 = (f32[256,128]{1,0:T(8,128)S(1)}, f32[256,128]{1,0:T(8,128)S(1)}, u32[]{:S(2)}, u32[]{:S(2)}) collective-permute-start(f32[256,128]{1,0:T(8,128)S(1)} %get-tuple-element.32), channel_id=1, source_target_pairs={{1,2},{2,1},{5,6},{6,5},{9,10},{10,9},{13,14},{14,13},{17,18},{18,... | collective-permute-start | bytes 393224 | tf_op jit(solution)/shard_map/ppermute | solution.py:604
  2.2 3.9 %collective-permute-start.2 = (f32[32,128]{1,0:T(8,128)S(1)}, f32[32,128]{1,0:T(8,128)S(1)}, u32[]{:S(2)}, u32[]{:S(2)}) collective-permute-start(f32[32,128]{1,0:T(8,128)S(1)} %get-tuple-element.33), channel_id=1, source_target_pairs={{0,2},{1,3},{2,0},{3,1},{4,6},{5,7},{6,4},{7,5},{8,10},{9,11},{10,... | collective-permute-start | bytes 49160 | tf_op jit(solution)/shard_map/ppermute | solution.py:627
  6.0 3.2 %collective-permute-done.2 = f32[32,128]{1,0:T(8,128)S(1)} collective-permute-done((f32[32,128]{1,0:T(8,128)S(1)}, f32[32,128]{1,0:T(8,128)S(1)}, u32[]{:S(2)}, u32[]{:S(2)}) %collective-permute-start.2) | collective-permute-done | bytes 16416 | tf_op jit(solution)/shard_map/ppermute | solution.py:627
  9.2 0.0 collective-permute-done.1
  9.2 0.0 collective-permute-done
  9.3 2.1 %collective-permute-start.4 = (f32[160,128]{1,0:T(8,128)S(1)}, f32[160,128]{1,0:T(8,128)S(1)}, u32[]{:S(2)}, u32[]{:S(2)}) collective-permute-start(f32[160,128]{1,0:T(8,128)S(1)} %get-tuple-element.35), channel_id=1, source_target_pairs={{0,4},{8,12},{16,20},{24,28},{4,0},{12,8},{20,16},{28,24},{1,5},{9... | collective-permute-start | bytes 245768 | tf_op jit(solution)/shard_map/ppermute | solution.py:604
  11.5 0.7 %collective-permute-start.3 = (f32[160,128]{1,0:T(8,128)S(1)}, f32[160,128]{1,0:T(8,128)S(1)}, u32[]{:S(2)}, u32[]{:S(2)}) collective-permute-start(f32[160,128]{1,0:T(8,128)S(1)} %get-tuple-element.34), channel_id=1, source_target_pairs={{4,8},{12,16},{20,24},{8,4},{16,12},{24,20},{5,9},{13,17},{21,25},... | collective-permute-start | bytes 245768 | tf_op jit(solution)/shard_map/ppermute | solution.py:604
  12.1 1.8 %collective-permute-done.4.near_ref = f32[160,128]{1,0:T(8,128)S(1)} collective-permute-done((f32[160,128]{1,0:T(8,128)S(1)}, f32[160,128]{1,0:T(8,128)S(1)}, u32[]{:S(2)}, u32[]{:S(2)}) %collective-permute-start.4) | collective-permute-done | bytes 81952 | tf_op jit(solution)/shard_map/ppermute | solution.py:604
  13.9 2.6 %shard_map.48 = (f32[26,64,128]{2,1,0:T(8,128)S(1)}, f32[26,64,128]{2,1,0:T(8,128)S(1)}, f32[3,26,64,128]{3,2,1,0:T(8,128)S(1)}, f32[3,26,64,128]{3,2,1,0:T(8,12...) custom-call(f32[936,128]{1,0:T(8,128)S(1)} %pad_maximum_fusion.x_ref, ...), custom_call_target="tpu_custom_call" | custom-call | flops 26542080 | bytes 17694720 | tf_op jit(solution)/shard_map/pallas_call | solution.py:649
  16.5 0.0 collective-permute-done.3.far_ref
  16.5 2.5 %shard_map.49 = (f32[544,128]{1,0:T(8,128)S(1)}, f32[12,40,128]{2,1,0:T(8,128)S(1)}, f32[2,12,40,128]{3,2,1,0:T(8,128)S(1)}, f32[3,12,40,128]{3,2,1,0:T(8,128)S(...) custom-call(f32[936,128]{1,0:T(8,128)S(1)} %pad_maximum_fusion.x_ref, ...), custom_call_target="tpu_custom_call", output_to_operand_aliasing={{6}: (2, {}), {7}: (3, {}), {8}: (4, {}), {9}: (5, {}), {10... | custom-call | tf_op jit(solution)/shard_map/pallas_call | solution.py:659
  18.9 17.2 %all_to_all.5 = f32[32,17,1,128]{3,2,1,0:T(1,128)S(1)} all-to-all(f32[32,17,1,128]{3,2,1,0:T(1,128)S(1)} %bitcast.3), channel_id=1, replica_groups=mesh['tile'=8,'height'=4] {'tile','height'}, dimensions={0} | all-to-all | bytes 557056 | tf_op jit(solution)/shard_map/all_to_all | solution.py:672
  36.2 2.9 %shard_map.50 = f32[3,8,32,128]{3,2,1,0:T(8,128)} custom-call(f32[544,128]{1,0:T(8,128)S(1)} %bitcast.2, f32[26,64,128]{2,1,0:T(8,128)S(1)} %get-tuple-element.47.s0, f32[2,26,64,128]{3,2,1,0:T(8,128)S(1)} %get-tuple-element.48.y0, f32[3,26,64,128]{3,2,1,0:T(8,128)S(1)} %get-tuple-element.49.v0, f32[3,26,64,128]{3,2,1,0:T(8,128)S(1)} %get-tuple-element.50.g0, ...), custom_call_target="tpu_custom_call" | custom-call | tf_op jit(solution)/shard_map/pallas_call | solution.py:678
  (2 shorter events, 0.1 us)
Async XLA Ops:
  1.0 8.3 %collective-permute-start = (f32[324,128]{1,0:T(8,128)S(1)}, f32[324,128]{1,0:T(8,128)S(1)}, u32[]{:S(2)}, u32[]{:S(2)}) collective-permute-start(f32[324,128]{1,0:T(8,128)S(1)} %get-tuple-element.31), channel_id=1, source_target_pairs={{0,1},{2,3},{1,0},{3,2},{4,5},{6,7},{5,4},{7,6},{8,9},{10,11},{9,8... | collective-permute-start | bytes 497672 | tf_op jit(solution)/shard_map/ppermute | solution.py:604
  1.5 7.7 %collective-permute-start.1 = (f32[256,128]{1,0:T(8,128)S(1)}, f32[256,128]{1,0:T(8,128)S(1)}, u32[]{:S(2)}, u32[]{:S(2)}) collective-permute-start(f32[256,128]{1,0:T(8,128)S(1)} %get-tuple-element.32), channel_id=1, source_target_pairs={{1,2},{2,1},{5,6},{6,5},{9,10},{10,9},{13,14},{14,13},{17,18},{18,... | collective-permute-start | bytes 393224 | tf_op jit(solution)/shard_map/ppermute | solution.py:604
  2.2 7.1 %collective-permute-start.2 = (f32[32,128]{1,0:T(8,128)S(1)}, f32[32,128]{1,0:T(8,128)S(1)}, u32[]{:S(2)}, u32[]{:S(2)}) collective-permute-start(f32[32,128]{1,0:T(8,128)S(1)} %get-tuple-element.33), channel_id=1, source_target_pairs={{0,2},{1,3},{2,0},{3,1},{4,6},{5,7},{6,4},{7,5},{8,10},{9,11},{10,... | collective-permute-start | bytes 49160 | tf_op jit(solution)/shard_map/ppermute | solution.py:627
  9.3 4.6 %collective-permute-start.4 = (f32[160,128]{1,0:T(8,128)S(1)}, f32[160,128]{1,0:T(8,128)S(1)}, u32[]{:S(2)}, u32[]{:S(2)}) collective-permute-start(f32[160,128]{1,0:T(8,128)S(1)} %get-tuple-element.35), channel_id=1, source_target_pairs={{0,4},{8,12},{16,20},{24,28},{4,0},{12,8},{20,16},{28,24},{1,5},{9... | collective-permute-start | bytes 245768 | tf_op jit(solution)/shard_map/ppermute | solution.py:604
  11.5 5.0 %collective-permute-start.3 = (f32[160,128]{1,0:T(8,128)S(1)}, f32[160,128]{1,0:T(8,128)S(1)}, u32[]{:S(2)}, u32[]{:S(2)}) collective-permute-start(f32[160,128]{1,0:T(8,128)S(1)} %get-tuple-element.34), channel_id=1, source_target_pairs={{4,8},{12,16},{20,24},{8,4},{16,12},{24,20},{5,9},{13,17},{21,25},... | collective-permute-start | bytes 245768 | tf_op jit(solution)/shard_map/ppermute | solution.py:604
